TPU v7x, 512 devices: a whole 4x8x8 slice. The times are simulated.
512 devices in a mesh: clip: 8 (over x, core), bank: 64 (over y, z).
Axes of the slice: x: 4, y: 8, z: 8, core: 2. Of those that a mesh axis runs over, the one named last changes fastest.
Arguments:
- queries: bfloat16 [8, 256, 1536], P('clip', 'bank'), may hold values from -120 to 120
- keys: bfloat16 [8, 8192, 1536], P('clip', 'bank'), may hold values from -6 to 6
- values: bfloat16 [8, 8192, 1536], P('clip', 'bank'), may hold values from -6 to 6
- grad_out: bfloat16 [8, 256, 1536], P('clip', 'bank'), may hold values from -6 to 6
- null_key: bfloat16 [1536], replicated, may hold values from -4 to 4
- null_value: bfloat16 [1536], replicated, may hold values from -4 to 4
- bank_counts: int32 [8], P('clip'), may hold values from 128 to 8192, as said below
- block_slot: int32 [8, 64], P('clip', 'bank'), may hold values from 0 to 63, each once within a row
Outputs:
- grad_queries: bfloat16 [8, 256, 1536], P('clip', 'bank')
- grad_keys: bfloat16 [8, 8192, 1536], P('clip', 'bank')
- grad_values: bfloat16 [8, 8192, 1536], P('clip', 'bank')
- grad_null_key: float32 [1536], replicated
- grad_null_value: float32 [1536], replicated
Inputs may be any that keep to these rules, and one draw needn't show every extreme that they name: `bank_counts`: a multiple of 128; exactly one group holds 8192 live tokens. `block_slot`: each row is a permutation of the device indices.
All inputs are finite; a program needn't handle non-finite values.
Results may differ from a plain program's by a relative error of at most 0.01155.
Values may be sent and summed in bfloat16 or wider, within the bound.
No kernel may reach another device: no remote copies, remote signals or barrier semaphores. Data moves between devices by JAX's collectives and lax.ppermute only.
A program may use at most 64 MiB of HBM per device.

v0:
```python
import jax
import jax.numpy as jnp
from jax import lax
from jax.sharding import PartitionSpec as P

HEADS = 12
HD = 128


def split_heads(matrix):
    return matrix.reshape(matrix.shape[0], HEADS, HD).transpose(1, 0, 2)


def join_heads(stacked):
    return stacked.transpose(1, 0, 2).reshape(stacked.shape[1], HEADS * HD)


def on_device(queries, keys, values, grad_out, null_key, null_value, bank_counts, block_slot):
    score_scale = HD ** (-0.5)
    whole_q, whole_do = (
        lax.all_gather(queries[0], "bank", axis=0, tiled=True),
        lax.all_gather(grad_out[0], "bank", axis=0, tiled=True),
    )
    row_count = whole_q.shape[0]
    block_rows = keys.shape[1]
    own_rows = queries.shape[1]
    valid_keys = jnp.clip(bank_counts[0] - block_slot[0, 0] * block_rows, 0, block_rows)
    live_keys = jnp.arange(block_rows, dtype=jnp.int32) < valid_keys
    live_float = live_keys.astype(jnp.float32)
    q_heads = split_heads(whole_q)
    do_heads = split_heads(whole_do)
    k_heads = split_heads(keys[0])
    v_heads = split_heads(values[0])
    nk_heads = null_key.reshape(HEADS, HD)
    nv_heads = null_value.reshape(HEADS, HD)
    null_score = (
        jnp.einsum("hqd,hd->hq", q_heads, nk_heads, preferred_element_type=jnp.float32)
        * score_scale
    )
    null_dp = jnp.einsum("hqd,hd->hq", do_heads, nv_heads, preferred_element_type=jnp.float32)

    def block_scores(q_head, k_head):
        scores = jnp.dot(q_head, k_head.T, preferred_element_type=jnp.float32) * score_scale
        return jnp.where(live_keys[None, :], scores, -1e30)

    def first_pass(pieces):
        q_head, k_head = pieces
        scores = block_scores(q_head, k_head)
        peaks = jnp.max(scores, axis=1)
        sums = jnp.sum(jnp.exp(scores - peaks[:, None]) * live_float[None, :], axis=1)
        return (peaks, sums)

    local_peaks, local_sums = lax.map(first_pass, (q_heads, k_heads))
    peaks_all = lax.pmax(local_peaks, "bank")
    sums_all = lax.psum(local_sums * jnp.exp(local_peaks - peaks_all), "bank")
    row_top = jnp.maximum(peaks_all, null_score)
    log_total = row_top + jnp.log(
        sums_all * jnp.exp(peaks_all - row_top) + jnp.exp(null_score - row_top)
    )
    null_prob = jnp.exp(null_score - log_total)

    def second_pass(pieces):
        q_head, k_head, do_head, v_head, log_head = pieces
        probs = jnp.exp(block_scores(q_head, k_head) - log_head[:, None]) * live_float[None, :]
        dprobs = jnp.dot(do_head, v_head.T, preferred_element_type=jnp.float32)
        return (probs, dprobs, jnp.sum(probs * dprobs, axis=1))

    probs_all, dprobs_all, partial_delta = lax.map(
        second_pass, (q_heads, k_heads, do_heads, v_heads, log_total)
    )
    row_delta = lax.psum(partial_delta, "bank") + null_prob * null_dp

    def third_pass(pieces):
        probs, dprobs, q_head, do_head, delta_head = pieces
        dscore = (probs * (dprobs - delta_head[:, None])).astype(jnp.bfloat16)
        grad_k = (
            jnp.dot(dscore.T, q_head, preferred_element_type=jnp.float32) * score_scale
        ).astype(jnp.bfloat16)
        grad_v = jnp.dot(
            probs.astype(jnp.bfloat16).T, do_head, preferred_element_type=jnp.float32
        ).astype(jnp.bfloat16)
        return (dscore, grad_k, grad_v)

    dscores, grad_k, grad_v = lax.map(
        third_pass, (probs_all, dprobs_all, q_heads, do_heads, row_delta)
    )
    product = jnp.einsum("hqk,hkd->qhd", dscores, k_heads, preferred_element_type=jnp.float32)
    own_terms = lax.psum_scatter(
        product.reshape(row_count, HEADS * HD) * score_scale,
        "bank",
        scatter_dimension=0,
        tiled=True,
    )
    row_start = lax.axis_index("bank") * own_rows
    null_ds = null_prob * (null_dp - row_delta)
    own_ds = lax.dynamic_slice_in_dim(null_ds, row_start, own_rows, 1)
    own_prob = lax.dynamic_slice_in_dim(null_prob, row_start, own_rows, 1)
    own_q = lax.dynamic_slice_in_dim(q_heads, row_start, own_rows, 1).astype(jnp.float32)
    own_do = lax.dynamic_slice_in_dim(do_heads, row_start, own_rows, 1).astype(jnp.float32)
    null_term = (
        own_ds[:, :, None] * nk_heads.astype(jnp.float32)[:, None, :] * score_scale
    ).transpose(1, 0, 2)
    grad_q = (own_terms + null_term.reshape(own_rows, HEADS * HD)).astype(jnp.bfloat16)
    local_nk = jnp.sum(own_ds[:, :, None] * own_q, axis=1) * score_scale
    local_nv = jnp.sum(own_prob[:, :, None] * own_do, axis=1)
    grad_nk, grad_nv = lax.psum((local_nk.reshape(-1), local_nv.reshape(-1)), ("clip", "bank"))
    return (grad_q[None], join_heads(grad_k)[None], join_heads(grad_v)[None], grad_nk, grad_nv)


def solution(mesh):
    return jax.shard_map(
        on_device,
        mesh=mesh,
        in_specs=(
            P("clip", "bank", None),
            P("clip", "bank", None),
            P("clip", "bank", None),
            P("clip", "bank", None),
            P(),
            P(),
            P("clip"),
            P("clip", "bank"),
        ),
        out_specs=(
            P("clip", "bank", None),
            P("clip", "bank", None),
            P("clip", "bank", None),
            P(),
            P(),
        ),
        check_vma=False,
    )
```

profile of v0, /device:TPU:1, one launch (start us, length us, event | category | flops | bytes accessed | tf_op | source)
XLA Modules:
  0.0 1211.6 jit_solution(13146304781003923662)
XLA Ops:
  8.0 48.2 %all-gather = bf16[1,256,1536]{2,0,1:T(2,128)(2,1)S(1)} all-gather(bf16[1,4,1536]{2,0,1:T(2,128)(2,1)S(1)} %copy.40), channel_id=2, replica_groups=mesh['clip'=8,'bank'=64] {'bank'}, dimensions={1}, use_global_device_ids=true | all-gather | bytes 798720 | tf_op jit(solution)/shard_map/all_gather | solution.py:21
  60.4 5.1 while.45
  65.5 221.9 %pmax.7 = f32[12,256]{1,0:T(8,128)S(1)} all-reduce(f32[12,256]{1,0:T(8,128)S(1)} %get-tuple-element.151), channel_id=1, replica_groups=mesh['clip'=8,'bank'=64] {'bank'}, use_global_device_ids=true, to_apply=%region_4.5 | all-reduce | flops 3072 | bytes 24576 | tf_op jit(solution)/shard_map/pmax | solution.py:54
  287.5 219.6 %psum.28 = f32[12,256]{1,0:T(8,128)} all-reduce(f32[12,256]{1,0:T(8,128)S(1)} %exponential_multiply_fusion), channel_id=1, replica_groups=mesh['clip'=8,'bank'=64] {'bank'}, use_global_device_ids=true, to_apply=%region_5.6 | all-reduce | flops 3072 | bytes 24576 | tf_op jit(solution)/shard_map/psum | solution.py:55
  507.3 36.2 %all-gather.1 = bf16[1,256,1536]{2,0,1:T(2,128)(2,1)S(1)} all-gather(bf16[1,4,1536]{2,0,1:T(2,128)(2,1)S(1)} %copy.45), channel_id=3, replica_groups=mesh['clip'=8,'bank'=64] {'bank'}, dimensions={1}, use_global_device_ids=true | all-gather | bytes 798720 | tf_op jit(solution)/shard_map/all_gather | solution.py:22
  547.0 32.0 %while.46 = (s32[]{:T(128)}, f32[12,256,128]{1,2,0:T(8,128)}, f32[12,256,128]{1,2,0:T(8,128)}, f32[12,256]{1,0:T(8,128)S(1)}, bf16[12,256,128]{2,1,0:T(8,128)(2,...) while((s32[]{:T(128)}, f32[12,256,128]{1,2,0:T(8,128)}, ...), condition=%wide.region_8.9_spmd.clone.clone, body=%wide.region_6.8_spmd.clone.clone.sunk | while | flops 16973824 | bytes 993665 | solution.py:68
  547.0 1.7 bitcast_dynamic-update-slice_fusion.4
  549.7 1.7 bitcast_dynamic-update-slice_fusion.4
  552.4 1.7 bitcast_dynamic-update-slice_fusion.4
  555.0 1.7 bitcast_dynamic-update-slice_fusion.4
  557.7 1.7 bitcast_dynamic-update-slice_fusion.4
  560.4 1.7 bitcast_dynamic-update-slice_fusion.4
  563.0 1.7 bitcast_dynamic-update-slice_fusion.4
  565.7 1.7 bitcast_dynamic-update-slice_fusion.4
  568.4 1.7 bitcast_dynamic-update-slice_fusion.4
  571.0 1.7 bitcast_dynamic-update-slice_fusion.4
  573.7 1.7 bitcast_dynamic-update-slice_fusion.4
  576.4 1.7 bitcast_dynamic-update-slice_fusion.4
  579.0 221.2 %psum.29 = f32[12,256]{1,0:T(8,128)S(1)} all-reduce(f32[12,256]{1,0:T(8,128)S(1)} %get-tuple-element.155), channel_id=1, replica_groups=mesh['clip'=8,'bank'=64] {'bank'}, use_global_device_ids=true, to_apply=%region_9.10 | all-reduce | flops 3072 | bytes 24576 | tf_op jit(solution)/shard_map/psum | solution.py:71
  801.0 58.9 %while.44 = (s32[]{:T(128)}, bf16[12,256,128]{2,1,0:T(8,128)(2,1)}, bf16[12,128,128]{1,2,0:T(8,128)(2,1)}, bf16[12,128,128]{1,2,0:T(8,128)(2,1)}, f32[12,256,128...) while((s32[]{:T(128)}, bf16[12,256,128]{2,1,0:T(8,128)(2,1)}, ...), condition=%wide.region_11.12_spmd, body=%wide.region_10.11_spmd.sunk | while | flops 16957440 | bytes 2101877 | solution.py:84
  860.5 1.5 convolution_multiply_fusion.3
  862.1 1.6 copy.56
  869.3 281.6 %all-reduce.1 = (f32[1536]{0:T(1024)}, f32[1536]{0:T(1024)}) all-reduce(f32[1536]{0:T(1024)S(1)} %multiply_bitcast_fusion, f32[1536]{0:T(1024)S(1)} %bitcast.209), channel_id=1, replica_groups=mesh['clip'=8,'bank'=64] {'clip','bank'}, use_global_device_ids=true, to_apply=%region_14.15 | all-reduce | flops 3072 | bytes 24576 | tf_op jit(solution)/shard_map/psum | solution.py:106
  1151.0 52.3 %all-reduce.4.cloned.1.call-done = f32[256,1536]{1,0:T(8,128)} async-done(((f32[256,1536]{1,0:T(8,128)}), f32[256,1536]{1,0:T(8,128)}) %all-reduce.4.cloned.1.call-update) | async-done | bytes 1572880
  (319 shorter events, 89.5 us)
Async XLA Ops:
  7.2 793.0 %copy-start = (bf16[1536]{0:T(1024)(128)(2,1)S(1)}, bf16[1536]{0:T(1024)(128)(2,1)}, u32[]{:S(2)}) copy-start(bf16[1536]{0:T(1024)(128)(2,1)} %param.19) | copy-start | bytes 9220
  7.2 1196.2 %all-reduce.4.cloned.1.call-start = ((), (), s32[]{:S(2)}) async-start(), calls=%async_computation | async-start | bytes 3145728
  57.6 1.0 copy-start.3
  58.8 448.3 %copy-start.13 = (bf16[1536]{0:T(1024)(128)(2,1)S(1)}, bf16[1536]{0:T(1024)(128)(2,1)}, u32[]{:S(2)}) copy-start(bf16[1536]{0:T(1024)(128)(2,1)} %param.18) | copy-start | bytes 9220
  59.0 448.2 %copy-start.15 = (bf16[1,4,1536]{2,1,0:T(4,128)(2,1)S(1)}, bf16[1,4,1536]{2,1,0:T(4,128)(2,1)}, u32[]{:S(2)}) copy-start(bf16[1,4,1536]{2,1,0:T(4,128)(2,1)} %param.17) | copy-start | bytes 36868
  65.5 441.8 %copy-start.2 = (bf16[12,128,128]{2,1,0:T(8,128)(2,1)}, bf16[12,128,128]{2,1,0:T(8,128)(2,1)S(1)}, u32[]{:S(2)}) copy-start(bf16[12,128,128]{2,1,0:T(8,128)(2,1)S(1)} %get-tuple-element.665) | copy-start | bytes 1179652
  65.5 441.8 %copy-start.1 = (bf16[12,256,128]{2,1,0:T(8,128)(2,1)}, bf16[12,256,128]{2,1,0:T(8,128)(2,1)S(1)}, u32[]{:S(2)}) copy-start(bf16[12,256,128]{2,1,0:T(8,128)(2,1)S(1)} %get-tuple-element.662) | copy-start | bytes 2359300
  287.4 219.8 %copy-start.7 = (f32[12,256]{1,0:T(8,128)}, f32[12,256]{1,0:T(8,128)S(1)}, u32[]{:S(2)}) copy-start(f32[12,256]{1,0:T(8,128)S(1)} %pmax.7) | copy-start | bytes 36868
  507.3 38.9 %copy-start.8 = (f32[12,1,256]{2,1,0:T(1,128)}, f32[12,1,256]{2,1,0:T(1,128)S(1)}, u32[]{:S(2)}) copy-start(f32[12,1,256]{2,1,0:T(1,128)S(1)} %fusion.63) | copy-start | bytes 36868
  545.0 1.0 copy-start.4
  547.0 253.4 %copy-start.9 = (f32[12,1,256]{2,1,0:T(1,128)S(1)}, f32[12,1,256]{2,1,0:T(1,128)}, u32[]{:S(2)}) copy-start(f32[12,1,256]{2,1,0:T(1,128)} %copy-done.8) | copy-start | bytes 36868
  859.9 0.6 copy-start.10
  863.7 0.7 copy-start.14
  863.7 0.7 copy-start.11
  863.7 0.7 copy-start.12
  863.7 1.0 copy-start.5
  863.7 2.0 copy-start.6
Sparse Core Ops, SparseCore 0:
  863.9 339.4 all-reduce.3
where the time goes:
time: 1220 us; the launch traced here: 1210 us
  blocking collectives  1030 us (84%)
  waiting for transfers between devices  52.4 us (4%)
  matrix products  49.6 us (4%)
  local copies, waits for them, and re-layouts  48.9 us (4%)
  between operations  16.3 us (1%)
  other arithmetic  14.3 us (1%)
    psum x1, blocking collectives, on_device(): lax.psum((local_nk.reshape(-1), local_nv.reshape(-1)), ('clip', 'bank'))  282 us
    pmax x1, blocking collectives, on_device(): peaks_all = lax.pmax(local_peaks, 'bank')  222 us
    psum x1, blocking collectives, on_device(): row_delta = lax.psum(partial_delta, 'bank') + null_prob * null_dp  221 us
    psum x1, blocking collectives, on_device(): sums_all = lax.psum(local_sums * jnp.exp(local_peaks - peaks_all), 'bank')  220 us
    unnamed x2, waiting for transfers between devices  52.4 us
    all_gather x1, blocking collectives, on_device(): lax.all_gather(queries[0], 'bank', axis=0, tiled=True)  48.2 us
    all_gather x1, blocking collectives, on_device(): lax.all_gather(grad_out[0], 'bank', axis=0, tiled=True)  36.2 us
  transfers between devices with their start and end apart: 1, of which 1 were waited for; matrix products, arithmetic and copies ran while one was open for 0% of the time, Pallas kernels for 0%

commit v1 on v0

v1 whole, which is shorter than its diff:
```python
import functools

import jax
import jax.numpy as jnp
from jax import lax
from jax.experimental import pallas as pl
from jax.experimental.pallas import tpu as pltpu
from jax.sharding import Mesh, PartitionSpec as P

HEADS = 12
HD = 128
QTOK = 256
BLK = 128
HW = HEADS * HD
OWN = 4
PAD = 16
SCALE = HD ** (-0.5)
NT = (((1,), (1,)), ((), ()))
TN = (((0,), (0,)), ((), ()))


def dot(a, b, dims):
    return lax.dot_general(a, b, dims, preferred_element_type=jnp.float32)


def with_null(block, null_row):
    return jnp.concatenate([block, jnp.broadcast_to(null_row, (PAD, HD))], axis=0)


def stats_kernel(valid_ref, q_ref, do_ref, k_ref, v_ref, out_ref):
    live = lax.broadcasted_iota(jnp.int32, (BLK, QTOK), 0) < valid_ref[0]
    for h in range(HEADS):
        cols = slice(h * HD, (h + 1) * HD)
        scores = dot(k_ref[:, cols], q_ref[:, cols], NT) * SCALE
        scores = jnp.where(live, scores, -1e30)
        dprobs = dot(v_ref[:, cols], do_ref[:, cols], NT)
        top = jnp.max(scores, axis=0, keepdims=True)
        terms = jnp.where(live, jnp.exp(scores - top), 0.0)
        out_ref[0, h : h + 1, :] = top
        out_ref[1, h : h + 1, :] = jnp.sum(terms, axis=0, keepdims=True)
        out_ref[2, h : h + 1, :] = jnp.sum(terms * dprobs, axis=0, keepdims=True)


def merge_kernel(in_ref, out_ref):
    tops = in_ref[:, 0]
    top = jnp.max(tops, axis=0)
    weight = jnp.exp(tops - top[None])
    out_ref[0] = top
    out_ref[1] = jnp.sum(in_ref[:, 1] * weight, axis=0)
    out_ref[2] = jnp.sum(in_ref[:, 2] * weight, axis=0)


def grad_kernel(
    place_ref, parts_ref, q_ref, do_ref, k_ref, v_ref, nk_ref, nv_ref, dq_ref, dk_ref, dv_ref, null_ref
):
    live = lax.broadcasted_iota(jnp.int32, (BLK, QTOK), 0) < place_ref[0]
    first = place_ref[1] * OWN
    column = lax.broadcasted_iota(jnp.int32, (PAD, QTOK), 1)
    pad_row = lax.broadcasted_iota(jnp.int32, (PAD, QTOK), 0)
    own = (column >= first) & (column < first + OWN)
    tops = parts_ref[:, 0]
    bank_top = jnp.max(tops, axis=0)
    weight = jnp.exp(tops - bank_top[None])
    bank_sum = jnp.sum(parts_ref[:, 1] * weight, axis=0)
    bank_dot = jnp.sum(parts_ref[:, 2] * weight, axis=0)

    def hi_lo(row):
        hi = row.astype(jnp.bfloat16).astype(jnp.float32)
        return jnp.where(pad_row == 0, hi, jnp.where(pad_row == 1, row - hi, 0.0))

    for h in range(HEADS):
        cols = slice(h * HD, (h + 1) * HD)
        q, do = q_ref[:, cols], do_ref[:, cols]
        keys = with_null(k_ref[:, cols], nk_ref[:, cols])
        vals = with_null(v_ref[:, cols], nv_ref[:, cols])
        scores = dot(keys, q, NT) * SCALE
        dprobs = dot(vals, do, NT)
        null_score = scores[BLK : BLK + 1]
        null_dp = dprobs[BLK : BLK + 1]
        top = jnp.maximum(bank_top[h : h + 1], null_score)
        rest = jnp.exp(bank_top[h : h + 1] - top)
        null_term = jnp.exp(null_score - top)
        total = bank_sum[h : h + 1] * rest + null_term
        delta = (bank_dot[h : h + 1] * rest + null_term * null_dp) / total
        lse = top + jnp.log(total)
        probs = jnp.exp(jnp.where(live, scores[:BLK], -1e30) - lse)
        null_prob = jnp.exp(null_score - lse)
        dscore = (probs * (dprobs[:BLK] - delta)).astype(jnp.bfloat16)
        null_ds = hi_lo(null_prob * (null_dp - delta))
        null_pb = hi_lo(null_prob)
        wide_ds = jnp.concatenate([dscore, null_ds.astype(jnp.bfloat16)], axis=0)
        wide_pb = jnp.concatenate([probs.astype(jnp.bfloat16), null_pb.astype(jnp.bfloat16)], axis=0)
        own_ds = jnp.concatenate([dscore, jnp.where(own, null_ds, 0.0).astype(jnp.bfloat16)], axis=0)
        grad_k = jnp.dot(wide_ds, q, preferred_element_type=jnp.float32) * SCALE
        grad_v = jnp.dot(wide_pb, do, preferred_element_type=jnp.float32)
        dk_ref[:, cols] = grad_k[:BLK].astype(jnp.bfloat16)
        dv_ref[:, cols] = grad_v[:BLK].astype(jnp.bfloat16)
        null_ref[0:1, cols] = jnp.sum(grad_k[BLK:], axis=0, keepdims=True)
        null_ref[1:2, cols] = jnp.sum(grad_v[BLK:], axis=0, keepdims=True)
        dq_ref[:, cols] = (dot(own_ds, keys, TN) * SCALE).astype(jnp.bfloat16)


VMEM = pl.BlockSpec(memory_space=pltpu.VMEM)
SMEM = pl.BlockSpec(memory_space=pltpu.SMEM)
PARAMS = pltpu.CompilerParams(vmem_limit_bytes=32 * 1024 * 1024)


def spread(block, axes, count):
    return lax.all_to_all(jnp.broadcast_to(block[None], (count,) + block.shape), axes, 0, 0)


def on_device(queries, keys, values, grad_out, null_key, null_value, bank_counts, block_slot):
    bank = ("y", "z")
    valid = jnp.clip(bank_counts[0] - block_slot[0, 0] * BLK, 0, BLK)
    place = jnp.stack([valid, lax.axis_index(bank).astype(jnp.int32)])
    mine = jnp.concatenate([queries[0], grad_out[0]], axis=1)
    whole = spread(mine, bank, 64).reshape(QTOK, 2 * HW)
    whole_q, whole_do = whole[:, :HW], whole[:, HW:]
    parts = pl.pallas_call(
        stats_kernel,
        out_shape=jax.ShapeDtypeStruct((3, HEADS, QTOK), jnp.float32),
        in_specs=[SMEM, VMEM, VMEM, VMEM, VMEM],
        out_specs=VMEM,
        compiler_params=PARAMS,
        name="stats",
    )(place, whole_q, whole_do, keys[0], values[0])
    merged = pl.pallas_call(
        merge_kernel,
        out_shape=jax.ShapeDtypeStruct((3, HEADS, QTOK), jnp.float32),
        in_specs=[VMEM],
        out_specs=VMEM,
        compiler_params=PARAMS,
        name="merge",
    )(spread(parts, "z", 8))
    grad_q, grad_k, grad_v, nulls = pl.pallas_call(
        grad_kernel,
        out_shape=(
            jax.ShapeDtypeStruct((QTOK, HW), jnp.bfloat16),
            jax.ShapeDtypeStruct((BLK, HW), jnp.bfloat16),
            jax.ShapeDtypeStruct((BLK, HW), jnp.bfloat16),
            jax.ShapeDtypeStruct((2, HW), jnp.float32),
        ),
        in_specs=[SMEM] + [VMEM] * 7,
        out_specs=(VMEM,) * 4,
        compiler_params=PARAMS,
        name="grads",
    )(
        place,
        spread(merged, "y", 8),
        whole_q,
        whole_do,
        keys[0],
        values[0],
        null_key.reshape(1, HW),
        null_value.reshape(1, HW),
    )
    terms = lax.all_to_all(grad_q.reshape(64, OWN, HW), bank, 0, 0)
    own_q = jnp.sum(terms.astype(jnp.float32), axis=0).astype(jnp.bfloat16)
    null_sum = jnp.sum(spread(nulls, "clip", 8), axis=0)
    return (own_q[None], grad_k[None], grad_v[None], null_sum[0], null_sum[1])


def solution(mesh):
    grid = Mesh(mesh.devices.reshape(8, 8, 8), ("clip", "y", "z"))
    rows = P("clip", ("y", "z"), None)
    return jax.shard_map(
        on_device,
        mesh=grid,
        in_specs=(rows, rows, rows, rows, P(), P(), P("clip"), P("clip", ("y", "z"))),
        out_specs=(rows, rows, rows, P(), P()),
        check_vma=False,
    )
```

time: 1220 us -> 147 us (0.12)
  the two profiles are of different devices: /device:TPU:1 before, /device:TPU:16 now
where the time goes in v1:
time: 147 us
  waiting for transfers between devices  77.7 us (53%)
  starting transfers between devices  35.3 us (24%)
  blocking collectives  15.3 us (10%)
  local copies, waits for them, and re-layouts  8.34 us (6%)
  Pallas kernels  6.24 us (4%)
  between operations  2.04 us (1%)
  other arithmetic  1.8 us (1%)
    all_to_all x3, waiting for transfers between devices, spread(): lax.all_to_all(jnp.broadcast_to(block[None], (count,) + block.shape), axe...  53.3 us
    all_to_all x3, starting transfers between devices, spread(): lax.all_to_all(jnp.broadcast_to(block[None], (count,) + block.shape), axe...  27.9 us
    all_to_all x1, waiting for transfers between devices, on_device(): terms = lax.all_to_all(grad_q.reshape(64, OWN, HW), bank, 0, 0)  24.4 us
    all_to_all x1, blocking collectives, spread(): lax.all_to_all(jnp.broadcast_to(block[None], (count,) + block.shape), axe...  15.3 us
    all_to_all x1, starting transfers between devices, on_device(): terms = lax.all_to_all(grad_q.reshape(64, OWN, HW), bank, 0, 0)  7.36 us
    pallas_call x1, Pallas kernels, on_device(): pl.pallas_call(grad_kernel, out_shape=(jax.ShapeDtypeStruct((QTOK, HW), j...  4.82 us
    broadcast_in_dim x4, local copies, waits for them, and re-layouts, spread(): jnp.broadcast_to(block[None], (count,) + block.shape)  3.04 us
  transfers between devices with their start and end apart: 4, of which 4 were waited for; matrix products, arithmetic and copies ran while one was open for 1% of the time, Pallas kernels for 0%

profile of v1, /device:TPU:16, one launch (start us, length us, event | category | flops | bytes accessed | tf_op | source)
XLA Modules:
  0.0 146.7 jit_solution(13785249620123945759)
XLA Ops:
  0.6 0.7 pad_maximum_fusion
  1.4 1.6 %broadcast_in_dim.14 = bf16[64,4,3072]{2,1,0:T(4,128)(2,1)} broadcast(bf16[4,3072]{1,0:T(4,128)(2,1)S(1)} %pad_maximum_fusion), dimensions={1,2} | broadcast | bytes 1597440 | tf_op jit(solution)/shard_map/broadcast_in_dim | solution.py:109
  2.9 16.5 %all-to-all-start = ((bf16[64,4,3072]{2,1,0:T(4,128)(2,1)}), bf16[64,4,3072]{2,1,0:T(4,128)(2,1)S(1)}, u32[]{:S(2)}, u32[]{:S(2)}) async-start(bf16[64,4,3072]{2,1,0:T(4,128)(2,1)} %broadcast_in_dim.14), calls=%async_computation | async-start | bytes 3145728 | tf_op jit(solution)/shard_map/all_to_all | solution.py:109
  20.7 0.1 pad_add_fusion.valid_ref.place_ref
  20.8 39.7 %all-to-all-done = bf16[64,4,3072]{2,1,0:T(4,128)(2,1)S(1)} async-done(((bf16[64,4,3072]{2,1,0:T(4,128)(2,1)}), bf16[64,4,3072]{2,1,0:T(4,128)(2,1)S(1)}, u32[]{:S(2)}, u32[]{:S(2)}) %all-to-all-start) | async-done | bytes 1572896 | tf_op jit(solution)/shard_map/all_to_all | solution.py:109
  60.5 1.3 reshape.28
  61.9 1.5 %fusion = (bf16[256,1536]{1,0:T(8,128)(2,1)S(1)}, bf16[256,1536]{1,0:T(8,128)(2,1)S(1)}) fusion(bf16[256,3072]{1,0:T(8,128)(2,1)} %reshape.28), kind=kLoop, calls=%fused_computation.4 | loop fusion | bytes 3145728 | tf_op jit(solution)/shard_map/slice | solution.py:118
  63.5 0.0 copy-done.1
  63.5 1.4 stats.1
  64.8 0.0 copy-start.4
  64.9 15.3 %all_to_all.25.in_ref = f32[8,3,12,256]{3,2,1,0:T(8,128)S(1)} all-to-all(f32[8,3,12,256]{3,2,1,0:T(8,128)S(1)} %broadcast_in_dim.15), channel_id=1, replica_groups=mesh['clip'=8,'y'=8,'z'=8] {'z'}, dimensions={0} | all-to-all | bytes 589824 | tf_op jit(solution)/shard_map/all_to_all | solution.py:109
  80.3 0.8 broadcast_in_dim.16
  81.0 7.2 %all-to-all-start.2 = ((f32[8,3,12,256]{3,2,1,0:T(8,128)}), f32[8,3,12,256]{3,2,1,0:T(8,128)S(1)}, u32[]{:S(2)}, u32[]{:S(2)}) async-start(f32[8,3,12,256]{3,2,1,0:T(8,128)} %broadcast_in_dim.16), calls=%async_computation.2 | async-start | bytes 786432 | tf_op jit(solution)/shard_map/all_to_all | solution.py:109
  88.2 8.9 %all-to-all-done.2.parts_ref = f32[8,3,12,256]{3,2,1,0:T(8,128)S(1)} async-done(((f32[8,3,12,256]{3,2,1,0:T(8,128)}), f32[8,3,12,256]{3,2,1,0:T(8,128)S(1)}, u32[]{:S(2)}, u32[]{:S(2)}) %all-to-all-start.2) | async-done | bytes 294944 | tf_op jit(solution)/shard_map/all_to_all | solution.py:109
  97.1 0.7 copy-done.3
  97.8 4.8 %grads.1 = (bf16[256,1536]{1,0:T(8,128)(2,1)S(1)}, bf16[128,1536]{1,0:T(8,128)(2,1)}, bf16[128,1536]{1,0:T(8,128)(2,1)}, f32[2,1536]{1,0:T(2,128)S(1)}) custom-call(s32[2]{0:T(128)S(1)} %copy-done.3, f32[8,3,12,256]{3,2,1,0:T(8,128)S(1)} %all-to-all-done.2.parts_ref, bf16[256,1536]{1,0:T(8,128)(2,1)S(1)} %get-tuple-element.16.q_ref, ...), custom_call_target="tpu_custom_call" | custom-call | tf_op jit(solution)/shard_map/grads/pallas_call | solution.py:135
  102.6 0.7 broadcast_in_dim.39
  103.3 4.3 %all-to-all-start.4 = ((f32[8,2,1536]{2,1,0:T(2,128)}), f32[8,2,1536]{2,1,0:T(2,128)S(1)}, u32[]{:S(2)}, u32[]{:S(2)}) async-start(f32[8,2,1536]{2,1,0:T(2,128)} %broadcast_in_dim.39), calls=%async_computation.4 | async-start | bytes 196608 | tf_op jit(solution)/shard_map/all_to_all | solution.py:109
  107.6 1.1 reshape.31
  108.6 4.7 %all-to-all-done.4 = f32[8,2,1536]{2,1,0:T(2,128)S(1)} async-done(((f32[8,2,1536]{2,1,0:T(2,128)}), f32[8,2,1536]{2,1,0:T(2,128)S(1)}, u32[]{:S(2)}, u32[]{:S(2)}) %all-to-all-start.4) | async-done | bytes 98336 | tf_op jit(solution)/shard_map/all_to_all | solution.py:109
  113.4 7.4 %all-to-all-start.3 = ((bf16[64,4,1536]{2,1,0:T(4,128)(2,1)}), bf16[64,4,1536]{2,1,0:T(4,128)(2,1)S(1)}, u32[]{:S(2)}, u32[]{:S(2)}) async-start(bf16[64,4,1536]{2,1,0:T(4,128)(2,1)} %reshape.31), calls=%async_computation.3 | async-start | bytes 1572864 | tf_op jit(solution)/shard_map/all_to_all | solution.py:157
  120.8 0.6 slice_reduce_fusion
  121.4 24.4 %all-to-all-done.3 = bf16[64,4,1536]{2,1,0:T(4,128)(2,1)S(1)} async-done(((bf16[64,4,1536]{2,1,0:T(4,128)(2,1)}), bf16[64,4,1536]{2,1,0:T(4,128)(2,1)S(1)}, u32[]{:S(2)}, u32[]{:S(2)}) %all-to-all-start.3) | async-done | bytes 786464 | tf_op jit(solution)/shard_map/all_to_all | solution.py:157
  145.8 0.9 reduce_sum.21
  (14 shorter events, 0.2 us)
Async XLA Ops:
  2.9 57.6 %all-to-all-start = ((bf16[64,4,3072]{2,1,0:T(4,128)(2,1)}), bf16[64,4,3072]{2,1,0:T(4,128)(2,1)S(1)}, u32[]{:S(2)}, u32[]{:S(2)}) async-start(bf16[64,4,3072]{2,1,0:T(4,128)(2,1)} %broadcast_in_dim.14), calls=%async_computation | async-start | bytes 3145728 | tf_op jit(solution)/shard_map/all_to_all | solution.py:109
  20.8 42.6 %copy-start.2 = (s32[2]{0:T(128)}, s32[2]{0:T(128)S(1)}, u32[]{:S(2)}) copy-start(s32[2]{0:T(128)S(1)} %pad_add_fusion.valid_ref.place_ref) | copy-start | bytes 28
  61.9 1.6 %copy-start = (bf16[1,128,1536]{2,1,0:T(8,128)(2,1)S(1)}, bf16[1,128,1536]{2,1,0:T(8,128)(2,1)}, u32[]{:S(2)}) copy-start(bf16[1,128,1536]{2,1,0:T(8,128)(2,1)} %param.9) | copy-start | bytes 1179652
  61.9 1.6 %copy-start.1 = (bf16[1,128,1536]{2,1,0:T(8,128)(2,1)S(1)}, bf16[1,128,1536]{2,1,0:T(8,128)(2,1)}, u32[]{:S(2)}) copy-start(bf16[1,128,1536]{2,1,0:T(8,128)(2,1)} %param.10) | copy-start | bytes 1179652
  64.8 23.4 %copy-start.4 = (bf16[1536]{0:T(1024)(128)(2,1)S(1)}, bf16[1536]{0:T(1024)(128)(2,1)}, u32[]{:S(2)}) copy-start(bf16[1536]{0:T(1024)(128)(2,1)} %param.12) | copy-start | bytes 9220
  64.9 23.4 %copy-start.5 = (bf16[1536]{0:T(1024)(128)(2,1)S(1)}, bf16[1536]{0:T(1024)(128)(2,1)}, u32[]{:S(2)}) copy-start(bf16[1536]{0:T(1024)(128)(2,1)} %param.13) | copy-start | bytes 9220
  81.0 16.1 %all-to-all-start.2 = ((f32[8,3,12,256]{3,2,1,0:T(8,128)}), f32[8,3,12,256]{3,2,1,0:T(8,128)S(1)}, u32[]{:S(2)}, u32[]{:S(2)}) async-start(f32[8,3,12,256]{3,2,1,0:T(8,128)} %broadcast_in_dim.16), calls=%async_computation.2 | async-start | bytes 786432 | tf_op jit(solution)/shard_map/all_to_all | solution.py:109
  97.1 0.7 copy-start.3
  103.3 10.1 %all-to-all-start.4 = ((f32[8,2,1536]{2,1,0:T(2,128)}), f32[8,2,1536]{2,1,0:T(2,128)S(1)}, u32[]{:S(2)}, u32[]{:S(2)}) async-start(f32[8,2,1536]{2,1,0:T(2,128)} %broadcast_in_dim.39), calls=%async_computation.4 | async-start | bytes 196608 | tf_op jit(solution)/shard_map/all_to_all | solution.py:109
  113.4 32.4 %all-to-all-start.3 = ((bf16[64,4,1536]{2,1,0:T(4,128)(2,1)}), bf16[64,4,1536]{2,1,0:T(4,128)(2,1)S(1)}, u32[]{:S(2)}, u32[]{:S(2)}) async-start(bf16[64,4,1536]{2,1,0:T(4,128)(2,1)} %reshape.31), calls=%async_computation.3 | async-start | bytes 1572864 | tf_op jit(solution)/shard_map/all_to_all | solution.py:157

commit v2 on v1

v2 whole, which is shorter than its diff:
```python
import jax
import jax.numpy as jnp
from jax import lax
from jax.experimental import pallas as pl
from jax.experimental.pallas import tpu as pltpu
from jax.sharding import Mesh, PartitionSpec as P

HEADS = 12
HD = 128
QTOK = 256
BLK = 128
OWN = 4
QUAD = 4
MINE = HEADS // QUAD
WIDTH = MINE * HD
SLOTS = QUAD * BLK
PAD = 16
SCALE = HD ** (-0.5)
NT = (((1,), (1,)), ((), ()))
TN = (((0,), (0,)), ((), ()))
BANK = ("yq", "yb", "zq", "zb")
NEAR = ("yb", "zb")
FAR = ("yq", "zq")


def dot(a, b, dims):
    return lax.dot_general(a, b, dims, preferred_element_type=jnp.float32)


def columns_of(group):
    return pl.ds(pl.multiple_of(group * WIDTH, WIDTH), WIDTH)


def share_kernel(place_ref, k_ref, v_ref, *out_refs):
    live = jnp.broadcast_to((place_ref[0] > 0).astype(jnp.float32), (PAD, WIDTH)).astype(jnp.bfloat16)
    for hop, out_ref in enumerate(out_refs):
        cols = columns_of(place_ref[1] ^ hop)
        out_ref[:BLK] = k_ref[:, cols]
        out_ref[BLK : 2 * BLK] = v_ref[:, cols]
        out_ref[2 * BLK :] = live


def join_kernel(place_ref, *refs):
    for hop in range(QUAD):
        cols = columns_of(place_ref[1] ^ hop)
        refs[QUAD][:, cols] = refs[hop][:BLK]
        refs[QUAD + 1][:, cols] = refs[hop][BLK:]


def bank_scores(keys, q, blocks):
    scores = dot(keys, q, NT) * SCALE
    pieces = []
    for at, block in enumerate(blocks):
        live = block[2 * BLK :, :QTOK].astype(jnp.float32)[:1]
        bias = jnp.where(live > 0.5, 0.0, -1e30)
        pieces.append(scores[at * BLK : (at + 1) * BLK] + bias)
    return jnp.concatenate(pieces, axis=0), scores[SLOTS:]


def stats_kernel(qd_ref, b0, b1, b2, b3, out_ref):
    blocks = (b0, b1, b2, b3)
    for h in range(MINE):
        cols = slice(h * HD, (h + 1) * HD)
        q, do = qd_ref[:, cols], qd_ref[:, WIDTH + h * HD : WIDTH + (h + 1) * HD]
        keys = jnp.concatenate([b[:BLK, cols] for b in blocks], axis=0)
        vals = jnp.concatenate([b[BLK : 2 * BLK, cols] for b in blocks], axis=0)
        scores, _ = bank_scores(keys, q, blocks)
        dprobs = dot(vals, do, NT)
        top = jnp.max(scores, axis=0, keepdims=True)
        terms = jnp.exp(scores - top)
        rows = (top, jnp.sum(terms, axis=0, keepdims=True), jnp.sum(terms * dprobs, axis=0, keepdims=True))
        for at, row in enumerate(rows):
            out_ref[:, at, h : h + 1, :] = jnp.broadcast_to(row[None], (out_ref.shape[0], 1, QTOK))


def grad_kernel(place_ref, parts_ref, qd_ref, b0, b1, b2, b3, nk_ref, nv_ref, dq_ref, d0, d1, d2, d3, null_ref):
    blocks, outs = (b0, b1, b2, b3), (d0, d1, d2, d3)
    owner = lax.broadcasted_iota(jnp.int32, (PAD, QTOK), 1) // OWN
    pad_row = lax.broadcasted_iota(jnp.int32, (PAD, QTOK), 0)
    ours = ((owner >> 4) == place_ref[2]) & (((owner >> 1) & 3) == place_ref[3])
    tops = parts_ref[:, 0]
    bank_top = jnp.max(tops, axis=0)
    weight = jnp.exp(tops - bank_top[None])
    bank_sum = jnp.sum(parts_ref[:, 1] * weight, axis=0)
    bank_dot = jnp.sum(parts_ref[:, 2] * weight, axis=0)

    def hi_lo(row):
        hi = row.astype(jnp.bfloat16).astype(jnp.float32)
        return jnp.where(pad_row == 0, hi, jnp.where(pad_row == 1, row - hi, 0.0))

    def null_rows(ref, h):
        row = ref[:, columns_of(place_ref[1])][:, h * HD : (h + 1) * HD]
        return jnp.broadcast_to(row, (PAD, HD))

    for h in range(MINE):
        cols = slice(h * HD, (h + 1) * HD)
        q, do = qd_ref[:, cols], qd_ref[:, WIDTH + h * HD : WIDTH + (h + 1) * HD]
        keys = jnp.concatenate([b[:BLK, cols] for b in blocks] + [null_rows(nk_ref, h)], axis=0)
        vals = jnp.concatenate([b[BLK : 2 * BLK, cols] for b in blocks] + [null_rows(nv_ref, h)], axis=0)
        scores, null_scores = bank_scores(keys, q, blocks)
        dprobs = dot(vals, do, NT)
        null_score = null_scores[:1]
        null_dp = dprobs[SLOTS : SLOTS + 1]
        top = jnp.maximum(bank_top[h : h + 1], null_score)
        rest = jnp.exp(bank_top[h : h + 1] - top)
        null_term = jnp.exp(null_score - top)
        total = bank_sum[h : h + 1] * rest + null_term
        delta = (bank_dot[h : h + 1] * rest + null_term * null_dp) / total
        lse = top + jnp.log(total)
        probs = jnp.exp(scores - lse)
        null_prob = jnp.exp(null_score - lse)
        dscore = (probs * (dprobs[:SLOTS] - delta)).astype(jnp.bfloat16)
        null_ds = hi_lo(null_prob * (null_dp - delta))
        null_pb = hi_lo(null_prob)
        wide_ds = jnp.concatenate([dscore, null_ds.astype(jnp.bfloat16)], axis=0)
        wide_pb = jnp.concatenate([probs.astype(jnp.bfloat16), null_pb.astype(jnp.bfloat16)], axis=0)
        own_ds = jnp.concatenate([dscore, jnp.where(ours, null_ds, 0.0).astype(jnp.bfloat16)], axis=0)
        grad_k = jnp.dot(wide_ds, q, preferred_element_type=jnp.float32) * SCALE
        grad_v = jnp.dot(wide_pb, do, preferred_element_type=jnp.float32)
        for at, out in enumerate(outs):
            out[:BLK, cols] = grad_k[at * BLK : (at + 1) * BLK].astype(jnp.bfloat16)
            out[BLK:, cols] = grad_v[at * BLK : (at + 1) * BLK].astype(jnp.bfloat16)
        for at, grad in enumerate((grad_k, grad_v)):
            row = jnp.sum(grad[SLOTS:], axis=0, keepdims=True)
            null_ref[:, at : at + 1, cols] = jnp.broadcast_to(row[None], (null_ref.shape[0], 1, HD))
        dq_ref[:, cols] = (dot(own_ds, keys, TN) * SCALE).astype(jnp.bfloat16)


VMEM = pl.BlockSpec(memory_space=pltpu.VMEM)
SMEM = pl.BlockSpec(memory_space=pltpu.SMEM)


def kernel(body, name, ins, *outs):
    return pl.pallas_call(
        body,
        out_shape=tuple(jax.ShapeDtypeStruct(shape, dtype) for shape, dtype in outs),
        in_specs=ins,
        out_specs=(VMEM,) * len(outs),
        compiler_params=pltpu.CompilerParams(vmem_limit_bytes=32 * 1024 * 1024),
        name=name,
    )


def swap(blocks):
    return [blocks[0]] + [
        lax.ppermute(blocks[hop], NEAR, [(i, i ^ hop) for i in range(QUAD)]) for hop in range(1, QUAD)
    ]


def on_device(queries, keys, values, grad_out, null_key, null_value, bank_counts, block_slot):
    bf16, f32 = jnp.bfloat16, jnp.float32
    valid = jnp.clip(bank_counts[0] - block_slot[0, 0] * BLK, 0, BLK)
    place = jnp.stack(
        [valid] + [lax.axis_index(axes).astype(jnp.int32) for axes in (NEAR, "yq", "zq")]
    )
    pieces = jnp.stack([queries[0], grad_out[0]], axis=1).reshape(OWN, 2, 2, 2, WIDTH)
    pieces = pieces.transpose(2, 3, 0, 1, 4).reshape(1, 2, 1, 2, OWN, 2 * WIDTH)
    outgoing = jnp.broadcast_to(pieces, (4, 2, 4, 2, OWN, 2 * WIDTH)).reshape(64, OWN, 2 * WIDTH)
    whole = lax.all_to_all(outgoing, BANK, 0, 0).reshape(QTOK, 2 * WIDTH)
    blocks = swap(
        kernel(share_kernel, "share", [SMEM, VMEM, VMEM], *[((2 * BLK + PAD, WIDTH), bf16)] * QUAD)(
            place, keys[0], values[0]
        )
    )
    (parts,) = kernel(stats_kernel, "stats", [VMEM] * 5, ((16, 3, MINE, QTOK), f32))(whole, *blocks)
    parts = lax.all_to_all(parts, FAR, 0, 0)
    grad_q, *grad_kv, nulls = kernel(
        grad_kernel,
        "grads",
        [SMEM] + [VMEM] * 8,
        ((QTOK, WIDTH), bf16),
        *[((2 * BLK, WIDTH), bf16)] * QUAD,
        ((32, 2, WIDTH), f32),
    )(place, parts, whole, *blocks, null_key[None], null_value[None])
    terms = lax.all_to_all(grad_q.reshape(64, OWN, WIDTH), BANK, 0, 0).reshape(4, 2, 4, 2, OWN, WIDTH)
    own_q = jnp.sum(terms.astype(f32), axis=(0, 2)).astype(bf16).reshape(QUAD, OWN, WIDTH)
    own_q = own_q.transpose(1, 0, 2).reshape(1, OWN, HEADS * HD)
    grad_k, grad_v = kernel(
        join_kernel, "join", [SMEM] + [VMEM] * QUAD, *[((BLK, HEADS * HD), bf16)] * 2
    )(place, *swap(grad_kv))
    nulls = lax.all_to_all(nulls, ("clip",) + NEAR, 0, 0).reshape(8, QUAD, 2, WIDTH)
    nulls = jnp.sum(nulls, axis=0)
    return (own_q, grad_k[None], grad_v[None], nulls[:, 0].reshape(-1), nulls[:, 1].reshape(-1))


def solution(mesh):
    grid = Mesh(mesh.devices.reshape(8, 4, 2, 4, 2), ("clip",) + BANK)
    rows = P("clip", BANK, None)
    return jax.shard_map(
        on_device,
        mesh=grid,
        in_specs=(rows, rows, rows, rows, P(), P(), P("clip"), P("clip", BANK)),
        out_specs=(rows, rows, rows, P(), P()),
        check_vma=False,
    )
```

time: 147 us -> 105 us (0.71)
  the two profiles are of different devices: /device:TPU:16 before, /device:TPU:1 now
where the time goes in v2:
time: 105 us; the launch traced here: 103 us
  starting transfers between devices  55.9 us (53%)
  waiting for transfers between devices  31.8 us (30%)
  Pallas kernels  6.9 us (7%)
  local copies, waits for them, and re-layouts  5.09 us (5%)
  between operations  2.09 us (2%)
    all_to_all x1, starting transfers between devices, on_device(): whole = lax.all_to_all(outgoing, BANK, 0, 0).reshape(QTOK, 2 * WIDTH)  17.3 us
    ppermute x6, starting transfers between devices, swap(): lax.ppermute(blocks[hop], NEAR, [(i, i ^ hop) for i in range(QUAD)])  16.7 us
    all_to_all x1, waiting for transfers between devices, on_device(): parts = lax.all_to_all(parts, FAR, 0, 0)  11.1 us
    ppermute x6, waiting for transfers between devices, swap(): lax.ppermute(blocks[hop], NEAR, [(i, i ^ hop) for i in range(QUAD)])  10.6 us
    all_to_all x1, starting transfers between devices, on_device(): lax.all_to_all(nulls, ('clip',) + NEAR, 0, 0).reshape(8, QUAD, 2, WIDTH)  9.42 us
    all_to_all x1, starting transfers between devices, on_device(): parts = lax.all_to_all(parts, FAR, 0, 0)  7.67 us
    all_to_all x1, waiting for transfers between devices, on_device(): lax.all_to_all(nulls, ('clip',) + NEAR, 0, 0).reshape(8, QUAD, 2, WIDTH)  5.78 us
    all_to_all x1, starting transfers between devices, on_device(): lax.all_to_all(grad_q.reshape(64, OWN, WIDTH), BANK, 0, 0)  4.79 us
  transfers between devices with their start and end apart: 10, of which 6 were waited for; matrix products, arithmetic and copies ran while one was open for 2% of the time, Pallas kernels for 2%

profile of v2, /device:TPU:1, one launch (start us, length us, event | category | flops | bytes accessed | tf_op | source)
XLA Modules:
  0.0 102.7 jit_solution(556696494843630173)
XLA Ops:
  0.6 0.7 stack.27
  1.4 0.7 copy-done.2
  2.2 0.8 broadcast_in_dim.20
  3.0 17.3 %all-to-all-start = ((bf16[64,4,768]{2,1,0:T(4,128)(2,1)}), bf16[64,4,768]{2,1,0:T(4,128)(2,1)S(1)}, u32[]{:S(2)}, u32[]{:S(2)}) async-start(bf16[64,4,768]{2,1,0:T(4,128)(2,1)} %bitcast.7), calls=%async_computation | async-start | bytes 786432 | tf_op jit(solution)/shard_map/all_to_all | solution.py:159
  22.3 2.9 %collective-permute-start = (bf16[272,384]{1,0:T(8,128)(2,1)S(1)}, bf16[272,384]{1,0:T(8,128)(2,1)S(1)}, u32[]{:S(2)}, u32[]{:S(2)}) collective-permute-start(bf16[272,384]{1,0:T(8,128)(2,1)S(1)} %get-tuple-element.18), channel_id=1, source_target_pairs={{0,1},{1,0},{8,9},{9,8},{2,3},{3,2},{10,11},{11,10},{4,5},{5,4},{1... | collective-permute-start | bytes 626696 | tf_op jit(solution)/shard_map/ppermute | solution.py:146
  25.3 3.1 %collective-permute-start.1 = (bf16[272,384]{1,0:T(8,128)(2,1)S(1)}, bf16[272,384]{1,0:T(8,128)(2,1)S(1)}, u32[]{:S(2)}, u32[]{:S(2)}) collective-permute-start(bf16[272,384]{1,0:T(8,128)(2,1)S(1)} %get-tuple-element.19), channel_id=1, source_target_pairs={{0,8},{1,9},{8,0},{9,1},{2,10},{3,11},{10,2},{11,3},{4,12},{5,13},... | collective-permute-start | bytes 626696 | tf_op jit(solution)/shard_map/ppermute | solution.py:146
  28.4 2.4 %collective-permute-start.2 = (bf16[272,384]{1,0:T(8,128)(2,1)S(1)}, bf16[272,384]{1,0:T(8,128)(2,1)S(1)}, u32[]{:S(2)}, u32[]{:S(2)}) collective-permute-start(bf16[272,384]{1,0:T(8,128)(2,1)S(1)} %get-tuple-element.20), channel_id=1, source_target_pairs={{0,9},{1,8},{8,1},{9,0},{2,11},{3,10},{10,3},{11,2},{4,13},{5,12},... | collective-permute-start | bytes 626696 | tf_op jit(solution)/shard_map/ppermute | solution.py:146
  30.7 4.3 %all-to-all-done = bf16[64,4,768]{2,1,0:T(4,128)(2,1)S(1)} async-done(((bf16[64,4,768]{2,1,0:T(4,128)(2,1)}), bf16[64,4,768]{2,1,0:T(4,128)(2,1)S(1)}, u32[]{:S(2)}, u32[]{:S(2)}) %all-to-all-start) | async-done | bytes 393248 | tf_op jit(solution)/shard_map/all_to_all | solution.py:159
  35.1 6.1 %collective-permute-done.b1 = bf16[272,384]{1,0:T(8,128)(2,1)S(1)} collective-permute-done((bf16[272,384]{1,0:T(8,128)(2,1)S(1)}, bf16[272,384]{1,0:T(8,128)(2,1)S(1)}, u32[]{:S(2)}, u32[]{:S(2)}) %collective-permute-start) | collective-permute-done | bytes 208928 | tf_op jit(solution)/shard_map/ppermute | solution.py:146
  41.3 1.6 %stats.1 = f32[16,3,3,256]{3,2,1,0:T(4,128)} custom-call(bf16[256,768]{1,0:T(8,128)(2,1)S(1)} %reshape.41.qd_ref, bf16[272,384]{1,0:T(8,128)(2,1)S(1)} %get-tuple-element.17.b0, bf16[272,384]{1,0:T(8,128)(2,1)S(1)} %collective-permute-done.b1, bf16[272,384]{1,0:T(8,128)(2,1)S(1)} %collective-permute-done.1.b2, bf16[272,384]{1,0:T(8,128)(2,1)S(1)} %collective-permute-done.2.b3), custom_call_target="tpu_custom_call" | custom-call | tf_op jit(solution)/shard_map/stats/pallas_call | solution.py:165
  42.9 7.7 %all-to-all-start.1 = ((f32[16,3,3,256]{3,2,1,0:T(4,128)}), f32[16,3,3,256]{3,2,1,0:T(4,128)S(1)}, u32[]{:S(2)}, u32[]{:S(2)}) async-start(f32[16,3,3,256]{3,2,1,0:T(4,128)} %stats.1), calls=%async_computation.1 | async-start | bytes 393216 | tf_op jit(solution)/shard_map/all_to_all | solution.py:166
  51.3 11.1 %all-to-all-done.1.parts_ref = f32[16,3,3,256]{3,2,1,0:T(4,128)S(1)} async-done(((f32[16,3,3,256]{3,2,1,0:T(4,128)}), f32[16,3,3,256]{3,2,1,0:T(4,128)S(1)}, u32[]{:S(2)}, u32[]{:S(2)}) %all-to-all-start.1) | async-done | bytes 147488 | tf_op jit(solution)/shard_map/all_to_all | solution.py:166
  62.4 3.2 %grads.1 = (bf16[256,384]{1,0:T(8,128)(2,1)S(1)}, bf16[256,384]{1,0:T(8,128)(2,1)S(1)}, bf16[256,384]{1,0:T(8,128)(2,1)S(1)}, bf16[256,384]{1,0:T(8,128)(2,1)S(1...) custom-call(s32[4]{0:T(128)S(1)} %pad_add_fusion.place_ref, f32[16,3,3,256]{3,2,1,0:T(4,128)S(1)} %all-to-all-done.1.parts_ref, ...), custom_call_target="tpu_custom_call" | custom-call | tf_op jit(solution)/shard_map/grads/pallas_call | solution.py:167
  65.5 9.4 %all-to-all-start.3 = ((f32[32,2,384]{2,1,0:T(2,128)}), f32[32,2,384]{2,1,0:T(2,128)S(1)}, u32[]{:S(2)}, u32[]{:S(2)}) async-start(f32[32,2,384]{2,1,0:T(2,128)} %get-tuple-element.28), calls=%async_computation.3 | async-start | bytes 196608 | tf_op jit(solution)/shard_map/all_to_all | solution.py:181
  75.0 0.7 reshape.42
  75.7 5.8 %all-to-all-done.3 = f32[32,2,384]{2,1,0:T(2,128)S(1)} async-done(((f32[32,2,384]{2,1,0:T(2,128)}), f32[32,2,384]{2,1,0:T(2,128)S(1)}, u32[]{:S(2)}, u32[]{:S(2)}) %all-to-all-start.3) | async-done | bytes 98336 | tf_op jit(solution)/shard_map/all_to_all | solution.py:181
  81.5 4.8 %all-to-all-start.2 = ((bf16[64,4,384]{2,1,0:T(4,128)(2,1)}), bf16[64,4,384]{2,1,0:T(4,128)(2,1)S(1)}, u32[]{:S(2)}, u32[]{:S(2)}) async-start(bf16[64,4,384]{2,1,0:T(4,128)(2,1)} %reshape.42), calls=%async_computation.2 | async-start | bytes 393216 | tf_op jit(solution)/shard_map/all_to_all | solution.py:175
  86.3 2.9 %collective-permute-start.3 = (bf16[256,384]{1,0:T(8,128)(2,1)S(1)}, bf16[256,384]{1,0:T(8,128)(2,1)S(1)}, u32[]{:S(2)}, u32[]{:S(2)}) collective-permute-start(bf16[256,384]{1,0:T(8,128)(2,1)S(1)} %get-tuple-element.23), channel_id=1, source_target_pairs={{0,1},{1,0},{8,9},{9,8},{2,3},{3,2},{10,11},{11,10},{4,5},{5,4},{1... | collective-permute-start | bytes 589832 | tf_op jit(solution)/shard_map/ppermute | solution.py:146
  89.2 3.1 %collective-permute-start.4 = (bf16[256,384]{1,0:T(8,128)(2,1)S(1)}, bf16[256,384]{1,0:T(8,128)(2,1)S(1)}, u32[]{:S(2)}, u32[]{:S(2)}) collective-permute-start(bf16[256,384]{1,0:T(8,128)(2,1)S(1)} %get-tuple-element.24), channel_id=1, source_target_pairs={{0,8},{1,9},{8,0},{9,1},{2,10},{3,11},{10,2},{11,3},{4,12},{5,13},... | collective-permute-start | bytes 589832 | tf_op jit(solution)/shard_map/ppermute | solution.py:146
  92.3 2.4 %collective-permute-start.5 = (bf16[256,384]{1,0:T(8,128)(2,1)S(1)}, bf16[256,384]{1,0:T(8,128)(2,1)S(1)}, u32[]{:S(2)}, u32[]{:S(2)}) collective-permute-start(bf16[256,384]{1,0:T(8,128)(2,1)S(1)} %get-tuple-element.25), channel_id=1, source_target_pairs={{0,9},{1,8},{8,1},{9,0},{2,11},{3,10},{10,3},{11,2},{4,13},{5,12},... | collective-permute-start | bytes 589832 | tf_op jit(solution)/shard_map/ppermute | solution.py:146
  96.0 2.0 %collective-permute-done.3.refs_1_ = bf16[256,384]{1,0:T(8,128)(2,1)S(1)} collective-permute-done((bf16[256,384]{1,0:T(8,128)(2,1)S(1)}, bf16[256,384]{1,0:T(8,128)(2,1)S(1)}, u32[]{:S(2)}, u32[]{:S(2)}) %collective-permute-start.3) | collective-permute-done | bytes 196640 | tf_op jit(solution)/shard_map/ppermute | solution.py:146
  98.0 2.5 %collective-permute-done.5.refs_3_ = bf16[256,384]{1,0:T(8,128)(2,1)S(1)} collective-permute-done((bf16[256,384]{1,0:T(8,128)(2,1)S(1)}, bf16[256,384]{1,0:T(8,128)(2,1)S(1)}, u32[]{:S(2)}, u32[]{:S(2)}) %collective-permute-start.5) | collective-permute-done | bytes 196640 | tf_op jit(solution)/shard_map/ppermute | solution.py:146
  100.5 1.5 %join.1 = (bf16[128,1536]{1,0:T(8,128)(2,1)}, bf16[128,1536]{1,0:T(8,128)(2,1)}) custom-call(s32[4]{0:T(128)S(1)} %pad_add_fusion.place_ref, bf16[256,384]{1,0:T(8,128)(2,1)S(1)} %get-tuple-element.22.refs_0_, bf16[256,384]{1,0:T(8,128)(2,1)S(1)} %collective-permute-done.3.refs_1_, bf16[256,384]{1,0:T(8,128)(2,1)S(1)} %collective-permute-done.4.refs_2_, ...), custom_call_target="tpu_custom_call" | custom-call | tf_op jit(solution)/shard_map/join/pallas_call | solution.py:178
  102.0 0.7 reduce_sum.21
  (27 shorter events, 2.9 us)
Async XLA Ops:
  1.4 0.7 copy-start.2
  3.0 18.7 %copy-start = (bf16[1,128,1536]{2,1,0:T(8,128)(2,1)S(1)}, bf16[1,128,1536]{2,1,0:T(8,128)(2,1)}, u32[]{:S(2)}) copy-start(bf16[1,128,1536]{2,1,0:T(8,128)(2,1)} %param.9) | copy-start | bytes 1179652
  3.0 18.7 %copy-start.1 = (bf16[1,128,1536]{2,1,0:T(8,128)(2,1)S(1)}, bf16[1,128,1536]{2,1,0:T(8,128)(2,1)}, u32[]{:S(2)}) copy-start(bf16[1,128,1536]{2,1,0:T(8,128)(2,1)} %param.10) | copy-start | bytes 1179652
  3.0 32.0 %all-to-all-start = ((bf16[64,4,768]{2,1,0:T(4,128)(2,1)}), bf16[64,4,768]{2,1,0:T(4,128)(2,1)S(1)}, u32[]{:S(2)}, u32[]{:S(2)}) async-start(bf16[64,4,768]{2,1,0:T(4,128)(2,1)} %bitcast.7), calls=%async_computation | async-start | bytes 786432 | tf_op jit(solution)/shard_map/all_to_all | solution.py:159
  22.3 18.9 %collective-permute-start = (bf16[272,384]{1,0:T(8,128)(2,1)S(1)}, bf16[272,384]{1,0:T(8,128)(2,1)S(1)}, u32[]{:S(2)}, u32[]{:S(2)}) collective-permute-start(bf16[272,384]{1,0:T(8,128)(2,1)S(1)} %get-tuple-element.18), channel_id=1, source_target_pairs={{0,1},{1,0},{8,9},{9,8},{2,3},{3,2},{10,11},{11,10},{4,5},{5,4},{1... | collective-permute-start | bytes 626696 | tf_op jit(solution)/shard_map/ppermute | solution.py:146
  25.3 16.0 %collective-permute-start.1 = (bf16[272,384]{1,0:T(8,128)(2,1)S(1)}, bf16[272,384]{1,0:T(8,128)(2,1)S(1)}, u32[]{:S(2)}, u32[]{:S(2)}) collective-permute-start(bf16[272,384]{1,0:T(8,128)(2,1)S(1)} %get-tuple-element.19), channel_id=1, source_target_pairs={{0,8},{1,9},{8,0},{9,1},{2,10},{3,11},{10,2},{11,3},{4,12},{5,13},... | collective-permute-start | bytes 626696 | tf_op jit(solution)/shard_map/ppermute | solution.py:146
  28.4 12.9 %collective-permute-start.2 = (bf16[272,384]{1,0:T(8,128)(2,1)S(1)}, bf16[272,384]{1,0:T(8,128)(2,1)S(1)}, u32[]{:S(2)}, u32[]{:S(2)}) collective-permute-start(bf16[272,384]{1,0:T(8,128)(2,1)S(1)} %get-tuple-element.20), channel_id=1, source_target_pairs={{0,9},{1,8},{8,1},{9,0},{2,11},{3,10},{10,3},{11,2},{4,13},{5,12},... | collective-permute-start | bytes 626696 | tf_op jit(solution)/shard_map/ppermute | solution.py:146
  42.9 7.7 %copy-start.3 = (bf16[1536]{0:T(1024)(128)(2,1)S(1)}, bf16[1536]{0:T(1024)(128)(2,1)}, u32[]{:S(2)}) copy-start(bf16[1536]{0:T(1024)(128)(2,1)} %param.12) | copy-start | bytes 9220
  42.9 19.5 %all-to-all-start.1 = ((f32[16,3,3,256]{3,2,1,0:T(4,128)}), f32[16,3,3,256]{3,2,1,0:T(4,128)S(1)}, u32[]{:S(2)}, u32[]{:S(2)}) async-start(f32[16,3,3,256]{3,2,1,0:T(4,128)} %stats.1), calls=%async_computation.1 | async-start | bytes 393216 | tf_op jit(solution)/shard_map/all_to_all | solution.py:166
  50.6 0.7 copy-start.4
  65.5 15.9 %all-to-all-start.3 = ((f32[32,2,384]{2,1,0:T(2,128)}), f32[32,2,384]{2,1,0:T(2,128)S(1)}, u32[]{:S(2)}, u32[]{:S(2)}) async-start(f32[32,2,384]{2,1,0:T(2,128)} %get-tuple-element.28), calls=%async_computation.3 | async-start | bytes 196608 | tf_op jit(solution)/shard_map/all_to_all | solution.py:181
  81.5 20.5 %all-to-all-start.2 = ((bf16[64,4,384]{2,1,0:T(4,128)(2,1)}), bf16[64,4,384]{2,1,0:T(4,128)(2,1)S(1)}, u32[]{:S(2)}, u32[]{:S(2)}) async-start(bf16[64,4,384]{2,1,0:T(4,128)(2,1)} %reshape.42), calls=%async_computation.2 | async-start | bytes 393216 | tf_op jit(solution)/shard_map/all_to_all | solution.py:175
  86.3 11.7 %collective-permute-start.3 = (bf16[256,384]{1,0:T(8,128)(2,1)S(1)}, bf16[256,384]{1,0:T(8,128)(2,1)S(1)}, u32[]{:S(2)}, u32[]{:S(2)}) collective-permute-start(bf16[256,384]{1,0:T(8,128)(2,1)S(1)} %get-tuple-element.23), channel_id=1, source_target_pairs={{0,1},{1,0},{8,9},{9,8},{2,3},{3,2},{10,11},{11,10},{4,5},{5,4},{1... | collective-permute-start | bytes 589832 | tf_op jit(solution)/shard_map/ppermute | solution.py:146
  89.2 8.8 %collective-permute-start.4 = (bf16[256,384]{1,0:T(8,128)(2,1)S(1)}, bf16[256,384]{1,0:T(8,128)(2,1)S(1)}, u32[]{:S(2)}, u32[]{:S(2)}) collective-permute-start(bf16[256,384]{1,0:T(8,128)(2,1)S(1)} %get-tuple-element.24), channel_id=1, source_target_pairs={{0,8},{1,9},{8,0},{9,1},{2,10},{3,11},{10,2},{11,3},{4,12},{5,13},... | collective-permute-start | bytes 589832 | tf_op jit(solution)/shard_map/ppermute | solution.py:146
  92.3 8.2 %collective-permute-start.5 = (bf16[256,384]{1,0:T(8,128)(2,1)S(1)}, bf16[256,384]{1,0:T(8,128)(2,1)S(1)}, u32[]{:S(2)}, u32[]{:S(2)}) collective-permute-start(bf16[256,384]{1,0:T(8,128)(2,1)S(1)} %get-tuple-element.25), channel_id=1, source_target_pairs={{0,9},{1,8},{8,1},{9,0},{2,11},{3,10},{10,3},{11,2},{4,13},{5,12},... | collective-permute-start | bytes 589832 | tf_op jit(solution)/shard_map/ppermute | solution.py:146

commit v3 on v2

--- a/solution.py
+++ b/solution.py
@@ -15,6 +15,7 @@
 WIDTH = MINE * HD
 SLOTS = QUAD * BLK
 PAD = 16
+DEAD = 1024.0
 SCALE = HD ** (-0.5)
 NT = (((1,), (1,)), ((), ()))
 TN = (((0,), (0,)), ((), ()))
@@ -31,13 +32,20 @@
     return pl.ds(pl.multiple_of(group * WIDTH, WIDTH), WIDTH)
 
 
+def outgoing_kernel(q_ref, do_ref, out_ref):
+    for device in range(out_ref.shape[0]):
+        group = ((device >> 3) & 1) * 2 + (device & 1)
+        cols = slice(group * WIDTH, (group + 1) * WIDTH)
+        out_ref[device, :, :WIDTH] = q_ref[:, cols]
+        out_ref[device, :, WIDTH:] = do_ref[:, cols]
+
+
 def share_kernel(place_ref, k_ref, v_ref, *out_refs):
-    live = jnp.broadcast_to((place_ref[0] > 0).astype(jnp.float32), (PAD, WIDTH)).astype(jnp.bfloat16)
+    live = place_ref[0] > 0
     for hop, out_ref in enumerate(out_refs):
         cols = columns_of(place_ref[1] ^ hop)
-        out_ref[:BLK] = k_ref[:, cols]
-        out_ref[BLK : 2 * BLK] = v_ref[:, cols]
-        out_ref[2 * BLK :] = live
+        out_ref[:BLK] = jnp.where(live, k_ref[:, cols], jnp.bfloat16(DEAD))
+        out_ref[BLK:] = v_ref[:, cols]
 
 
 def join_kernel(place_ref, *refs):
@@ -51,8 +59,8 @@
     scores = dot(keys, q, NT) * SCALE
     pieces = []
     for at, block in enumerate(blocks):
-        live = block[2 * BLK :, :QTOK].astype(jnp.float32)[:1]
-        bias = jnp.where(live > 0.5, 0.0, -1e30)
+        mark = block[:PAD, :QTOK].astype(jnp.float32)[:1]
+        bias = jnp.where(mark < 0.5 * DEAD, 0.0, -1e30)
         pieces.append(scores[at * BLK : (at + 1) * BLK] + bias)
     return jnp.concatenate(pieces, axis=0), scores[SLOTS:]
 
@@ -73,7 +81,7 @@
             out_ref[:, at, h : h + 1, :] = jnp.broadcast_to(row[None], (out_ref.shape[0], 1, QTOK))
 
 
-def grad_kernel(place_ref, parts_ref, qd_ref, b0, b1, b2, b3, nk_ref, nv_ref, dq_ref, d0, d1, d2, d3, null_ref):
+def grad_kernel(place_ref, parts_ref, qd_ref, b0, b1, b2, b3, nk_ref, nv_ref, dq_ref, d0, d1, d2, d3):
     blocks, outs = (b0, b1, b2, b3), (d0, d1, d2, d3)
     owner = lax.broadcasted_iota(jnp.int32, (PAD, QTOK), 1) // OWN
     pad_row = lax.broadcasted_iota(jnp.int32, (PAD, QTOK), 0)
@@ -120,10 +128,27 @@
         for at, out in enumerate(outs):
             out[:BLK, cols] = grad_k[at * BLK : (at + 1) * BLK].astype(jnp.bfloat16)
             out[BLK:, cols] = grad_v[at * BLK : (at + 1) * BLK].astype(jnp.bfloat16)
-        for at, grad in enumerate((grad_k, grad_v)):
+        null_grads = []
+        for grad in (grad_k, grad_v):
             row = jnp.sum(grad[SLOTS:], axis=0, keepdims=True)
-            null_ref[:, at : at + 1, cols] = jnp.broadcast_to(row[None], (null_ref.shape[0], 1, HD))
-        dq_ref[:, cols] = (dot(own_ds, keys, TN) * SCALE).astype(jnp.bfloat16)
+            hi = row.astype(jnp.bfloat16).astype(jnp.float32)
+            null_grads += [hi, row - hi]
+        null_grads = jnp.broadcast_to(jnp.concatenate(null_grads, axis=0)[None], (QTOK // OWN, 4, HD))
+        grad_q = (dot(own_ds, keys, TN) * SCALE).reshape(QTOK // OWN, OWN, HD)
+        dq_ref[:, :, cols] = jnp.concatenate([grad_q, null_grads], axis=1).astype(jnp.bfloat16)
+
+
+def finish_kernel(terms_ref, q_ref, null_ref):
+    for group in range(QUAD):
+        cols = slice(group * WIDTH, (group + 1) * WIDTH)
+        at = (group >> 1) * 8 + (group & 1)
+        parts = terms_ref[at].astype(jnp.float32)
+        total = parts
+        for far in range(1, 16):
+            total += terms_ref[at + (far >> 2) * 16 + (far & 3) * 2].astype(jnp.float32)
+        q_ref[:, cols] = total[:OWN].astype(jnp.bfloat16)
+        rows = jnp.concatenate([parts[4:5] + parts[5:6], parts[6:7] + parts[7:8]], axis=0)
+        null_ref[:, :, cols] = jnp.broadcast_to(rows[None], (null_ref.shape[0], 2, WIDTH))
 
 
 VMEM = pl.BlockSpec(memory_space=pltpu.VMEM)
@@ -153,34 +178,33 @@
     place = jnp.stack(
         [valid] + [lax.axis_index(axes).astype(jnp.int32) for axes in (NEAR, "yq", "zq")]
     )
-    pieces = jnp.stack([queries[0], grad_out[0]], axis=1).reshape(OWN, 2, 2, 2, WIDTH)
-    pieces = pieces.transpose(2, 3, 0, 1, 4).reshape(1, 2, 1, 2, OWN, 2 * WIDTH)
-    outgoing = jnp.broadcast_to(pieces, (4, 2, 4, 2, OWN, 2 * WIDTH)).reshape(64, OWN, 2 * WIDTH)
+    (outgoing,) = kernel(outgoing_kernel, "outgoing", [VMEM] * 2, ((64, OWN, 2 * WIDTH), bf16))(
+        queries[0], grad_out[0]
+    )
     whole = lax.all_to_all(outgoing, BANK, 0, 0).reshape(QTOK, 2 * WIDTH)
     blocks = swap(
-        kernel(share_kernel, "share", [SMEM, VMEM, VMEM], *[((2 * BLK + PAD, WIDTH), bf16)] * QUAD)(
+        kernel(share_kernel, "share", [SMEM, VMEM, VMEM], *[((2 * BLK, WIDTH), bf16)] * QUAD)(
             place, keys[0], values[0]
         )
     )
     (parts,) = kernel(stats_kernel, "stats", [VMEM] * 5, ((16, 3, MINE, QTOK), f32))(whole, *blocks)
     parts = lax.all_to_all(parts, FAR, 0, 0)
-    grad_q, *grad_kv, nulls = kernel(
+    grad_q, *grad_kv = kernel(
         grad_kernel,
         "grads",
         [SMEM] + [VMEM] * 8,
-        ((QTOK, WIDTH), bf16),
+        ((64, 2 * OWN, WIDTH), bf16),
         *[((2 * BLK, WIDTH), bf16)] * QUAD,
-        ((32, 2, WIDTH), f32),
     )(place, parts, whole, *blocks, null_key[None], null_value[None])
-    terms = lax.all_to_all(grad_q.reshape(64, OWN, WIDTH), BANK, 0, 0).reshape(4, 2, 4, 2, OWN, WIDTH)
-    own_q = jnp.sum(terms.astype(f32), axis=(0, 2)).astype(bf16).reshape(QUAD, OWN, WIDTH)
-    own_q = own_q.transpose(1, 0, 2).reshape(1, OWN, HEADS * HD)
+    terms = lax.all_to_all(grad_q, BANK, 0, 0)
+    own_q, nulls = kernel(
+        finish_kernel, "finish", [VMEM], ((OWN, HEADS * HD), bf16), ((8, 2, HEADS * HD), f32)
+    )(terms)
     grad_k, grad_v = kernel(
         join_kernel, "join", [SMEM] + [VMEM] * QUAD, *[((BLK, HEADS * HD), bf16)] * 2
     )(place, *swap(grad_kv))
-    nulls = lax.all_to_all(nulls, ("clip",) + NEAR, 0, 0).reshape(8, QUAD, 2, WIDTH)
-    nulls = jnp.sum(nulls, axis=0)
-    return (own_q, grad_k[None], grad_v[None], nulls[:, 0].reshape(-1), nulls[:, 1].reshape(-1))
+    nulls = jnp.sum(lax.all_to_all(nulls, "clip", 0, 0), axis=0)
+    return (own_q[None], grad_k[None], grad_v[None], nulls[0], nulls[1])
 
 
 def solution(mesh):

time: 105 us -> 103 us (0.981); the launches traced: 103 us -> 102 us
  starting transfers between devices: 55.9 us -> 59 us
  local copies, waits for them, and re-layouts: 5.09 us -> 2.82 us
  waiting for transfers between devices: 31.8 us -> 29.6 us
  Pallas kernels: 6.9 us -> 8.58 us
    ppermute x6, waiting for transfers between devices: 10.6 us -> 5.6 us  [swap(): lax.ppermute(blocks[hop], NEAR, [(i, i ^ hop) for i in range(QUAD)])]
    all_to_all x2, starting transfers between devices: 14.2 us -> 17.3 us  [the longest x1 10.3 us: on_device(): nulls = jnp.sum(lax.all_to_all(nulls, 'clip', 0, 0), axis=0)]
    all_to_all x2, waiting for transfers between devices: 5.78 us -> 8.62 us  [the longest x1 5.15 us: on_device(): terms = lax.all_to_all(grad_q, BANK, 0, 0)]
    another operation x6 -> x0, local copies, waits for them, and re-layouts: 1.99 us -> none  [the longest x4 0.78 us: on_device(): jnp.stack([queries[0], grad_out[0]], axis=1).reshape(OWN, 2, 2, 2, WIDTH)]
    pallas_call x2 -> x4, Pallas kernels: 3.78 us -> 5.48 us  [the longest x1 3.36 us: on_device(): kernel(grad_kernel, 'grads', [SMEM] + [VMEM] * 8, ((64, 2 * OWN, WIDTH),...]
  transfers between devices with their start and end apart: 10 -> 10, of which waited for: 6 -> 5; matrix products, arithmetic and copies ran while one was open for 2% -> 0% of each run, Pallas kernels for 2% -> 3%
where the time goes in v3:
time: 103 us; the launch traced here: 102 us
  starting transfers between devices  59 us (57%)
  waiting for transfers between devices  29.6 us (29%)
  Pallas kernels  8.58 us (8%)
  local copies, waits for them, and re-layouts  2.82 us (3%)
  between operations  2.08 us (2%)
    all_to_all x1, starting transfers between devices, on_device(): whole = lax.all_to_all(outgoing, BANK, 0, 0).reshape(QTOK, 2 * WIDTH)  17.3 us
    ppermute x6, starting transfers between devices, swap(): lax.ppermute(blocks[hop], NEAR, [(i, i ^ hop) for i in range(QUAD)])  16.8 us
    all_to_all x1, waiting for transfers between devices, on_device(): parts = lax.all_to_all(parts, FAR, 0, 0)  11.1 us
    all_to_all x1, starting transfers between devices, on_device(): nulls = jnp.sum(lax.all_to_all(nulls, 'clip', 0, 0), axis=0)  10.3 us
    all_to_all x1, starting transfers between devices, on_device(): parts = lax.all_to_all(parts, FAR, 0, 0)  7.67 us
    all_to_all x1, starting transfers between devices, on_device(): terms = lax.all_to_all(grad_q, BANK, 0, 0)  6.97 us
    ppermute x6, waiting for transfers between devices, swap(): lax.ppermute(blocks[hop], NEAR, [(i, i ^ hop) for i in range(QUAD)])  5.6 us
    all_to_all x1, waiting for transfers between devices, on_device(): terms = lax.all_to_all(grad_q, BANK, 0, 0)  5.15 us
  transfers between devices with their start and end apart: 10, of which 5 were waited for; matrix products, arithmetic and copies ran while one was open for 0% of the time, Pallas kernels for 3%

profile of v3, /device:TPU:1, one launch (start us, length us, event | category | flops | bytes accessed | tf_op | source)
XLA Modules:
  0.0 102.2 jit_solution(14851596480988213955)
XLA Ops:
  0.6 0.7 copy-done.2
  1.3 0.7 copy-done.3
  2.0 0.8 outgoing.1
  2.8 17.3 %all-to-all-start = ((bf16[64,4,768]{2,1,0:T(4,128)(2,1)}), bf16[64,4,768]{2,1,0:T(4,128)(2,1)S(1)}, u32[]{:S(2)}, u32[]{:S(2)}) async-start(bf16[64,4,768]{2,1,0:T(4,128)(2,1)} %outgoing.1), calls=%async_computation | async-start | bytes 786432 | tf_op jit(solution)/shard_map/all_to_all | solution.py:184
  21.5 0.6 share.1
  22.1 2.9 %collective-permute-start = (bf16[256,384]{1,0:T(8,128)(2,1)S(1)}, bf16[256,384]{1,0:T(8,128)(2,1)S(1)}, u32[]{:S(2)}, u32[]{:S(2)}) collective-permute-start(bf16[256,384]{1,0:T(8,128)(2,1)S(1)} %get-tuple-element.19), channel_id=1, source_target_pairs={{0,1},{1,0},{8,9},{9,8},{2,3},{3,2},{10,11},{11,10},{4,5},{5,4},{1... | collective-permute-start | bytes 589832 | tf_op jit(solution)/shard_map/ppermute | solution.py:171
  25.1 3.1 %collective-permute-start.1 = (bf16[256,384]{1,0:T(8,128)(2,1)S(1)}, bf16[256,384]{1,0:T(8,128)(2,1)S(1)}, u32[]{:S(2)}, u32[]{:S(2)}) collective-permute-start(bf16[256,384]{1,0:T(8,128)(2,1)S(1)} %get-tuple-element.20), channel_id=1, source_target_pairs={{0,8},{1,9},{8,0},{9,1},{2,10},{3,11},{10,2},{11,3},{4,12},{5,13},... | collective-permute-start | bytes 589832 | tf_op jit(solution)/shard_map/ppermute | solution.py:171
  28.2 2.4 %collective-permute-start.2 = (bf16[256,384]{1,0:T(8,128)(2,1)S(1)}, bf16[256,384]{1,0:T(8,128)(2,1)S(1)}, u32[]{:S(2)}, u32[]{:S(2)}) collective-permute-start(bf16[256,384]{1,0:T(8,128)(2,1)S(1)} %get-tuple-element.21), channel_id=1, source_target_pairs={{0,9},{1,8},{8,1},{9,0},{2,11},{3,10},{10,3},{11,2},{4,13},{5,12},... | collective-permute-start | bytes 589832 | tf_op jit(solution)/shard_map/ppermute | solution.py:171
  30.5 4.3 %all-to-all-done = bf16[64,4,768]{2,1,0:T(4,128)(2,1)S(1)} async-done(((bf16[64,4,768]{2,1,0:T(4,128)(2,1)}), bf16[64,4,768]{2,1,0:T(4,128)(2,1)S(1)}, u32[]{:S(2)}, u32[]{:S(2)}) %all-to-all-start) | async-done | bytes 393248 | tf_op jit(solution)/shard_map/all_to_all | solution.py:184
  34.9 5.6 %collective-permute-done.b1 = bf16[256,384]{1,0:T(8,128)(2,1)S(1)} collective-permute-done((bf16[256,384]{1,0:T(8,128)(2,1)S(1)}, bf16[256,384]{1,0:T(8,128)(2,1)S(1)}, u32[]{:S(2)}, u32[]{:S(2)}) %collective-permute-start) | collective-permute-done | bytes 196640 | tf_op jit(solution)/shard_map/ppermute | solution.py:171
  40.5 1.6 %stats.1 = f32[16,3,3,256]{3,2,1,0:T(4,128)} custom-call(bf16[256,768]{1,0:T(8,128)(2,1)S(1)} %reshape.15.qd_ref, bf16[256,384]{1,0:T(8,128)(2,1)S(1)} %get-tuple-element.18.b0, bf16[256,384]{1,0:T(8,128)(2,1)S(1)} %collective-permute-done.b1, bf16[256,384]{1,0:T(8,128)(2,1)S(1)} %collective-permute-done.1.b2, bf16[256,384]{1,0:T(8,128)(2,1)S(1)} %collective-permute-done.2.b3), custom_call_target="tpu_custom_call" | custom-call | tf_op jit(solution)/shard_map/stats/pallas_call | solution.py:190
  42.1 7.7 %all-to-all-start.1 = ((f32[16,3,3,256]{3,2,1,0:T(4,128)}), f32[16,3,3,256]{3,2,1,0:T(4,128)S(1)}, u32[]{:S(2)}, u32[]{:S(2)}) async-start(f32[16,3,3,256]{3,2,1,0:T(4,128)} %stats.1), calls=%async_computation.1 | async-start | bytes 393216 | tf_op jit(solution)/shard_map/all_to_all | solution.py:191
  49.8 0.7 copy-done.5
  50.5 11.1 %all-to-all-done.1.parts_ref = f32[16,3,3,256]{3,2,1,0:T(4,128)S(1)} async-done(((f32[16,3,3,256]{3,2,1,0:T(4,128)}), f32[16,3,3,256]{3,2,1,0:T(4,128)S(1)}, u32[]{:S(2)}, u32[]{:S(2)}) %all-to-all-start.1) | async-done | bytes 147488 | tf_op jit(solution)/shard_map/all_to_all | solution.py:191
  61.6 3.4 %grads.1 = (bf16[64,8,384]{2,1,0:T(8,128)(2,1)}, bf16[256,384]{1,0:T(8,128)(2,1)S(1)}, bf16[256,384]{1,0:T(8,128)(2,1)S(1)}, bf16[256,384]{1,0:T(8,128)(2,1)S(1)}, bf16[256,384]{1,0:T(8,128)(2,1)S(1)}) custom-call(s32[4]{0:T(128)S(1)} %pad_add_fusion.place_ref, f32[16,3,3,256]{3,2,1,0:T(4,128)S(1)} %all-to-all-done.1.parts_ref, ...), custom_call_target="tpu_custom_call" | custom-call | tf_op jit(solution)/shard_map/grads/pallas_call | solution.py:192
  65.0 7.0 %all-to-all-start.2 = ((bf16[64,8,384]{2,1,0:T(8,128)(2,1)}), bf16[64,8,384]{2,1,0:T(8,128)(2,1)S(1)}, u32[]{:S(2)}, u32[]{:S(2)}) async-start(bf16[64,8,384]{2,1,0:T(8,128)(2,1)} %get-tuple-element.22), calls=%async_computation.2 | async-start | bytes 786432 | tf_op jit(solution)/shard_map/all_to_all | solution.py:199
  72.0 2.9 %collective-permute-start.3 = (bf16[256,384]{1,0:T(8,128)(2,1)S(1)}, bf16[256,384]{1,0:T(8,128)(2,1)S(1)}, u32[]{:S(2)}, u32[]{:S(2)}) collective-permute-start(bf16[256,384]{1,0:T(8,128)(2,1)S(1)} %get-tuple-element.25), channel_id=1, source_target_pairs={{0,1},{1,0},{8,9},{9,8},{2,3},{3,2},{10,11},{11,10},{4,5},{5,4},{1... | collective-permute-start | bytes 589832 | tf_op jit(solution)/shard_map/ppermute | solution.py:171
  74.9 3.1 %collective-permute-start.4 = (bf16[256,384]{1,0:T(8,128)(2,1)S(1)}, bf16[256,384]{1,0:T(8,128)(2,1)S(1)}, u32[]{:S(2)}, u32[]{:S(2)}) collective-permute-start(bf16[256,384]{1,0:T(8,128)(2,1)S(1)} %get-tuple-element.26), channel_id=1, source_target_pairs={{0,8},{1,9},{8,0},{9,1},{2,10},{3,11},{10,2},{11,3},{4,12},{5,13},... | collective-permute-start | bytes 589832 | tf_op jit(solution)/shard_map/ppermute | solution.py:171
  78.0 2.4 %collective-permute-start.5 = (bf16[256,384]{1,0:T(8,128)(2,1)S(1)}, bf16[256,384]{1,0:T(8,128)(2,1)S(1)}, u32[]{:S(2)}, u32[]{:S(2)}) collective-permute-start(bf16[256,384]{1,0:T(8,128)(2,1)S(1)} %get-tuple-element.27), channel_id=1, source_target_pairs={{0,9},{1,8},{8,1},{9,0},{2,11},{3,10},{10,3},{11,2},{4,13},{5,12},... | collective-permute-start | bytes 589832 | tf_op jit(solution)/shard_map/ppermute | solution.py:171
  80.4 5.2 %all-to-all-done.2.terms_ref = bf16[64,8,384]{2,1,0:T(8,128)(2,1)S(1)} async-done(((bf16[64,8,384]{2,1,0:T(8,128)(2,1)}), bf16[64,8,384]{2,1,0:T(8,128)(2,1)S(1)}, u32[]{:S(2)}, u32[]{:S(2)}) %all-to-all-start.2) | async-done | bytes 393248 | tf_op jit(solution)/shard_map/all_to_all | solution.py:199
  85.5 0.7 finish.1
  86.2 10.3 %all-to-all-start.3 = ((f32[8,2,1536]{2,1,0:T(2,128)}), f32[8,2,1536]{2,1,0:T(2,128)S(1)}, u32[]{:S(2)}, u32[]{:S(2)}) async-start(f32[8,2,1536]{2,1,0:T(2,128)} %get-tuple-element.30), calls=%async_computation.3 | async-start | bytes 196608 | tf_op jit(solution)/shard_map/all_to_all | solution.py:206
  96.5 1.5 %join.1 = (bf16[128,1536]{1,0:T(8,128)(2,1)}, bf16[128,1536]{1,0:T(8,128)(2,1)}) custom-call(s32[4]{0:T(128)S(1)} %pad_add_fusion.place_ref, bf16[256,384]{1,0:T(8,128)(2,1)S(1)} %get-tuple-element.24.refs_0_, bf16[256,384]{1,0:T(8,128)(2,1)S(1)} %collective-permute-done.3.refs_1_, bf16[256,384]{1,0:T(8,128)(2,1)S(1)} %collective-permute-done.4.refs_2_, ...), custom_call_target="tpu_custom_call" | custom-call | tf_op jit(solution)/shard_map/join/pallas_call | solution.py:203
  98.0 3.5 %all-to-all-done.3 = f32[8,2,1536]{2,1,0:T(2,128)S(1)} async-done(((f32[8,2,1536]{2,1,0:T(2,128)}), f32[8,2,1536]{2,1,0:T(2,128)S(1)}, u32[]{:S(2)}, u32[]{:S(2)}) %all-to-all-start.3) | async-done | bytes 98336 | tf_op jit(solution)/shard_map/all_to_all | solution.py:206
  (20 shorter events, 0.9 us)
Async XLA Ops:
  0.6 0.7 copy-start.2
  1.3 0.7 copy-start.3
  2.8 18.7 %copy-start = (bf16[1,128,1536]{2,1,0:T(8,128)(2,1)S(1)}, bf16[1,128,1536]{2,1,0:T(8,128)(2,1)}, u32[]{:S(2)}) copy-start(bf16[1,128,1536]{2,1,0:T(8,128)(2,1)} %param.9) | copy-start | bytes 1179652
  2.8 18.7 %copy-start.1 = (bf16[1,128,1536]{2,1,0:T(8,128)(2,1)S(1)}, bf16[1,128,1536]{2,1,0:T(8,128)(2,1)}, u32[]{:S(2)}) copy-start(bf16[1,128,1536]{2,1,0:T(8,128)(2,1)} %param.10) | copy-start | bytes 1179652
  2.8 32.0 %all-to-all-start = ((bf16[64,4,768]{2,1,0:T(4,128)(2,1)}), bf16[64,4,768]{2,1,0:T(4,128)(2,1)S(1)}, u32[]{:S(2)}, u32[]{:S(2)}) async-start(bf16[64,4,768]{2,1,0:T(4,128)(2,1)} %outgoing.1), calls=%async_computation | async-start | bytes 786432 | tf_op jit(solution)/shard_map/all_to_all | solution.py:184
  22.1 18.4 %collective-permute-start = (bf16[256,384]{1,0:T(8,128)(2,1)S(1)}, bf16[256,384]{1,0:T(8,128)(2,1)S(1)}, u32[]{:S(2)}, u32[]{:S(2)}) collective-permute-start(bf16[256,384]{1,0:T(8,128)(2,1)S(1)} %get-tuple-element.19), channel_id=1, source_target_pairs={{0,1},{1,0},{8,9},{9,8},{2,3},{3,2},{10,11},{11,10},{4,5},{5,4},{1... | collective-permute-start | bytes 589832 | tf_op jit(solution)/shard_map/ppermute | solution.py:171
  25.1 15.4 %collective-permute-start.1 = (bf16[256,384]{1,0:T(8,128)(2,1)S(1)}, bf16[256,384]{1,0:T(8,128)(2,1)S(1)}, u32[]{:S(2)}, u32[]{:S(2)}) collective-permute-start(bf16[256,384]{1,0:T(8,128)(2,1)S(1)} %get-tuple-element.20), channel_id=1, source_target_pairs={{0,8},{1,9},{8,0},{9,1},{2,10},{3,11},{10,2},{11,3},{4,12},{5,13},... | collective-permute-start | bytes 589832 | tf_op jit(solution)/shard_map/ppermute | solution.py:171
  28.2 12.3 %collective-permute-start.2 = (bf16[256,384]{1,0:T(8,128)(2,1)S(1)}, bf16[256,384]{1,0:T(8,128)(2,1)S(1)}, u32[]{:S(2)}, u32[]{:S(2)}) collective-permute-start(bf16[256,384]{1,0:T(8,128)(2,1)S(1)} %get-tuple-element.21), channel_id=1, source_target_pairs={{0,9},{1,8},{8,1},{9,0},{2,11},{3,10},{10,3},{11,2},{4,13},{5,12},... | collective-permute-start | bytes 589832 | tf_op jit(solution)/shard_map/ppermute | solution.py:171
  42.1 7.7 %copy-start.4 = (bf16[1536]{0:T(1024)(128)(2,1)S(1)}, bf16[1536]{0:T(1024)(128)(2,1)}, u32[]{:S(2)}) copy-start(bf16[1536]{0:T(1024)(128)(2,1)} %param.12) | copy-start | bytes 9220
  42.1 19.5 %all-to-all-start.1 = ((f32[16,3,3,256]{3,2,1,0:T(4,128)}), f32[16,3,3,256]{3,2,1,0:T(4,128)S(1)}, u32[]{:S(2)}, u32[]{:S(2)}) async-start(f32[16,3,3,256]{3,2,1,0:T(4,128)} %stats.1), calls=%async_computation.1 | async-start | bytes 393216 | tf_op jit(solution)/shard_map/all_to_all | solution.py:191
  49.8 0.7 copy-start.5
  65.0 20.5 %all-to-all-start.2 = ((bf16[64,8,384]{2,1,0:T(8,128)(2,1)}), bf16[64,8,384]{2,1,0:T(8,128)(2,1)S(1)}, u32[]{:S(2)}, u32[]{:S(2)}) async-start(bf16[64,8,384]{2,1,0:T(8,128)(2,1)} %get-tuple-element.22), calls=%async_computation.2 | async-start | bytes 786432 | tf_op jit(solution)/shard_map/all_to_all | solution.py:199
  72.0 24.6 %collective-permute-start.3 = (bf16[256,384]{1,0:T(8,128)(2,1)S(1)}, bf16[256,384]{1,0:T(8,128)(2,1)S(1)}, u32[]{:S(2)}, u32[]{:S(2)}) collective-permute-start(bf16[256,384]{1,0:T(8,128)(2,1)S(1)} %get-tuple-element.25), channel_id=1, source_target_pairs={{0,1},{1,0},{8,9},{9,8},{2,3},{3,2},{10,11},{11,10},{4,5},{5,4},{1... | collective-permute-start | bytes 589832 | tf_op jit(solution)/shard_map/ppermute | solution.py:171
  74.9 21.6 %collective-permute-start.4 = (bf16[256,384]{1,0:T(8,128)(2,1)S(1)}, bf16[256,384]{1,0:T(8,128)(2,1)S(1)}, u32[]{:S(2)}, u32[]{:S(2)}) collective-permute-start(bf16[256,384]{1,0:T(8,128)(2,1)S(1)} %get-tuple-element.26), channel_id=1, source_target_pairs={{0,8},{1,9},{8,0},{9,1},{2,10},{3,11},{10,2},{11,3},{4,12},{5,13},... | collective-permute-start | bytes 589832 | tf_op jit(solution)/shard_map/ppermute | solution.py:171
  78.0 18.5 %collective-permute-start.5 = (bf16[256,384]{1,0:T(8,128)(2,1)S(1)}, bf16[256,384]{1,0:T(8,128)(2,1)S(1)}, u32[]{:S(2)}, u32[]{:S(2)}) collective-permute-start(bf16[256,384]{1,0:T(8,128)(2,1)S(1)} %get-tuple-element.27), channel_id=1, source_target_pairs={{0,9},{1,8},{8,1},{9,0},{2,11},{3,10},{10,3},{11,2},{4,13},{5,12},... | collective-permute-start | bytes 589832 | tf_op jit(solution)/shard_map/ppermute | solution.py:171
  86.2 15.3 %all-to-all-start.3 = ((f32[8,2,1536]{2,1,0:T(2,128)}), f32[8,2,1536]{2,1,0:T(2,128)S(1)}, u32[]{:S(2)}, u32[]{:S(2)}) async-start(f32[8,2,1536]{2,1,0:T(2,128)} %get-tuple-element.30), calls=%async_computation.3 | async-start | bytes 196608 | tf_op jit(solution)/shard_map/all_to_all | solution.py:206

commit v4 on v3

v4 whole, which is shorter than its diff:
```python
import jax
import jax.numpy as jnp
from jax import lax
from jax.experimental import pallas as pl
from jax.experimental.pallas import tpu as pltpu
from jax.sharding import Mesh, PartitionSpec as P

HEADS = 12
HD = 128
QTOK = 256
BLK = 128
OWN = 4
QUAD = 4
MINE = HEADS // QUAD
WIDTH = MINE * HD
SLOTS = QUAD * BLK
PAD = 16
DEAD = 1024.0
SCALE = HD ** (-0.5)
HOPS = (0, 3, 1, 2)
NT = (((1,), (1,)), ((), ()))
TN = (((0,), (0,)), ((), ()))
BANK = ("yq", "yb", "zq", "zb")
NEAR = ("yb", "zb")
FAR = ("yq", "zq")


def dot(a, b, dims):
    return lax.dot_general(a, b, dims, preferred_element_type=jnp.float32)


def columns_of(group):
    return pl.ds(pl.multiple_of(group * WIDTH, WIDTH), WIDTH)


def my_group():
    return lax.axis_index("yb") * 2 + lax.axis_index("zb")


def outgoing_kernel(q_hbm, do_hbm, out_ref, q_ref, do_ref, sems):
    copies = [
        pltpu.make_async_copy(q_hbm, q_ref, sems.at[0]),
        pltpu.make_async_copy(do_hbm, do_ref, sems.at[1]),
    ]
    for copy in copies:
        copy.start()
    for copy in copies:
        copy.wait()
    for device in range(out_ref.shape[0]):
        group = ((device >> 3) & 1) * 2 + (device & 1)
        cols = slice(group * WIDTH, (group + 1) * WIDTH)
        out_ref[device, :, :WIDTH] = q_ref[0, :, cols]
        out_ref[device, :, WIDTH:] = do_ref[0, :, cols]


def share_kernel(count_ref, slot_ref, k_ref, v_ref, *out_refs):
    live = count_ref[0] > slot_ref[0, 0] * BLK
    for hop, out_ref in zip(HOPS, out_refs):
        cols = columns_of(my_group() ^ hop)
        out_ref[:BLK] = jnp.where(live, k_ref[:, cols], jnp.bfloat16(DEAD))
        out_ref[BLK:] = v_ref[:, cols]


def join_kernel(*refs):
    for hop, block in zip(HOPS, refs):
        cols = columns_of(my_group() ^ hop)
        refs[QUAD][:, cols] = block[:BLK]
        refs[QUAD + 1][:, cols] = block[BLK:]


def bank_kernel(b0, b1, b2, b3, nk_ref, nv_ref, keys_ref, vals_ref):
    for at, block in enumerate((b0, b1, b2, b3)):
        keys_ref[at * BLK : (at + 1) * BLK] = block[:BLK]
        vals_ref[at * BLK : (at + 1) * BLK] = block[BLK:]
    for ref, out in ((nk_ref, keys_ref), (nv_ref, vals_ref)):
        out[SLOTS:] = jnp.broadcast_to(ref[:, columns_of(my_group())], (PAD, WIDTH))


def bank_scores(keys_ref, q, cols):
    scores = dot(keys_ref[:, cols], q, NT) * SCALE
    pieces = []
    for at in range(QUAD):
        mark = keys_ref[at * BLK : at * BLK + PAD, :QTOK].astype(jnp.float32)[:1]
        bias = jnp.where(mark < 0.5 * DEAD, 0.0, -1e30)
        pieces.append(scores[at * BLK : (at + 1) * BLK] + bias)
    return jnp.concatenate(pieces, axis=0), scores[SLOTS:]


def stats_kernel(qd_ref, keys_ref, vals_ref, out_ref):
    for h in range(MINE):
        cols = slice(h * HD, (h + 1) * HD)
        q, do = qd_ref[:, cols], qd_ref[:, WIDTH + h * HD : WIDTH + (h + 1) * HD]
        scores, _ = bank_scores(keys_ref, q, cols)
        dprobs = dot(vals_ref[:SLOTS, cols], do, NT)
        top = jnp.max(scores, axis=0, keepdims=True)
        terms = jnp.exp(scores - top)
        rows = (top, jnp.sum(terms, axis=0, keepdims=True), jnp.sum(terms * dprobs, axis=0, keepdims=True))
        for at, row in enumerate(rows):
            out_ref[:, at, h : h + 1, :] = jnp.broadcast_to(row[None], (out_ref.shape[0], 1, QTOK))


def grad_kernel(parts_ref, qd_ref, keys_ref, vals_ref, dq_ref, *outs):
    owner = lax.broadcasted_iota(jnp.int32, (PAD, QTOK), 1) // OWN
    pad_row = lax.broadcasted_iota(jnp.int32, (PAD, QTOK), 0)
    far_y, far_z = lax.axis_index("yq"), lax.axis_index("zq")
    ours = ((owner >> 4) == far_y) & (((owner >> 1) & 3) == far_z)
    carried = lax.rem(far_y * 4 + far_z, MINE)
    tops = parts_ref[:, 0]
    bank_top = jnp.max(tops, axis=0)
    weight = jnp.exp(tops - bank_top[None])
    bank_sum = jnp.sum(parts_ref[:, 1] * weight, axis=0)
    bank_dot = jnp.sum(parts_ref[:, 2] * weight, axis=0)

    def hi_lo(row):
        hi = row.astype(jnp.bfloat16).astype(jnp.float32)
        return jnp.where(pad_row == 0, hi, jnp.where(pad_row == 1, row - hi, 0.0))

    for h in range(MINE):
        cols = slice(h * HD, (h + 1) * HD)
        q, do = qd_ref[:, cols], qd_ref[:, WIDTH + h * HD : WIDTH + (h + 1) * HD]
        scores, null_scores = bank_scores(keys_ref, q, cols)
        dprobs = dot(vals_ref[:, cols], do, NT)
        null_score = null_scores[:1]
        null_dp = dprobs[SLOTS : SLOTS + 1]
        top = jnp.maximum(bank_top[h : h + 1], null_score)
        rest = jnp.exp(bank_top[h : h + 1] - top)
        null_term = jnp.exp(null_score - top)
        total = bank_sum[h : h + 1] * rest + null_term
        delta = (bank_dot[h : h + 1] * rest + null_term * null_dp) / total
        lse = top + jnp.log(total)
        probs = jnp.exp(scores - lse)
        null_prob = jnp.exp(null_score - lse)
        dscore = (probs * (dprobs[:SLOTS] - delta)).astype(jnp.bfloat16)
        null_ds = hi_lo(null_prob * (null_dp - delta))
        null_pb = hi_lo(null_prob)
        wide_ds = jnp.concatenate([dscore, null_ds.astype(jnp.bfloat16)], axis=0)
        wide_pb = jnp.concatenate([probs.astype(jnp.bfloat16), null_pb.astype(jnp.bfloat16)], axis=0)
        own_ds = jnp.concatenate([dscore, jnp.where(ours, null_ds, 0.0).astype(jnp.bfloat16)], axis=0)
        grad_k = jnp.dot(wide_ds, q, preferred_element_type=jnp.float32) * SCALE
        grad_v = jnp.dot(wide_pb, do, preferred_element_type=jnp.float32)
        for at, out in enumerate(outs):
            out[:BLK, cols] = grad_k[at * BLK : (at + 1) * BLK].astype(jnp.bfloat16)
            out[BLK:, cols] = grad_v[at * BLK : (at + 1) * BLK].astype(jnp.bfloat16)
        rows = []
        for grad in (grad_k, grad_v):
            row = jnp.sum(grad[SLOTS:], axis=0, keepdims=True)
            hi = row.astype(jnp.bfloat16).astype(jnp.float32)
            rows += [hi, row - hi]
        rows = jnp.concatenate(rows, axis=0)
        null_rows_out = rows if h == 0 else jnp.where(carried == h, rows, null_rows_out)
        grad_q = (dot(own_ds, keys_ref[:, cols], TN) * SCALE).reshape(QTOK // OWN, OWN, HD)
        dq_ref[:, :, cols] = grad_q.astype(jnp.bfloat16)
    dq_ref[:, :, WIDTH:] = jnp.broadcast_to(null_rows_out[None], (QTOK // OWN, OWN, HD)).astype(jnp.bfloat16)


def finish_kernel(terms_ref, q_ref, null_ref):
    def term(group, far):
        at = (group >> 1) * 8 + (group & 1) + (far >> 2) * 16 + (far & 3) * 2
        return terms_ref[at].astype(jnp.float32)

    for group in range(QUAD):
        total = term(group, 0)
        for far in range(1, 16):
            total += term(group, far)
        q_ref[:, group * WIDTH : (group + 1) * WIDTH] = total[:, :WIDTH].astype(jnp.bfloat16)
        for h in range(MINE):
            parts = term(group, h)[:, WIDTH:]
            rows = jnp.concatenate([parts[0:1] + parts[1:2], parts[2:3] + parts[3:4]], axis=0)
            at = group * WIDTH + h * HD
            null_ref[:, :, at : at + HD] = jnp.broadcast_to(rows[None], (null_ref.shape[0], 2, HD))


VMEM = pl.BlockSpec(memory_space=pltpu.VMEM)
SMEM = pl.BlockSpec(memory_space=pltpu.SMEM)


def kernel(body, name, ins, *outs, scratch=(), megabytes=32):
    return pl.pallas_call(
        body,
        out_shape=tuple(jax.ShapeDtypeStruct(shape, dtype) for shape, dtype in outs),
        in_specs=ins,
        out_specs=(VMEM,) * len(outs),
        scratch_shapes=scratch,
        compiler_params=pltpu.CompilerParams(vmem_limit_bytes=megabytes * 1024 * 1024),
        name=name,
    )


def partners(hop):
    pairs = []
    for clip in range(8):
        shift = clip & 1
        for y in range(8):
            for z in range(8):
                far_y = (((y + shift) ^ (hop >> 1)) - shift) % 8
                far_z = (((z + shift) ^ (hop & 1)) - shift) % 8
                pairs.append((clip * 64 + y * 8 + z, clip * 64 + far_y * 8 + far_z))
    return pairs


def swap(blocks):
    return [blocks[0]] + [
        lax.ppermute(block, ("clip",) + BANK, partners(hop)) for hop, block in zip(HOPS[1:], blocks[1:])
    ]


def on_device(queries, keys, values, grad_out, null_key, null_value, bank_counts, block_slot):
    bf16, f32 = jnp.bfloat16, jnp.float32
    (outgoing,) = kernel(
        outgoing_kernel,
        "outgoing",
        [pl.BlockSpec(memory_space=pltpu.HBM)] * 2,
        ((64, OWN, 2 * WIDTH), bf16),
        scratch=[pltpu.VMEM(queries.shape, bf16)] * 2 + [pltpu.SemaphoreType.DMA((2,))],
        megabytes=60,
    )(queries, grad_out)
    whole = lax.all_to_all(outgoing, BANK, 0, 0).reshape(QTOK, 2 * WIDTH)
    blocks = swap(
        kernel(share_kernel, "share", [SMEM, SMEM, VMEM, VMEM], *[((2 * BLK, WIDTH), bf16)] * QUAD)(
            bank_counts, block_slot, keys[0], values[0]
        )
    )
    keys, vals = kernel(
        bank_kernel,
        "bank",
        [VMEM] * 6,
        *[((SLOTS + PAD, WIDTH), bf16)] * 2,
    )(*blocks, null_key[None], null_value[None])
    (parts,) = kernel(stats_kernel, "stats", [VMEM] * 3, ((16, 3, MINE, QTOK), f32))(whole, keys, vals)
    parts = lax.all_to_all(parts, FAR, 0, 0)
    grad_q, *grad_kv = kernel(
        grad_kernel,
        "grads",
        [VMEM] * 4,
        ((64, OWN, WIDTH + HD), bf16),
        *[((2 * BLK, WIDTH), bf16)] * QUAD,
    )(parts, whole, keys, vals)
    terms = lax.all_to_all(grad_q, BANK, 0, 0)
    own_q, nulls = kernel(
        finish_kernel, "finish", [VMEM], ((OWN, HEADS * HD), bf16), ((8, 2, HEADS * HD), f32)
    )(terms)
    grad_k, grad_v = kernel(
        join_kernel, "join", [VMEM] * QUAD, *[((BLK, HEADS * HD), bf16)] * 2
    )(*swap(grad_kv))
    nulls = jnp.sum(lax.all_to_all(nulls, "clip", 0, 0), axis=0)
    return (own_q[None], grad_k[None], grad_v[None], nulls[0], nulls[1])


def solution(mesh):
    grid = Mesh(mesh.devices.reshape(8, 4, 2, 4, 2), ("clip",) + BANK)
    rows = P("clip", BANK, None)
    return jax.shard_map(
        on_device,
        mesh=grid,
        in_specs=(rows, rows, rows, rows, P(), P(), P("clip"), P("clip", BANK)),
        out_specs=(rows, rows, rows, P(), P()),
        check_vma=False,
    )
```

time: 103 us -> 95.1 us (0.923)
  blocking collectives: 0 us -> 19.6 us
  waiting for transfers between devices: 29.6 us -> 12.8 us
  starting transfers between devices: 59 us -> 52 us
  local copies, waits for them, and re-layouts: 2.82 us -> 0.76 us
  Pallas kernels: 8.58 us -> 7 us
    all_to_all x0 -> x1, blocking collectives: none -> 19.6 us  [on_device(): parts = lax.all_to_all(parts, FAR, 0, 0)]
    all_to_all x1 -> x0, waiting for transfers between devices: 11.1 us -> none  [on_device(): parts = lax.all_to_all(parts, FAR, 0, 0)]
    all_to_all x1 -> x0, starting transfers between devices: 7.67 us -> none  [on_device(): parts = lax.all_to_all(parts, FAR, 0, 0)]
    ppermute x6, starting transfers between devices: 16.8 us -> 21.6 us  [swap(): lax.ppermute(block, ('clip',) + BANK, partners(hop))]
    all_to_all x1, waiting for transfers between devices: 4.28 us -> 0.01 us  [on_device(): whole = lax.all_to_all(outgoing, BANK, 0, 0).reshape(QTOK, 2 * WIDTH)]
    all_to_all x1, starting transfers between devices: 10.3 us -> 7.44 us  [on_device(): nulls = jnp.sum(lax.all_to_all(nulls, 'clip', 0, 0), axis=0)]
    all_to_all x1, waiting for transfers between devices: 5.15 us -> 2.47 us  [on_device(): terms = lax.all_to_all(grad_q, BANK, 0, 0)]
    unnamed x12 -> x8, local copies, waits for them, and re-layouts: 2.09 us -> 0.03 us
  transfers between devices with their start and end apart: 10 -> 9, of which waited for: 5 -> 4; matrix products, arithmetic and copies ran while one was open for 0% -> 0% of each run, Pallas kernels for 3% -> 2%
where the time goes in v4:
time: 95.1 us; the launch traced here: 94.4 us
  starting transfers between devices  52 us (55%)
  blocking collectives  19.6 us (21%)
  waiting for transfers between devices  12.8 us (13%)
  Pallas kernels  7 us (7%)
  between operations  2.12 us (2%)
    ppermute x6, starting transfers between devices, swap(): lax.ppermute(block, ('clip',) + BANK, partners(hop))  21.6 us
    all_to_all x1, blocking collectives, on_device(): parts = lax.all_to_all(parts, FAR, 0, 0)  19.6 us
    all_to_all x1, starting transfers between devices, on_device(): whole = lax.all_to_all(outgoing, BANK, 0, 0).reshape(QTOK, 2 * WIDTH)  17.3 us
    all_to_all x1, starting transfers between devices, on_device(): nulls = jnp.sum(lax.all_to_all(nulls, 'clip', 0, 0), axis=0)  7.44 us
    ppermute x6, waiting for transfers between devices, swap(): lax.ppermute(block, ('clip',) + BANK, partners(hop))  6.33 us
    all_to_all x1, starting transfers between devices, on_device(): terms = lax.all_to_all(grad_q, BANK, 0, 0)  5.67 us
    all_to_all x1, waiting for transfers between devices, on_device(): nulls = jnp.sum(lax.all_to_all(nulls, 'clip', 0, 0), axis=0)  4.01 us
    pallas_call x1, Pallas kernels, on_device(): kernel(grad_kernel, 'grads', [VMEM] * 4, ((64, OWN, WIDTH + HD), bf16), *...  2.77 us
  transfers between devices with their start and end apart: 9, of which 4 were waited for; matrix products, arithmetic and copies ran while one was open for 0% of the time, Pallas kernels for 2%

profile of v4, /device:TPU:1, one launch (start us, length us, event | category | flops | bytes accessed | tf_op | source)
XLA Modules:
  0.0 94.4 jit_solution(4659908339938694816)
XLA Ops:
  0.6 1.5 %outgoing.1 = bf16[64,4,768]{2,1,0:T(4,128)(2,1)} custom-call(bf16[1,4,1536]{2,1,0:T(4,128)(2,1)} %q_hbm.1, bf16[1,4,1536]{2,1,0:T(4,128)(2,1)} %do_hbm.1), custom_call_target="tpu_custom_call" | custom-call | tf_op jit(solution)/shard_map/outgoing/pallas_call | solution.py:209
  2.2 0.0 copy-start
  2.2 17.3 %all-to-all-start = ((bf16[64,4,768]{2,1,0:T(4,128)(2,1)}), bf16[64,4,768]{2,1,0:T(4,128)(2,1)S(1)}, u32[]{:S(2)}, u32[]{:S(2)}) async-start(bf16[64,4,768]{2,1,0:T(4,128)(2,1)} %outgoing.1), calls=%async_computation | async-start | bytes 786432 | tf_op jit(solution)/shard_map/all_to_all | solution.py:217
  20.8 0.1 share.1
  20.9 6.6 %collective-permute-start = (bf16[256,384]{1,0:T(8,128)(2,1)S(1)}, bf16[256,384]{1,0:T(8,128)(2,1)S(1)}, u32[]{:S(2)}, u32[]{:S(2)}) collective-permute-start(bf16[256,384]{1,0:T(8,128)(2,1)S(1)} %get-tuple-element.21), channel_id=1, source_target_pairs={{0,9},{1,8},{2,11},{3,10},{4,13},{5,12},{6,15},{7,14},{8,1},{9,0},... | collective-permute-start | bytes 589832 | tf_op jit(solution)/shard_map/ppermute | solution.py:203
  27.5 2.1 %collective-permute-start.1 = (bf16[256,384]{1,0:T(8,128)(2,1)S(1)}, bf16[256,384]{1,0:T(8,128)(2,1)S(1)}, u32[]{:S(2)}, u32[]{:S(2)}) collective-permute-start(bf16[256,384]{1,0:T(8,128)(2,1)S(1)} %get-tuple-element.22), channel_id=1, source_target_pairs={{0,1},{1,0},{2,3},{3,2},{4,5},{5,4},{6,7},{7,6},{8,9},{9,8},{10,11... | collective-permute-start | bytes 589832 | tf_op jit(solution)/shard_map/ppermute | solution.py:203
  29.6 2.1 %collective-permute-start.2 = (bf16[256,384]{1,0:T(8,128)(2,1)S(1)}, bf16[256,384]{1,0:T(8,128)(2,1)S(1)}, u32[]{:S(2)}, u32[]{:S(2)}) collective-permute-start(bf16[256,384]{1,0:T(8,128)(2,1)S(1)} %get-tuple-element.23), channel_id=1, source_target_pairs={{0,8},{1,9},{2,10},{3,11},{4,12},{5,13},{6,14},{7,15},{8,0},{9,1},... | collective-permute-start | bytes 589832 | tf_op jit(solution)/shard_map/ppermute | solution.py:203
  31.8 3.8 %collective-permute-done.b1 = bf16[256,384]{1,0:T(8,128)(2,1)S(1)} collective-permute-done((bf16[256,384]{1,0:T(8,128)(2,1)S(1)}, bf16[256,384]{1,0:T(8,128)(2,1)S(1)}, u32[]{:S(2)}, u32[]{:S(2)}) %collective-permute-start) | collective-permute-done | bytes 196640 | tf_op jit(solution)/shard_map/ppermute | solution.py:203
  35.6 2.5 %collective-permute-done.1.b2 = bf16[256,384]{1,0:T(8,128)(2,1)S(1)} collective-permute-done((bf16[256,384]{1,0:T(8,128)(2,1)S(1)}, bf16[256,384]{1,0:T(8,128)(2,1)S(1)}, u32[]{:S(2)}, u32[]{:S(2)}) %collective-permute-start.1) | collective-permute-done | bytes 196640 | tf_op jit(solution)/shard_map/ppermute | solution.py:203
  38.1 0.1 bank.1
  38.2 0.1 reshape.13.qd_ref
  38.3 0.9 stats.1
  39.2 19.6 %all_to_all.20.parts_ref = f32[16,3,3,256]{3,2,1,0:T(4,128)S(1)} all-to-all(f32[16,3,3,256]{3,2,1,0:T(4,128)S(1)} %stats.1), channel_id=1, replica_groups=mesh['clip'=8,'yq'=4,'yb'=2,'zq'=4,'zb'=2] {'yq','zq'}, dimensions={0} | all-to-all | bytes 294912 | tf_op jit(solution)/shard_map/all_to_all | solution.py:230
  58.8 2.8 %grads.1 = (bf16[64,4,512]{2,1,0:T(4,128)(2,1)}, bf16[256,384]{1,0:T(8,128)(2,1)S(1)}, bf16[256,384]{1,0:T(8,128)(2,1)S(1)}, bf16[256,384]{1,0:T(8,128)(2,1)S(1)}, bf16[256,384]{1,0:T(8,128)(2,1)S(1)}) custom-call(f32[16,3,3,256]{3,2,1,0:T(4,128)S(1)} %all_to_all.20.parts_ref, bf16[256,768]{1,0:T(8,128)(2,1)S(1)} %reshape.13.qd_ref, ...), custom_call_target="tpu_custom_call" | custom-call | tf_op jit(solution)/shard_map/grads/pallas_call | solution.py:231
  61.6 5.7 %all-to-all-start.2 = ((bf16[64,4,512]{2,1,0:T(4,128)(2,1)}), bf16[64,4,512]{2,1,0:T(4,128)(2,1)S(1)}, u32[]{:S(2)}, u32[]{:S(2)}) async-start(bf16[64,4,512]{2,1,0:T(4,128)(2,1)} %get-tuple-element.26), calls=%async_computation.2 | async-start | bytes 524288 | tf_op jit(solution)/shard_map/all_to_all | solution.py:238
  67.3 6.6 %collective-permute-start.3 = (bf16[256,384]{1,0:T(8,128)(2,1)S(1)}, bf16[256,384]{1,0:T(8,128)(2,1)S(1)}, u32[]{:S(2)}, u32[]{:S(2)}) collective-permute-start(bf16[256,384]{1,0:T(8,128)(2,1)S(1)} %get-tuple-element.29), channel_id=1, source_target_pairs={{0,9},{1,8},{2,11},{3,10},{4,13},{5,12},{6,15},{7,14},{8,1},{9,0},... | collective-permute-start | bytes 589832 | tf_op jit(solution)/shard_map/ppermute | solution.py:203
  73.9 2.1 %collective-permute-start.4 = (bf16[256,384]{1,0:T(8,128)(2,1)S(1)}, bf16[256,384]{1,0:T(8,128)(2,1)S(1)}, u32[]{:S(2)}, u32[]{:S(2)}) collective-permute-start(bf16[256,384]{1,0:T(8,128)(2,1)S(1)} %get-tuple-element.30), channel_id=1, source_target_pairs={{0,1},{1,0},{2,3},{3,2},{4,5},{5,4},{6,7},{7,6},{8,9},{9,8},{10,11... | collective-permute-start | bytes 589832 | tf_op jit(solution)/shard_map/ppermute | solution.py:203
  76.0 2.1 %collective-permute-start.5 = (bf16[256,384]{1,0:T(8,128)(2,1)S(1)}, bf16[256,384]{1,0:T(8,128)(2,1)S(1)}, u32[]{:S(2)}, u32[]{:S(2)}) collective-permute-start(bf16[256,384]{1,0:T(8,128)(2,1)S(1)} %get-tuple-element.31), channel_id=1, source_target_pairs={{0,8},{1,9},{2,10},{3,11},{4,12},{5,13},{6,14},{7,15},{8,0},{9,1},... | collective-permute-start | bytes 589832 | tf_op jit(solution)/shard_map/ppermute | solution.py:203
  78.1 2.5 %all-to-all-done.2.terms_ref = bf16[64,4,512]{2,1,0:T(4,128)(2,1)S(1)} async-done(((bf16[64,4,512]{2,1,0:T(4,128)(2,1)}), bf16[64,4,512]{2,1,0:T(4,128)(2,1)S(1)}, u32[]{:S(2)}, u32[]{:S(2)}) %all-to-all-start.2) | async-done | bytes 262176 | tf_op jit(solution)/shard_map/all_to_all | solution.py:238
  80.6 0.7 finish.1
  81.3 7.4 %all-to-all-start.3 = ((f32[8,2,1536]{2,1,0:T(2,128)}), f32[8,2,1536]{2,1,0:T(2,128)S(1)}, u32[]{:S(2)}, u32[]{:S(2)}) async-start(f32[8,2,1536]{2,1,0:T(2,128)} %get-tuple-element.34), calls=%async_computation.3 | async-start | bytes 196608 | tf_op jit(solution)/shard_map/all_to_all | solution.py:245
  88.7 1.0 %join.1 = (bf16[128,1536]{1,0:T(8,128)(2,1)}, bf16[128,1536]{1,0:T(8,128)(2,1)}) custom-call(bf16[256,384]{1,0:T(8,128)(2,1)S(1)} %get-tuple-element.28.refs_0_, bf16[256,384]{1,0:T(8,128)(2,1)S(1)} %collective-permute-done.3.refs_1_, bf16[256,384]{1,0:T(8,128)(2,1)S(1)} %collective-permute-done.4.refs_2_, bf16[256,384]{1,0:T(8,128)(2,1)S(1)} %collective-permute-done.5.refs_3_), custom_call_target="tpu_custom_call" | custom-call | tf_op jit(solution)/shard_map/join/pallas_call | solution.py:242
  89.7 4.0 %all-to-all-done.3 = f32[8,2,1536]{2,1,0:T(2,128)S(1)} async-done(((f32[8,2,1536]{2,1,0:T(2,128)}), f32[8,2,1536]{2,1,0:T(2,128)S(1)}, u32[]{:S(2)}, u32[]{:S(2)}) %all-to-all-start.3) | async-done | bytes 98336 | tf_op jit(solution)/shard_map/all_to_all | solution.py:245
  93.7 0.6 slice_reduce_fusion
  (15 shorter events, 0.1 us)
Async XLA Ops:
  2.2 18.6 %copy-start = (bf16[1,128,1536]{2,1,0:T(8,128)(2,1)S(1)}, bf16[1,128,1536]{2,1,0:T(8,128)(2,1)}, u32[]{:S(2)}) copy-start(bf16[1,128,1536]{2,1,0:T(8,128)(2,1)} %param.9) | copy-start | bytes 1179652
  2.2 18.6 %copy-start.1 = (bf16[1,128,1536]{2,1,0:T(8,128)(2,1)S(1)}, bf16[1,128,1536]{2,1,0:T(8,128)(2,1)}, u32[]{:S(2)}) copy-start(bf16[1,128,1536]{2,1,0:T(8,128)(2,1)} %param.10) | copy-start | bytes 1179652
  2.2 36.0 %all-to-all-start = ((bf16[64,4,768]{2,1,0:T(4,128)(2,1)}), bf16[64,4,768]{2,1,0:T(4,128)(2,1)S(1)}, u32[]{:S(2)}, u32[]{:S(2)}) async-start(bf16[64,4,768]{2,1,0:T(4,128)(2,1)} %outgoing.1), calls=%async_computation | async-start | bytes 786432 | tf_op jit(solution)/shard_map/all_to_all | solution.py:217
  20.9 10.8 %copy-start.2 = (bf16[1536]{0:T(1024)(128)(2,1)S(1)}, bf16[1536]{0:T(1024)(128)(2,1)}, u32[]{:S(2)}) copy-start(bf16[1536]{0:T(1024)(128)(2,1)} %param.12) | copy-start | bytes 9220
  20.9 14.7 %collective-permute-start = (bf16[256,384]{1,0:T(8,128)(2,1)S(1)}, bf16[256,384]{1,0:T(8,128)(2,1)S(1)}, u32[]{:S(2)}, u32[]{:S(2)}) collective-permute-start(bf16[256,384]{1,0:T(8,128)(2,1)S(1)} %get-tuple-element.21), channel_id=1, source_target_pairs={{0,9},{1,8},{2,11},{3,10},{4,13},{5,12},{6,15},{7,14},{8,1},{9,0},... | collective-permute-start | bytes 589832 | tf_op jit(solution)/shard_map/ppermute | solution.py:203
  27.5 10.6 %collective-permute-start.1 = (bf16[256,384]{1,0:T(8,128)(2,1)S(1)}, bf16[256,384]{1,0:T(8,128)(2,1)S(1)}, u32[]{:S(2)}, u32[]{:S(2)}) collective-permute-start(bf16[256,384]{1,0:T(8,128)(2,1)S(1)} %get-tuple-element.22), channel_id=1, source_target_pairs={{0,1},{1,0},{2,3},{3,2},{4,5},{5,4},{6,7},{7,6},{8,9},{9,8},{10,11... | collective-permute-start | bytes 589832 | tf_op jit(solution)/shard_map/ppermute | solution.py:203
  29.6 2.1 %copy-start.3 = (bf16[1536]{0:T(1024)(128)(2,1)S(1)}, bf16[1536]{0:T(1024)(128)(2,1)}, u32[]{:S(2)}) copy-start(bf16[1536]{0:T(1024)(128)(2,1)} %param.13) | copy-start | bytes 9220
  29.6 8.5 %collective-permute-start.2 = (bf16[256,384]{1,0:T(8,128)(2,1)S(1)}, bf16[256,384]{1,0:T(8,128)(2,1)S(1)}, u32[]{:S(2)}, u32[]{:S(2)}) collective-permute-start(bf16[256,384]{1,0:T(8,128)(2,1)S(1)} %get-tuple-element.23), channel_id=1, source_target_pairs={{0,8},{1,9},{2,10},{3,11},{4,12},{5,13},{6,14},{7,15},{8,0},{9,1},... | collective-permute-start | bytes 589832 | tf_op jit(solution)/shard_map/ppermute | solution.py:203
  61.6 19.0 %all-to-all-start.2 = ((bf16[64,4,512]{2,1,0:T(4,128)(2,1)}), bf16[64,4,512]{2,1,0:T(4,128)(2,1)S(1)}, u32[]{:S(2)}, u32[]{:S(2)}) async-start(bf16[64,4,512]{2,1,0:T(4,128)(2,1)} %get-tuple-element.26), calls=%async_computation.2 | async-start | bytes 524288 | tf_op jit(solution)/shard_map/all_to_all | solution.py:238
  67.3 21.4 %collective-permute-start.3 = (bf16[256,384]{1,0:T(8,128)(2,1)S(1)}, bf16[256,384]{1,0:T(8,128)(2,1)S(1)}, u32[]{:S(2)}, u32[]{:S(2)}) collective-permute-start(bf16[256,384]{1,0:T(8,128)(2,1)S(1)} %get-tuple-element.29), channel_id=1, source_target_pairs={{0,9},{1,8},{2,11},{3,10},{4,13},{5,12},{6,15},{7,14},{8,1},{9,0},... | collective-permute-start | bytes 589832 | tf_op jit(solution)/shard_map/ppermute | solution.py:203
  73.9 14.9 %collective-permute-start.4 = (bf16[256,384]{1,0:T(8,128)(2,1)S(1)}, bf16[256,384]{1,0:T(8,128)(2,1)S(1)}, u32[]{:S(2)}, u32[]{:S(2)}) collective-permute-start(bf16[256,384]{1,0:T(8,128)(2,1)S(1)} %get-tuple-element.30), channel_id=1, source_target_pairs={{0,1},{1,0},{2,3},{3,2},{4,5},{5,4},{6,7},{7,6},{8,9},{9,8},{10,11... | collective-permute-start | bytes 589832 | tf_op jit(solution)/shard_map/ppermute | solution.py:203
  76.0 12.7 %collective-permute-start.5 = (bf16[256,384]{1,0:T(8,128)(2,1)S(1)}, bf16[256,384]{1,0:T(8,128)(2,1)S(1)}, u32[]{:S(2)}, u32[]{:S(2)}) collective-permute-start(bf16[256,384]{1,0:T(8,128)(2,1)S(1)} %get-tuple-element.31), channel_id=1, source_target_pairs={{0,8},{1,9},{2,10},{3,11},{4,12},{5,13},{6,14},{7,15},{8,0},{9,1},... | collective-permute-start | bytes 589832 | tf_op jit(solution)/shard_map/ppermute | solution.py:203
  81.3 12.4 %all-to-all-start.3 = ((f32[8,2,1536]{2,1,0:T(2,128)}), f32[8,2,1536]{2,1,0:T(2,128)S(1)}, u32[]{:S(2)}, u32[]{:S(2)}) async-start(f32[8,2,1536]{2,1,0:T(2,128)} %get-tuple-element.34), calls=%async_computation.3 | async-start | bytes 196608 | tf_op jit(solution)/shard_map/all_to_all | solution.py:245

commit v5 on v4

--- a/solution.py
+++ b/solution.py
@@ -22,7 +22,10 @@
 TN = (((0,), (0,)), ((), ()))
 BANK = ("yq", "yb", "zq", "zb")
 NEAR = ("yb", "zb")
-FAR = ("yq", "zq")
+ALL = ("clip",) + BANK
+GATHER_CORNER = (4, 0)
+STATS_CORNER = (4, 4)
+SUMS_CORNER = (0, 4)
 
 
 def dot(a, b, dims):
@@ -103,8 +106,11 @@
     owner = lax.broadcasted_iota(jnp.int32, (PAD, QTOK), 1) // OWN
     pad_row = lax.broadcasted_iota(jnp.int32, (PAD, QTOK), 0)
     far_y, far_z = lax.axis_index("yq"), lax.axis_index("zq")
-    ours = ((owner >> 4) == far_y) & (((owner >> 1) & 3) == far_z)
-    carried = lax.rem(far_y * 4 + far_z, MINE)
+    owner_y = ((owner >> 4) + GATHER_CORNER[0] // 2) & 3
+    owner_z = ((owner >> 1) + GATHER_CORNER[1] // 2) & 3
+    ours = (owner_y == far_y) & (owner_z == far_z)
+    far_at = ((far_y - SUMS_CORNER[0] // 2) & 3) * 4 + ((far_z - SUMS_CORNER[1] // 2) & 3)
+    carried = lax.rem(far_at, MINE)
     tops = parts_ref[:, 0]
     bank_top = jnp.max(tops, axis=0)
     weight = jnp.exp(tops - bank_top[None])
@@ -149,25 +155,51 @@
         rows = jnp.concatenate(rows, axis=0)
         null_rows_out = rows if h == 0 else jnp.where(carried == h, rows, null_rows_out)
         grad_q = (dot(own_ds, keys_ref[:, cols], TN) * SCALE).reshape(QTOK // OWN, OWN, HD)
-        dq_ref[:, :, cols] = grad_q.astype(jnp.bfloat16)
+        grad_q = grad_q.astype(jnp.bfloat16)
+        for y in range(8):
+            for z in range(0, 8, 4):
+                at = (y + SUMS_CORNER[0] - GATHER_CORNER[0]) % 8 * 8 + (z + SUMS_CORNER[1] - GATHER_CORNER[1]) % 8
+                dq_ref[y * 8 + z : y * 8 + z + 4, :, cols] = grad_q[at : at + 4]
     dq_ref[:, :, WIDTH:] = jnp.broadcast_to(null_rows_out[None], (QTOK // OWN, OWN, HD)).astype(jnp.bfloat16)
 
 
-def finish_kernel(terms_ref, q_ref, null_ref):
-    def term(group, far):
-        at = (group >> 1) * 8 + (group & 1) + (far >> 2) * 16 + (far & 3) * 2
-        return terms_ref[at].astype(jnp.float32)
-
+def term(terms_ref, group, far):
+    at = (group >> 1) * 8 + (group & 1) + (far >> 2) * 16 + (far & 3) * 2
+    return terms_ref[at].astype(jnp.float32)
+
+
+def null_kernel(terms_ref, null_ref):
     for group in range(QUAD):
-        total = term(group, 0)
-        for far in range(1, 16):
-            total += term(group, far)
-        q_ref[:, group * WIDTH : (group + 1) * WIDTH] = total[:, :WIDTH].astype(jnp.bfloat16)
         for h in range(MINE):
-            parts = term(group, h)[:, WIDTH:]
+            parts = term(terms_ref, group, h)[:, WIDTH:]
             rows = jnp.concatenate([parts[0:1] + parts[1:2], parts[2:3] + parts[3:4]], axis=0)
             at = group * WIDTH + h * HD
             null_ref[:, :, at : at + HD] = jnp.broadcast_to(rows[None], (null_ref.shape[0], 2, HD))
+
+
+def own_kernel(terms_ref, q_ref):
+    for group in range(QUAD):
+        total = term(terms_ref, group, 0)
+        for far in range(1, 16):
+            total += term(terms_ref, group, far)
+        q_ref[:, group * WIDTH : (group + 1) * WIDTH] = total[:, :WIDTH].astype(jnp.bfloat16)
+
+
+def place(clip, y, z, corner):
+    return clip * 64 + (y + corner[0]) % 8 * 8 + (z + corner[1]) % 8
+
+
+def bank_groups(corner):
+    return [[place(clip, y, z, corner) for y in range(8) for z in range(8)] for clip in range(8)]
+
+
+def far_groups(corner):
+    return [
+        [place(clip, 2 * yq + yb, 2 * zq + zb, corner) for yq in range(4) for zq in range(4)]
+        for clip in range(8)
+        for yb in range(2)
+        for zb in range(2)
+    ]
 
 
 VMEM = pl.BlockSpec(memory_space=pltpu.VMEM)
@@ -214,7 +246,8 @@
         scratch=[pltpu.VMEM(queries.shape, bf16)] * 2 + [pltpu.SemaphoreType.DMA((2,))],
         megabytes=60,
     )(queries, grad_out)
-    whole = lax.all_to_all(outgoing, BANK, 0, 0).reshape(QTOK, 2 * WIDTH)
+    whole = lax.all_to_all(outgoing, ALL, 0, 0, axis_index_groups=bank_groups(GATHER_CORNER), tiled=True)
+    whole = whole.reshape(QTOK, 2 * WIDTH)
     blocks = swap(
         kernel(share_kernel, "share", [SMEM, SMEM, VMEM, VMEM], *[((2 * BLK, WIDTH), bf16)] * QUAD)(
             bank_counts, block_slot, keys[0], values[0]
@@ -227,7 +260,7 @@
         *[((SLOTS + PAD, WIDTH), bf16)] * 2,
     )(*blocks, null_key[None], null_value[None])
     (parts,) = kernel(stats_kernel, "stats", [VMEM] * 3, ((16, 3, MINE, QTOK), f32))(whole, keys, vals)
-    parts = lax.all_to_all(parts, FAR, 0, 0)
+    parts = lax.all_to_all(parts, ALL, 0, 0, axis_index_groups=far_groups(STATS_CORNER), tiled=True)
     grad_q, *grad_kv = kernel(
         grad_kernel,
         "grads",
@@ -235,10 +268,9 @@
         ((64, OWN, WIDTH + HD), bf16),
         *[((2 * BLK, WIDTH), bf16)] * QUAD,
     )(parts, whole, keys, vals)
-    terms = lax.all_to_all(grad_q, BANK, 0, 0)
-    own_q, nulls = kernel(
-        finish_kernel, "finish", [VMEM], ((OWN, HEADS * HD), bf16), ((8, 2, HEADS * HD), f32)
-    )(terms)
+    terms = lax.all_to_all(grad_q, ALL, 0, 0, axis_index_groups=bank_groups(SUMS_CORNER), tiled=True)
+    (nulls,) = kernel(null_kernel, "nulls", [VMEM], ((8, 2, HEADS * HD), f32))(terms)
+    (own_q,) = kernel(own_kernel, "own", [VMEM], ((OWN, HEADS * HD), bf16))(terms)
     grad_k, grad_v = kernel(
         join_kernel, "join", [VMEM] * QUAD, *[((BLK, HEADS * HD), bf16)] * 2
     )(*swap(grad_kv))

time: 95.1 us -> 91.1 us (0.958)
  waiting for transfers between devices: 12.8 us -> 7.6 us
  starting transfers between devices: 52 us -> 55.6 us
  blocking collectives: 19.6 us -> 16.6 us
    all_to_all x2, starting transfers between devices: 23 us -> 28 us  [the longest x1 17.5 us: on_device(): lax.all_to_all(outgoing, ALL, 0, 0, axis_index_groups=bank_groups(GATHER_...]
    all_to_all x1, blocking collectives: 19.6 us -> 16.6 us  [on_device(): lax.all_to_all(parts, ALL, 0, 0, axis_index_groups=far_groups(STATS_CORNE...]
    all_to_all x2, waiting for transfers between devices: 2.47 us -> 0.01 us  [the longest x1 0.01 us: on_device(): lax.all_to_all(outgoing, ALL, 0, 0, axis_index_groups=bank_groups(GATHER_...]
    ppermute x6, waiting for transfers between devices: 6.33 us -> 4.23 us  [swap(): lax.ppermute(block, ('clip',) + BANK, partners(hop))]
    all_to_all x1, starting transfers between devices: 7.44 us -> 6.05 us  [on_device(): nulls = jnp.sum(lax.all_to_all(nulls, 'clip', 0, 0), axis=0)]
  transfers between devices with their start and end apart: 9 -> 9, of which waited for: 4 -> 3; matrix products, arithmetic and copies ran while one was open for 0% -> 0% of each run, Pallas kernels for 2% -> 3%
where the time goes in v5:
time: 91.1 us; the launch traced here: 90.4 us
  starting transfers between devices  55.6 us (61%)
  blocking collectives  16.6 us (18%)
  Pallas kernels  7.63 us (8%)
  waiting for transfers between devices  7.6 us (8%)
  between operations  2.13 us (2%)
    ppermute x6, starting transfers between devices, swap(): lax.ppermute(block, ('clip',) + BANK, partners(hop))  21.6 us
    all_to_all x1, starting transfers between devices, on_device(): lax.all_to_all(outgoing, ALL, 0, 0, axis_index_groups=bank_groups(GATHER_...  17.5 us
    all_to_all x1, blocking collectives, on_device(): lax.all_to_all(parts, ALL, 0, 0, axis_index_groups=far_groups(STATS_CORNE...  16.6 us
    all_to_all x1, starting transfers between devices, on_device(): lax.all_to_all(grad_q, ALL, 0, 0, axis_index_groups=bank_groups(SUMS_CORN...  10.4 us
    all_to_all x1, starting transfers between devices, on_device(): nulls = jnp.sum(lax.all_to_all(nulls, 'clip', 0, 0), axis=0)  6.05 us
    ppermute x6, waiting for transfers between devices, swap(): lax.ppermute(block, ('clip',) + BANK, partners(hop))  4.23 us
    all_to_all x1, waiting for transfers between devices, on_device(): nulls = jnp.sum(lax.all_to_all(nulls, 'clip', 0, 0), axis=0)  3.36 us
    pallas_call x1, Pallas kernels, on_device(): kernel(grad_kernel, 'grads', [VMEM] * 4, ((64, OWN, WIDTH + HD), bf16), *...  2.76 us
  transfers between devices with their start and end apart: 9, of which 3 were waited for; matrix products, arithmetic and copies ran while one was open for 0% of the time, Pallas kernels for 3%

profile of v5, /device:TPU:1, one launch (start us, length us, event | category | flops | bytes accessed | tf_op | source)
XLA Modules:
  0.0 90.4 jit_solution(12961315384954074223)
XLA Ops:
  0.6 1.5 %outgoing.1 = bf16[64,4,768]{2,1,0:T(4,128)(2,1)} custom-call(bf16[1,4,1536]{2,1,0:T(4,128)(2,1)} %q_hbm.1, bf16[1,4,1536]{2,1,0:T(4,128)(2,1)} %do_hbm.1), custom_call_target="tpu_custom_call" | custom-call | tf_op jit(solution)/shard_map/outgoing/pallas_call | solution.py:241
  2.2 0.0 copy-start
  2.2 17.5 %all-to-all-start = ((bf16[64,4,768]{2,1,0:T(4,128)(2,1)}), bf16[64,4,768]{2,1,0:T(4,128)(2,1)S(1)}, u32[]{:S(2)}, u32[]{:S(2)}) async-start(bf16[64,4,768]{2,1,0:T(4,128)(2,1)} %outgoing.1), calls=%async_computation | async-start | bytes 786432 | tf_op jit(solution)/shard_map/all_to_all | solution.py:249
  21.1 0.1 share.1
  21.2 4.3 %collective-permute-start = (bf16[256,384]{1,0:T(8,128)(2,1)S(1)}, bf16[256,384]{1,0:T(8,128)(2,1)S(1)}, u32[]{:S(2)}, u32[]{:S(2)}) collective-permute-start(bf16[256,384]{1,0:T(8,128)(2,1)S(1)} %get-tuple-element.19), channel_id=1, source_target_pairs={{0,9},{1,8},{2,11},{3,10},{4,13},{5,12},{6,15},{7,14},{8,1},{9,0},... | collective-permute-start | bytes 589832 | tf_op jit(solution)/shard_map/ppermute | solution.py:235
  25.5 2.1 %collective-permute-start.1 = (bf16[256,384]{1,0:T(8,128)(2,1)S(1)}, bf16[256,384]{1,0:T(8,128)(2,1)S(1)}, u32[]{:S(2)}, u32[]{:S(2)}) collective-permute-start(bf16[256,384]{1,0:T(8,128)(2,1)S(1)} %get-tuple-element.20), channel_id=1, source_target_pairs={{0,1},{1,0},{2,3},{3,2},{4,5},{5,4},{6,7},{7,6},{8,9},{9,8},{10,11... | collective-permute-start | bytes 589832 | tf_op jit(solution)/shard_map/ppermute | solution.py:235
  27.6 4.4 %collective-permute-start.2 = (bf16[256,384]{1,0:T(8,128)(2,1)S(1)}, bf16[256,384]{1,0:T(8,128)(2,1)S(1)}, u32[]{:S(2)}, u32[]{:S(2)}) collective-permute-start(bf16[256,384]{1,0:T(8,128)(2,1)S(1)} %get-tuple-element.21), channel_id=1, source_target_pairs={{0,8},{1,9},{2,10},{3,11},{4,12},{5,13},{6,14},{7,15},{8,0},{9,1},... | collective-permute-start | bytes 589832 | tf_op jit(solution)/shard_map/ppermute | solution.py:235
  32.1 1.9 %collective-permute-done.b1 = bf16[256,384]{1,0:T(8,128)(2,1)S(1)} collective-permute-done((bf16[256,384]{1,0:T(8,128)(2,1)S(1)}, bf16[256,384]{1,0:T(8,128)(2,1)S(1)}, u32[]{:S(2)}, u32[]{:S(2)}) %collective-permute-start) | collective-permute-done | bytes 196640 | tf_op jit(solution)/shard_map/ppermute | solution.py:235
  34.0 2.3 %collective-permute-done.1.b2 = bf16[256,384]{1,0:T(8,128)(2,1)S(1)} collective-permute-done((bf16[256,384]{1,0:T(8,128)(2,1)S(1)}, bf16[256,384]{1,0:T(8,128)(2,1)S(1)}, u32[]{:S(2)}, u32[]{:S(2)}) %collective-permute-start.1) | collective-permute-done | bytes 196640 | tf_op jit(solution)/shard_map/ppermute | solution.py:235
  36.3 0.1 bank.1
  36.4 0.1 reshape.13.qd_ref
  36.5 0.9 stats.1
  37.4 16.6 %all_to_all.20.parts_ref = f32[16,3,3,256]{3,2,1,0:T(4,128)S(1)} all-to-all(f32[16,3,3,256]{3,2,1,0:T(4,128)S(1)} %stats.1), channel_id=1, replica_groups={{36,38,32,34,52,54,48,50,4,6,0,2,20,22,16,18},{37,39,33,35,53,55,49,51,..., dimensions={0} | all-to-all | bytes 294912 | tf_op jit(solution)/shard_map/all_to_all | solution.py:263
  54.0 2.8 %grads.1 = (bf16[64,4,512]{2,1,0:T(4,128)(2,1)}, bf16[256,384]{1,0:T(8,128)(2,1)S(1)}, bf16[256,384]{1,0:T(8,128)(2,1)S(1)}, bf16[256,384]{1,0:T(8,128)(2,1)S(1)}, bf16[256,384]{1,0:T(8,128)(2,1)S(1)}) custom-call(f32[16,3,3,256]{3,2,1,0:T(4,128)S(1)} %all_to_all.20.parts_ref, bf16[256,768]{1,0:T(8,128)(2,1)S(1)} %reshape.13.qd_ref, ...), custom_call_target="tpu_custom_call" | custom-call | tf_op jit(solution)/shard_map/grads/pallas_call | solution.py:264
  56.7 10.4 %all-to-all-start.2 = ((bf16[64,4,512]{2,1,0:T(4,128)(2,1)}), bf16[64,4,512]{2,1,0:T(4,128)(2,1)S(1)}, u32[]{:S(2)}, u32[]{:S(2)}) async-start(bf16[64,4,512]{2,1,0:T(4,128)(2,1)} %get-tuple-element.24), calls=%async_computation.2 | async-start | bytes 524288 | tf_op jit(solution)/shard_map/all_to_all | solution.py:271
  67.1 4.6 %collective-permute-start.3 = (bf16[256,384]{1,0:T(8,128)(2,1)S(1)}, bf16[256,384]{1,0:T(8,128)(2,1)S(1)}, u32[]{:S(2)}, u32[]{:S(2)}) collective-permute-start(bf16[256,384]{1,0:T(8,128)(2,1)S(1)} %get-tuple-element.26), channel_id=1, source_target_pairs={{0,9},{1,8},{2,11},{3,10},{4,13},{5,12},{6,15},{7,14},{8,1},{9,0},... | collective-permute-start | bytes 589832 | tf_op jit(solution)/shard_map/ppermute | solution.py:235
  71.7 4.3 %collective-permute-start.4 = (bf16[256,384]{1,0:T(8,128)(2,1)S(1)}, bf16[256,384]{1,0:T(8,128)(2,1)S(1)}, u32[]{:S(2)}, u32[]{:S(2)}) collective-permute-start(bf16[256,384]{1,0:T(8,128)(2,1)S(1)} %get-tuple-element.27), channel_id=1, source_target_pairs={{0,1},{1,0},{2,3},{3,2},{4,5},{5,4},{6,7},{7,6},{8,9},{9,8},{10,11... | collective-permute-start | bytes 589832 | tf_op jit(solution)/shard_map/ppermute | solution.py:235
  76.1 1.9 %collective-permute-start.5 = (bf16[256,384]{1,0:T(8,128)(2,1)S(1)}, bf16[256,384]{1,0:T(8,128)(2,1)S(1)}, u32[]{:S(2)}, u32[]{:S(2)}) collective-permute-start(bf16[256,384]{1,0:T(8,128)(2,1)S(1)} %get-tuple-element.28), channel_id=1, source_target_pairs={{0,8},{1,9},{2,10},{3,11},{4,12},{5,13},{6,14},{7,15},{8,0},{9,1},... | collective-permute-start | bytes 589832 | tf_op jit(solution)/shard_map/ppermute | solution.py:235
  78.0 0.7 nulls.1
  78.7 6.1 %all-to-all-start.3 = ((f32[8,2,1536]{2,1,0:T(2,128)}), f32[8,2,1536]{2,1,0:T(2,128)S(1)}, u32[]{:S(2)}, u32[]{:S(2)}) async-start(f32[8,2,1536]{2,1,0:T(2,128)} %nulls.1), calls=%async_computation.3 | async-start | bytes 196608 | tf_op jit(solution)/shard_map/all_to_all | solution.py:277
  84.7 1.0 %join.1 = (bf16[128,1536]{1,0:T(8,128)(2,1)}, bf16[128,1536]{1,0:T(8,128)(2,1)}) custom-call(bf16[256,384]{1,0:T(8,128)(2,1)S(1)} %get-tuple-element.25.refs_0_, bf16[256,384]{1,0:T(8,128)(2,1)S(1)} %collective-permute-done.3.refs_1_, bf16[256,384]{1,0:T(8,128)(2,1)S(1)} %collective-permute-done.4.refs_2_, bf16[256,384]{1,0:T(8,128)(2,1)S(1)} %collective-permute-done.5.refs_3_), custom_call_target="tpu_custom_call" | custom-call | tf_op jit(solution)/shard_map/join/pallas_call | solution.py:274
  85.7 0.6 own.1
  86.3 3.4 %all-to-all-done.3 = f32[8,2,1536]{2,1,0:T(2,128)S(1)} async-done(((f32[8,2,1536]{2,1,0:T(2,128)}), f32[8,2,1536]{2,1,0:T(2,128)S(1)}, u32[]{:S(2)}, u32[]{:S(2)}) %all-to-all-start.3) | async-done | bytes 98336 | tf_op jit(solution)/shard_map/all_to_all | solution.py:277
  89.7 0.6 slice_reduce_fusion
  (16 shorter events, 0.1 us)
Async XLA Ops:
  2.2 18.9 %copy-start = (bf16[1,128,1536]{2,1,0:T(8,128)(2,1)S(1)}, bf16[1,128,1536]{2,1,0:T(8,128)(2,1)}, u32[]{:S(2)}) copy-start(bf16[1,128,1536]{2,1,0:T(8,128)(2,1)} %param.9) | copy-start | bytes 1179652
  2.2 18.9 %copy-start.1 = (bf16[1,128,1536]{2,1,0:T(8,128)(2,1)S(1)}, bf16[1,128,1536]{2,1,0:T(8,128)(2,1)}, u32[]{:S(2)}) copy-start(bf16[1,128,1536]{2,1,0:T(8,128)(2,1)} %param.10) | copy-start | bytes 1179652
  2.2 34.2 %all-to-all-start = ((bf16[64,4,768]{2,1,0:T(4,128)(2,1)}), bf16[64,4,768]{2,1,0:T(4,128)(2,1)S(1)}, u32[]{:S(2)}, u32[]{:S(2)}) async-start(bf16[64,4,768]{2,1,0:T(4,128)(2,1)} %outgoing.1), calls=%async_computation | async-start | bytes 786432 | tf_op jit(solution)/shard_map/all_to_all | solution.py:249
  21.2 10.8 %copy-start.2 = (bf16[1536]{0:T(1024)(128)(2,1)S(1)}, bf16[1536]{0:T(1024)(128)(2,1)}, u32[]{:S(2)}) copy-start(bf16[1536]{0:T(1024)(128)(2,1)} %param.12) | copy-start | bytes 9220
  21.2 12.8 %collective-permute-start = (bf16[256,384]{1,0:T(8,128)(2,1)S(1)}, bf16[256,384]{1,0:T(8,128)(2,1)S(1)}, u32[]{:S(2)}, u32[]{:S(2)}) collective-permute-start(bf16[256,384]{1,0:T(8,128)(2,1)S(1)} %get-tuple-element.19), channel_id=1, source_target_pairs={{0,9},{1,8},{2,11},{3,10},{4,13},{5,12},{6,15},{7,14},{8,1},{9,0},... | collective-permute-start | bytes 589832 | tf_op jit(solution)/shard_map/ppermute | solution.py:235
  25.5 10.8 %collective-permute-start.1 = (bf16[256,384]{1,0:T(8,128)(2,1)S(1)}, bf16[256,384]{1,0:T(8,128)(2,1)S(1)}, u32[]{:S(2)}, u32[]{:S(2)}) collective-permute-start(bf16[256,384]{1,0:T(8,128)(2,1)S(1)} %get-tuple-element.20), channel_id=1, source_target_pairs={{0,1},{1,0},{2,3},{3,2},{4,5},{5,4},{6,7},{7,6},{8,9},{9,8},{10,11... | collective-permute-start | bytes 589832 | tf_op jit(solution)/shard_map/ppermute | solution.py:235
  27.6 4.4 %copy-start.3 = (bf16[1536]{0:T(1024)(128)(2,1)S(1)}, bf16[1536]{0:T(1024)(128)(2,1)}, u32[]{:S(2)}) copy-start(bf16[1536]{0:T(1024)(128)(2,1)} %param.13) | copy-start | bytes 9220
  27.6 8.6 %collective-permute-start.2 = (bf16[256,384]{1,0:T(8,128)(2,1)S(1)}, bf16[256,384]{1,0:T(8,128)(2,1)S(1)}, u32[]{:S(2)}, u32[]{:S(2)}) collective-permute-start(bf16[256,384]{1,0:T(8,128)(2,1)S(1)} %get-tuple-element.21), channel_id=1, source_target_pairs={{0,8},{1,9},{2,10},{3,11},{4,12},{5,13},{6,14},{7,15},{8,0},{9,1},... | collective-permute-start | bytes 589832 | tf_op jit(solution)/shard_map/ppermute | solution.py:235
  56.7 21.3 %all-to-all-start.2 = ((bf16[64,4,512]{2,1,0:T(4,128)(2,1)}), bf16[64,4,512]{2,1,0:T(4,128)(2,1)S(1)}, u32[]{:S(2)}, u32[]{:S(2)}) async-start(bf16[64,4,512]{2,1,0:T(4,128)(2,1)} %get-tuple-element.24), calls=%async_computation.2 | async-start | bytes 524288 | tf_op jit(solution)/shard_map/all_to_all | solution.py:271
  67.1 17.6 %collective-permute-start.3 = (bf16[256,384]{1,0:T(8,128)(2,1)S(1)}, bf16[256,384]{1,0:T(8,128)(2,1)S(1)}, u32[]{:S(2)}, u32[]{:S(2)}) collective-permute-start(bf16[256,384]{1,0:T(8,128)(2,1)S(1)} %get-tuple-element.26), channel_id=1, source_target_pairs={{0,9},{1,8},{2,11},{3,10},{4,13},{5,12},{6,15},{7,14},{8,1},{9,0},... | collective-permute-start | bytes 589832 | tf_op jit(solution)/shard_map/ppermute | solution.py:235
  71.7 13.0 %collective-permute-start.4 = (bf16[256,384]{1,0:T(8,128)(2,1)S(1)}, bf16[256,384]{1,0:T(8,128)(2,1)S(1)}, u32[]{:S(2)}, u32[]{:S(2)}) collective-permute-start(bf16[256,384]{1,0:T(8,128)(2,1)S(1)} %get-tuple-element.27), channel_id=1, source_target_pairs={{0,1},{1,0},{2,3},{3,2},{4,5},{5,4},{6,7},{7,6},{8,9},{9,8},{10,11... | collective-permute-start | bytes 589832 | tf_op jit(solution)/shard_map/ppermute | solution.py:235
  76.1 8.7 %collective-permute-start.5 = (bf16[256,384]{1,0:T(8,128)(2,1)S(1)}, bf16[256,384]{1,0:T(8,128)(2,1)S(1)}, u32[]{:S(2)}, u32[]{:S(2)}) collective-permute-start(bf16[256,384]{1,0:T(8,128)(2,1)S(1)} %get-tuple-element.28), channel_id=1, source_target_pairs={{0,8},{1,9},{2,10},{3,11},{4,12},{5,13},{6,14},{7,15},{8,0},{9,1},... | collective-permute-start | bytes 589832 | tf_op jit(solution)/shard_map/ppermute | solution.py:235
  78.7 11.0 %all-to-all-start.3 = ((f32[8,2,1536]{2,1,0:T(2,128)}), f32[8,2,1536]{2,1,0:T(2,128)S(1)}, u32[]{:S(2)}, u32[]{:S(2)}) async-start(f32[8,2,1536]{2,1,0:T(2,128)} %nulls.1), calls=%async_computation.3 | async-start | bytes 196608 | tf_op jit(solution)/shard_map/all_to_all | solution.py:277

commit v6 on v5

--- a/solution.py
+++ b/solution.py
@@ -24,7 +24,7 @@
 NEAR = ("yb", "zb")
 ALL = ("clip",) + BANK
 GATHER_CORNER = (4, 0)
-STATS_CORNER = (4, 4)
+STATS_CORNER = (2, 4)
 SUMS_CORNER = (0, 4)
 
 

time: 91.1 us -> 90.6 us (level)
  starting transfers between devices: 55.6 us -> 54.5 us
where the time goes in v6:
time: 90.6 us; the launch traced here: 89.8 us
  starting transfers between devices  54.5 us (60%)
  blocking collectives  17.2 us (19%)
  Pallas kernels  7.63 us (8%)
  waiting for transfers between devices  7.6 us (8%)
  between operations  2.13 us (2%)
    ppermute x6, starting transfers between devices, swap(): lax.ppermute(block, ('clip',) + BANK, partners(hop))  21.6 us
    all_to_all x1, starting transfers between devices, on_device(): lax.all_to_all(outgoing, ALL, 0, 0, axis_index_groups=bank_groups(GATHER_...  17.5 us
    all_to_all x1, blocking collectives, on_device(): lax.all_to_all(parts, ALL, 0, 0, axis_index_groups=far_groups(STATS_CORNE...  17.2 us
    all_to_all x1, starting transfers between devices, on_device(): lax.all_to_all(grad_q, ALL, 0, 0, axis_index_groups=bank_groups(SUMS_CORN...  9.7 us
    all_to_all x1, starting transfers between devices, on_device(): nulls = jnp.sum(lax.all_to_all(nulls, 'clip', 0, 0), axis=0)  5.63 us
    ppermute x6, waiting for transfers between devices, swap(): lax.ppermute(block, ('clip',) + BANK, partners(hop))  4.23 us
    all_to_all x1, waiting for transfers between devices, on_device(): nulls = jnp.sum(lax.all_to_all(nulls, 'clip', 0, 0), axis=0)  3.36 us
    pallas_call x1, Pallas kernels, on_device(): kernel(grad_kernel, 'grads', [VMEM] * 4, ((64, OWN, WIDTH + HD), bf16), *...  2.77 us
  transfers between devices with their start and end apart: 9, of which 3 were waited for; matrix products, arithmetic and copies ran while one was open for 0% of the time, Pallas kernels for 3%

profile of v6, /device:TPU:1, one launch (start us, length us, event | category | flops | bytes accessed | tf_op | source)
XLA Modules:
  0.0 89.8 jit_solution(14386934953244318269)
XLA Ops:
  0.6 1.5 %outgoing.1 = bf16[64,4,768]{2,1,0:T(4,128)(2,1)} custom-call(bf16[1,4,1536]{2,1,0:T(4,128)(2,1)} %q_hbm.1, bf16[1,4,1536]{2,1,0:T(4,128)(2,1)} %do_hbm.1), custom_call_target="tpu_custom_call" | custom-call | tf_op jit(solution)/shard_map/outgoing/pallas_call | solution.py:241
  2.2 0.0 copy-start
  2.2 17.5 %all-to-all-start = ((bf16[64,4,768]{2,1,0:T(4,128)(2,1)}), bf16[64,4,768]{2,1,0:T(4,128)(2,1)S(1)}, u32[]{:S(2)}, u32[]{:S(2)}) async-start(bf16[64,4,768]{2,1,0:T(4,128)(2,1)} %outgoing.1), calls=%async_computation | async-start | bytes 786432 | tf_op jit(solution)/shard_map/all_to_all | solution.py:249
  21.1 0.1 share.1
  21.2 4.3 %collective-permute-start = (bf16[256,384]{1,0:T(8,128)(2,1)S(1)}, bf16[256,384]{1,0:T(8,128)(2,1)S(1)}, u32[]{:S(2)}, u32[]{:S(2)}) collective-permute-start(bf16[256,384]{1,0:T(8,128)(2,1)S(1)} %get-tuple-element.19), channel_id=1, source_target_pairs={{0,9},{1,8},{2,11},{3,10},{4,13},{5,12},{6,15},{7,14},{8,1},{9,0},... | collective-permute-start | bytes 589832 | tf_op jit(solution)/shard_map/ppermute | solution.py:235
  25.5 2.1 %collective-permute-start.1 = (bf16[256,384]{1,0:T(8,128)(2,1)S(1)}, bf16[256,384]{1,0:T(8,128)(2,1)S(1)}, u32[]{:S(2)}, u32[]{:S(2)}) collective-permute-start(bf16[256,384]{1,0:T(8,128)(2,1)S(1)} %get-tuple-element.20), channel_id=1, source_target_pairs={{0,1},{1,0},{2,3},{3,2},{4,5},{5,4},{6,7},{7,6},{8,9},{9,8},{10,11... | collective-permute-start | bytes 589832 | tf_op jit(solution)/shard_map/ppermute | solution.py:235
  27.6 4.4 %collective-permute-start.2 = (bf16[256,384]{1,0:T(8,128)(2,1)S(1)}, bf16[256,384]{1,0:T(8,128)(2,1)S(1)}, u32[]{:S(2)}, u32[]{:S(2)}) collective-permute-start(bf16[256,384]{1,0:T(8,128)(2,1)S(1)} %get-tuple-element.21), channel_id=1, source_target_pairs={{0,8},{1,9},{2,10},{3,11},{4,12},{5,13},{6,14},{7,15},{8,0},{9,1},... | collective-permute-start | bytes 589832 | tf_op jit(solution)/shard_map/ppermute | solution.py:235
  32.1 1.9 %collective-permute-done.b1 = bf16[256,384]{1,0:T(8,128)(2,1)S(1)} collective-permute-done((bf16[256,384]{1,0:T(8,128)(2,1)S(1)}, bf16[256,384]{1,0:T(8,128)(2,1)S(1)}, u32[]{:S(2)}, u32[]{:S(2)}) %collective-permute-start) | collective-permute-done | bytes 196640 | tf_op jit(solution)/shard_map/ppermute | solution.py:235
  34.0 2.3 %collective-permute-done.1.b2 = bf16[256,384]{1,0:T(8,128)(2,1)S(1)} collective-permute-done((bf16[256,384]{1,0:T(8,128)(2,1)S(1)}, bf16[256,384]{1,0:T(8,128)(2,1)S(1)}, u32[]{:S(2)}, u32[]{:S(2)}) %collective-permute-start.1) | collective-permute-done | bytes 196640 | tf_op jit(solution)/shard_map/ppermute | solution.py:235
  36.3 0.1 bank.1
  36.4 0.1 reshape.13.qd_ref
  36.5 0.9 stats.1
  37.4 17.2 %all_to_all.20.parts_ref = f32[16,3,3,256]{3,2,1,0:T(4,128)S(1)} all-to-all(f32[16,3,3,256]{3,2,1,0:T(4,128)S(1)} %stats.1), channel_id=1, replica_groups={{20,22,16,18,36,38,32,34,52,54,48,50,4,6,0,2},{21,23,17,19,37,39,33,35,..., dimensions={0} | all-to-all | bytes 294912 | tf_op jit(solution)/shard_map/all_to_all | solution.py:263
  54.6 2.8 %grads.1 = (bf16[64,4,512]{2,1,0:T(4,128)(2,1)}, bf16[256,384]{1,0:T(8,128)(2,1)S(1)}, bf16[256,384]{1,0:T(8,128)(2,1)S(1)}, bf16[256,384]{1,0:T(8,128)(2,1)S(1)}, bf16[256,384]{1,0:T(8,128)(2,1)S(1)}) custom-call(f32[16,3,3,256]{3,2,1,0:T(4,128)S(1)} %all_to_all.20.parts_ref, bf16[256,768]{1,0:T(8,128)(2,1)S(1)} %reshape.13.qd_ref, ...), custom_call_target="tpu_custom_call" | custom-call | tf_op jit(solution)/shard_map/grads/pallas_call | solution.py:264
  57.3 9.7 %all-to-all-start.2 = ((bf16[64,4,512]{2,1,0:T(4,128)(2,1)}), bf16[64,4,512]{2,1,0:T(4,128)(2,1)S(1)}, u32[]{:S(2)}, u32[]{:S(2)}) async-start(bf16[64,4,512]{2,1,0:T(4,128)(2,1)} %get-tuple-element.24), calls=%async_computation.2 | async-start | bytes 524288 | tf_op jit(solution)/shard_map/all_to_all | solution.py:271
  67.1 4.6 %collective-permute-start.3 = (bf16[256,384]{1,0:T(8,128)(2,1)S(1)}, bf16[256,384]{1,0:T(8,128)(2,1)S(1)}, u32[]{:S(2)}, u32[]{:S(2)}) collective-permute-start(bf16[256,384]{1,0:T(8,128)(2,1)S(1)} %get-tuple-element.26), channel_id=1, source_target_pairs={{0,9},{1,8},{2,11},{3,10},{4,13},{5,12},{6,15},{7,14},{8,1},{9,0},... | collective-permute-start | bytes 589832 | tf_op jit(solution)/shard_map/ppermute | solution.py:235
  71.6 4.3 %collective-permute-start.4 = (bf16[256,384]{1,0:T(8,128)(2,1)S(1)}, bf16[256,384]{1,0:T(8,128)(2,1)S(1)}, u32[]{:S(2)}, u32[]{:S(2)}) collective-permute-start(bf16[256,384]{1,0:T(8,128)(2,1)S(1)} %get-tuple-element.27), channel_id=1, source_target_pairs={{0,1},{1,0},{2,3},{3,2},{4,5},{5,4},{6,7},{7,6},{8,9},{9,8},{10,11... | collective-permute-start | bytes 589832 | tf_op jit(solution)/shard_map/ppermute | solution.py:235
  76.0 1.9 %collective-permute-start.5 = (bf16[256,384]{1,0:T(8,128)(2,1)S(1)}, bf16[256,384]{1,0:T(8,128)(2,1)S(1)}, u32[]{:S(2)}, u32[]{:S(2)}) collective-permute-start(bf16[256,384]{1,0:T(8,128)(2,1)S(1)} %get-tuple-element.28), channel_id=1, source_target_pairs={{0,8},{1,9},{2,10},{3,11},{4,12},{5,13},{6,14},{7,15},{8,0},{9,1},... | collective-permute-start | bytes 589832 | tf_op jit(solution)/shard_map/ppermute | solution.py:235
  77.9 0.7 nulls.1
  78.6 5.6 %all-to-all-start.3 = ((f32[8,2,1536]{2,1,0:T(2,128)}), f32[8,2,1536]{2,1,0:T(2,128)S(1)}, u32[]{:S(2)}, u32[]{:S(2)}) async-start(f32[8,2,1536]{2,1,0:T(2,128)} %nulls.1), calls=%async_computation.3 | async-start | bytes 196608 | tf_op jit(solution)/shard_map/all_to_all | solution.py:277
  84.2 1.0 %join.1 = (bf16[128,1536]{1,0:T(8,128)(2,1)}, bf16[128,1536]{1,0:T(8,128)(2,1)}) custom-call(bf16[256,384]{1,0:T(8,128)(2,1)S(1)} %get-tuple-element.25.refs_0_, bf16[256,384]{1,0:T(8,128)(2,1)S(1)} %collective-permute-done.3.refs_1_, bf16[256,384]{1,0:T(8,128)(2,1)S(1)} %collective-permute-done.4.refs_2_, bf16[256,384]{1,0:T(8,128)(2,1)S(1)} %collective-permute-done.5.refs_3_), custom_call_target="tpu_custom_call" | custom-call | tf_op jit(solution)/shard_map/join/pallas_call | solution.py:274
  85.2 0.6 own.1
  85.8 3.4 %all-to-all-done.3 = f32[8,2,1536]{2,1,0:T(2,128)S(1)} async-done(((f32[8,2,1536]{2,1,0:T(2,128)}), f32[8,2,1536]{2,1,0:T(2,128)S(1)}, u32[]{:S(2)}, u32[]{:S(2)}) %all-to-all-start.3) | async-done | bytes 98336 | tf_op jit(solution)/shard_map/all_to_all | solution.py:277
  89.2 0.6 slice_reduce_fusion
  (16 shorter events, 0.1 us)
Async XLA Ops:
  2.2 18.9 %copy-start = (bf16[1,128,1536]{2,1,0:T(8,128)(2,1)S(1)}, bf16[1,128,1536]{2,1,0:T(8,128)(2,1)}, u32[]{:S(2)}) copy-start(bf16[1,128,1536]{2,1,0:T(8,128)(2,1)} %param.9) | copy-start | bytes 1179652
  2.2 18.9 %copy-start.1 = (bf16[1,128,1536]{2,1,0:T(8,128)(2,1)S(1)}, bf16[1,128,1536]{2,1,0:T(8,128)(2,1)}, u32[]{:S(2)}) copy-start(bf16[1,128,1536]{2,1,0:T(8,128)(2,1)} %param.10) | copy-start | bytes 1179652
  2.2 34.2 %all-to-all-start = ((bf16[64,4,768]{2,1,0:T(4,128)(2,1)}), bf16[64,4,768]{2,1,0:T(4,128)(2,1)S(1)}, u32[]{:S(2)}, u32[]{:S(2)}) async-start(bf16[64,4,768]{2,1,0:T(4,128)(2,1)} %outgoing.1), calls=%async_computation | async-start | bytes 786432 | tf_op jit(solution)/shard_map/all_to_all | solution.py:249
  21.2 10.8 %copy-start.2 = (bf16[1536]{0:T(1024)(128)(2,1)S(1)}, bf16[1536]{0:T(1024)(128)(2,1)}, u32[]{:S(2)}) copy-start(bf16[1536]{0:T(1024)(128)(2,1)} %param.12) | copy-start | bytes 9220
  21.2 12.8 %collective-permute-start = (bf16[256,384]{1,0:T(8,128)(2,1)S(1)}, bf16[256,384]{1,0:T(8,128)(2,1)S(1)}, u32[]{:S(2)}, u32[]{:S(2)}) collective-permute-start(bf16[256,384]{1,0:T(8,128)(2,1)S(1)} %get-tuple-element.19), channel_id=1, source_target_pairs={{0,9},{1,8},{2,11},{3,10},{4,13},{5,12},{6,15},{7,14},{8,1},{9,0},... | collective-permute-start | bytes 589832 | tf_op jit(solution)/shard_map/ppermute | solution.py:235
  25.5 10.8 %collective-permute-start.1 = (bf16[256,384]{1,0:T(8,128)(2,1)S(1)}, bf16[256,384]{1,0:T(8,128)(2,1)S(1)}, u32[]{:S(2)}, u32[]{:S(2)}) collective-permute-start(bf16[256,384]{1,0:T(8,128)(2,1)S(1)} %get-tuple-element.20), channel_id=1, source_target_pairs={{0,1},{1,0},{2,3},{3,2},{4,5},{5,4},{6,7},{7,6},{8,9},{9,8},{10,11... | collective-permute-start | bytes 589832 | tf_op jit(solution)/shard_map/ppermute | solution.py:235
  27.6 4.4 %copy-start.3 = (bf16[1536]{0:T(1024)(128)(2,1)S(1)}, bf16[1536]{0:T(1024)(128)(2,1)}, u32[]{:S(2)}) copy-start(bf16[1536]{0:T(1024)(128)(2,1)} %param.13) | copy-start | bytes 9220
  27.6 8.6 %collective-permute-start.2 = (bf16[256,384]{1,0:T(8,128)(2,1)S(1)}, bf16[256,384]{1,0:T(8,128)(2,1)S(1)}, u32[]{:S(2)}, u32[]{:S(2)}) collective-permute-start(bf16[256,384]{1,0:T(8,128)(2,1)S(1)} %get-tuple-element.21), channel_id=1, source_target_pairs={{0,8},{1,9},{2,10},{3,11},{4,12},{5,13},{6,14},{7,15},{8,0},{9,1},... | collective-permute-start | bytes 589832 | tf_op jit(solution)/shard_map/ppermute | solution.py:235
  57.3 20.5 %all-to-all-start.2 = ((bf16[64,4,512]{2,1,0:T(4,128)(2,1)}), bf16[64,4,512]{2,1,0:T(4,128)(2,1)S(1)}, u32[]{:S(2)}, u32[]{:S(2)}) async-start(bf16[64,4,512]{2,1,0:T(4,128)(2,1)} %get-tuple-element.24), calls=%async_computation.2 | async-start | bytes 524288 | tf_op jit(solution)/shard_map/all_to_all | solution.py:271
  67.1 17.1 %collective-permute-start.3 = (bf16[256,384]{1,0:T(8,128)(2,1)S(1)}, bf16[256,384]{1,0:T(8,128)(2,1)S(1)}, u32[]{:S(2)}, u32[]{:S(2)}) collective-permute-start(bf16[256,384]{1,0:T(8,128)(2,1)S(1)} %get-tuple-element.26), channel_id=1, source_target_pairs={{0,9},{1,8},{2,11},{3,10},{4,13},{5,12},{6,15},{7,14},{8,1},{9,0},... | collective-permute-start | bytes 589832 | tf_op jit(solution)/shard_map/ppermute | solution.py:235
  71.6 12.6 %collective-permute-start.4 = (bf16[256,384]{1,0:T(8,128)(2,1)S(1)}, bf16[256,384]{1,0:T(8,128)(2,1)S(1)}, u32[]{:S(2)}, u32[]{:S(2)}) collective-permute-start(bf16[256,384]{1,0:T(8,128)(2,1)S(1)} %get-tuple-element.27), channel_id=1, source_target_pairs={{0,1},{1,0},{2,3},{3,2},{4,5},{5,4},{6,7},{7,6},{8,9},{9,8},{10,11... | collective-permute-start | bytes 589832 | tf_op jit(solution)/shard_map/ppermute | solution.py:235
  76.0 8.2 %collective-permute-start.5 = (bf16[256,384]{1,0:T(8,128)(2,1)S(1)}, bf16[256,384]{1,0:T(8,128)(2,1)S(1)}, u32[]{:S(2)}, u32[]{:S(2)}) collective-permute-start(bf16[256,384]{1,0:T(8,128)(2,1)S(1)} %get-tuple-element.28), channel_id=1, source_target_pairs={{0,8},{1,9},{2,10},{3,11},{4,12},{5,13},{6,14},{7,15},{8,0},{9,1},... | collective-permute-start | bytes 589832 | tf_op jit(solution)/shard_map/ppermute | solution.py:235
  78.6 10.6 %all-to-all-start.3 = ((f32[8,2,1536]{2,1,0:T(2,128)}), f32[8,2,1536]{2,1,0:T(2,128)S(1)}, u32[]{:S(2)}, u32[]{:S(2)}) async-start(f32[8,2,1536]{2,1,0:T(2,128)} %nulls.1), calls=%async_computation.3 | async-start | bytes 196608 | tf_op jit(solution)/shard_map/all_to_all | solution.py:277

commit v7 on v6

--- a/solution.py
+++ b/solution.py
@@ -26,6 +26,7 @@
 GATHER_CORNER = (4, 0)
 STATS_CORNER = (2, 4)
 SUMS_CORNER = (0, 4)
+CLIP_FIRST = 5
 
 
 def dot(a, b, dims):
@@ -193,6 +194,10 @@
     return [[place(clip, y, z, corner) for y in range(8) for z in range(8)] for clip in range(8)]
 
 
+def clip_groups(first):
+    return [[(clip + first) % 8 * 64 + at for clip in range(8)] for at in range(64)]
+
+
 def far_groups(corner):
     return [
         [place(clip, 2 * yq + yb, 2 * zq + zb, corner) for yq in range(4) for zq in range(4)]
@@ -274,7 +279,7 @@
     grad_k, grad_v = kernel(
         join_kernel, "join", [VMEM] * QUAD, *[((BLK, HEADS * HD), bf16)] * 2
     )(*swap(grad_kv))
-    nulls = jnp.sum(lax.all_to_all(nulls, "clip", 0, 0), axis=0)
+    nulls = jnp.sum(lax.all_to_all(nulls, ALL, 0, 0, axis_index_groups=clip_groups(CLIP_FIRST), tiled=True), axis=0)
     return (own_q[None], grad_k[None], grad_v[None], nulls[0], nulls[1])
 
 

time: 90.6 us -> 89.1 us (0.983)
  waiting for transfers between devices: 7.6 us -> 5.53 us
    all_to_all x1, waiting for transfers between devices: 3.36 us -> 1.29 us  [on_device(): lax.all_to_all(nulls, ALL, 0, 0, axis_index_groups=clip_groups(CLIP_FIRST...]
where the time goes in v7:
time: 89.1 us; the launch traced here: 88.3 us
  starting transfers between devices  55 us (62%)
  blocking collectives  17.2 us (19%)
  Pallas kernels  7.63 us (9%)
  waiting for transfers between devices  5.53 us (6%)
  between operations  2.13 us (2%)
    ppermute x6, starting transfers between devices, swap(): lax.ppermute(block, ('clip',) + BANK, partners(hop))  21.6 us
    all_to_all x1, starting transfers between devices, on_device(): lax.all_to_all(outgoing, ALL, 0, 0, axis_index_groups=bank_groups(GATHER_...  17.5 us
    all_to_all x1, blocking collectives, on_device(): lax.all_to_all(parts, ALL, 0, 0, axis_index_groups=far_groups(STATS_CORNE...  17.2 us
    all_to_all x1, starting transfers between devices, on_device(): lax.all_to_all(grad_q, ALL, 0, 0, axis_index_groups=bank_groups(SUMS_CORN...  9.7 us
    all_to_all x1, starting transfers between devices, on_device(): lax.all_to_all(nulls, ALL, 0, 0, axis_index_groups=clip_groups(CLIP_FIRST...  6.16 us
    ppermute x6, waiting for transfers between devices, swap(): lax.ppermute(block, ('clip',) + BANK, partners(hop))  4.23 us
    pallas_call x1, Pallas kernels, on_device(): kernel(grad_kernel, 'grads', [VMEM] * 4, ((64, OWN, WIDTH + HD), bf16), *...  2.77 us
  transfers between devices with their start and end apart: 9, of which 3 were waited for; matrix products, arithmetic and copies ran while one was open for 0% of the time, Pallas kernels for 3%

profile of v7, /device:TPU:1, one launch (start us, length us, event | category | flops | bytes accessed | tf_op | source)
XLA Modules:
  0.0 88.3 jit_solution(4967591537934886082)
XLA Ops:
  0.6 1.5 %outgoing.1 = bf16[64,4,768]{2,1,0:T(4,128)(2,1)} custom-call(bf16[1,4,1536]{2,1,0:T(4,128)(2,1)} %q_hbm.1, bf16[1,4,1536]{2,1,0:T(4,128)(2,1)} %do_hbm.1), custom_call_target="tpu_custom_call" | custom-call | tf_op jit(solution)/shard_map/outgoing/pallas_call | solution.py:246
  2.2 0.0 copy-start
  2.2 17.5 %all-to-all-start = ((bf16[64,4,768]{2,1,0:T(4,128)(2,1)}), bf16[64,4,768]{2,1,0:T(4,128)(2,1)S(1)}, u32[]{:S(2)}, u32[]{:S(2)}) async-start(bf16[64,4,768]{2,1,0:T(4,128)(2,1)} %outgoing.1), calls=%async_computation | async-start | bytes 786432 | tf_op jit(solution)/shard_map/all_to_all | solution.py:254
  21.1 0.1 share.1
  21.2 4.3 %collective-permute-start = (bf16[256,384]{1,0:T(8,128)(2,1)S(1)}, bf16[256,384]{1,0:T(8,128)(2,1)S(1)}, u32[]{:S(2)}, u32[]{:S(2)}) collective-permute-start(bf16[256,384]{1,0:T(8,128)(2,1)S(1)} %get-tuple-element.19), channel_id=1, source_target_pairs={{0,9},{1,8},{2,11},{3,10},{4,13},{5,12},{6,15},{7,14},{8,1},{9,0},... | collective-permute-start | bytes 589832 | tf_op jit(solution)/shard_map/ppermute | solution.py:240
  25.5 2.1 %collective-permute-start.1 = (bf16[256,384]{1,0:T(8,128)(2,1)S(1)}, bf16[256,384]{1,0:T(8,128)(2,1)S(1)}, u32[]{:S(2)}, u32[]{:S(2)}) collective-permute-start(bf16[256,384]{1,0:T(8,128)(2,1)S(1)} %get-tuple-element.20), channel_id=1, source_target_pairs={{0,1},{1,0},{2,3},{3,2},{4,5},{5,4},{6,7},{7,6},{8,9},{9,8},{10,11... | collective-permute-start | bytes 589832 | tf_op jit(solution)/shard_map/ppermute | solution.py:240
  27.6 4.4 %collective-permute-start.2 = (bf16[256,384]{1,0:T(8,128)(2,1)S(1)}, bf16[256,384]{1,0:T(8,128)(2,1)S(1)}, u32[]{:S(2)}, u32[]{:S(2)}) collective-permute-start(bf16[256,384]{1,0:T(8,128)(2,1)S(1)} %get-tuple-element.21), channel_id=1, source_target_pairs={{0,8},{1,9},{2,10},{3,11},{4,12},{5,13},{6,14},{7,15},{8,0},{9,1},... | collective-permute-start | bytes 589832 | tf_op jit(solution)/shard_map/ppermute | solution.py:240
  32.1 1.9 %collective-permute-done.b1 = bf16[256,384]{1,0:T(8,128)(2,1)S(1)} collective-permute-done((bf16[256,384]{1,0:T(8,128)(2,1)S(1)}, bf16[256,384]{1,0:T(8,128)(2,1)S(1)}, u32[]{:S(2)}, u32[]{:S(2)}) %collective-permute-start) | collective-permute-done | bytes 196640 | tf_op jit(solution)/shard_map/ppermute | solution.py:240
  34.0 2.3 %collective-permute-done.1.b2 = bf16[256,384]{1,0:T(8,128)(2,1)S(1)} collective-permute-done((bf16[256,384]{1,0:T(8,128)(2,1)S(1)}, bf16[256,384]{1,0:T(8,128)(2,1)S(1)}, u32[]{:S(2)}, u32[]{:S(2)}) %collective-permute-start.1) | collective-permute-done | bytes 196640 | tf_op jit(solution)/shard_map/ppermute | solution.py:240
  36.3 0.1 bank.1
  36.4 0.1 reshape.13.qd_ref
  36.5 0.9 %stats.1 = f32[16,3,3,256]{3,2,1,0:T(4,128)S(1)} custom-call(bf16[256,768]{1,0:T(8,128)(2,1)S(1)} %reshape.13.qd_ref, bf16[528,384]{1,0:T(8,128)(2,1)S(1)} %get-tuple-element.22.keys_ref, bf16[528,384]{1,0:T(8,128)(2,1)S(1)} %get-tuple-element.23.vals_ref), custom_call_target="tpu_custom_call" | custom-call | tf_op jit(solution)/shard_map/stats/pallas_call | solution.py:267
  37.4 17.2 %all_to_all.20.parts_ref = f32[16,3,3,256]{3,2,1,0:T(4,128)S(1)} all-to-all(f32[16,3,3,256]{3,2,1,0:T(4,128)S(1)} %stats.1), channel_id=1, replica_groups={{20,22,16,18,36,38,32,34,52,54,48,50,4,6,0,2},{21,23,17,19,37,39,33,35,..., dimensions={0} | all-to-all | bytes 294912 | tf_op jit(solution)/shard_map/all_to_all | solution.py:268
  54.6 2.8 %grads.1 = (bf16[64,4,512]{2,1,0:T(4,128)(2,1)}, bf16[256,384]{1,0:T(8,128)(2,1)S(1)}, bf16[256,384]{1,0:T(8,128)(2,1)S(1)}, bf16[256,384]{1,0:T(8,128)(2,1)S(1)}, bf16[256,384]{1,0:T(8,128)(2,1)S(1)}) custom-call(f32[16,3,3,256]{3,2,1,0:T(4,128)S(1)} %all_to_all.20.parts_ref, bf16[256,768]{1,0:T(8,128)(2,1)S(1)} %reshape.13.qd_ref, ...), custom_call_target="tpu_custom_call" | custom-call | tf_op jit(solution)/shard_map/grads/pallas_call | solution.py:269
  57.3 9.7 %all-to-all-start.2 = ((bf16[64,4,512]{2,1,0:T(4,128)(2,1)}), bf16[64,4,512]{2,1,0:T(4,128)(2,1)S(1)}, u32[]{:S(2)}, u32[]{:S(2)}) async-start(bf16[64,4,512]{2,1,0:T(4,128)(2,1)} %get-tuple-element.24), calls=%async_computation.2 | async-start | bytes 524288 | tf_op jit(solution)/shard_map/all_to_all | solution.py:276
  67.1 4.6 %collective-permute-start.3 = (bf16[256,384]{1,0:T(8,128)(2,1)S(1)}, bf16[256,384]{1,0:T(8,128)(2,1)S(1)}, u32[]{:S(2)}, u32[]{:S(2)}) collective-permute-start(bf16[256,384]{1,0:T(8,128)(2,1)S(1)} %get-tuple-element.26), channel_id=1, source_target_pairs={{0,9},{1,8},{2,11},{3,10},{4,13},{5,12},{6,15},{7,14},{8,1},{9,0},... | collective-permute-start | bytes 589832 | tf_op jit(solution)/shard_map/ppermute | solution.py:240
  71.6 4.3 %collective-permute-start.4 = (bf16[256,384]{1,0:T(8,128)(2,1)S(1)}, bf16[256,384]{1,0:T(8,128)(2,1)S(1)}, u32[]{:S(2)}, u32[]{:S(2)}) collective-permute-start(bf16[256,384]{1,0:T(8,128)(2,1)S(1)} %get-tuple-element.27), channel_id=1, source_target_pairs={{0,1},{1,0},{2,3},{3,2},{4,5},{5,4},{6,7},{7,6},{8,9},{9,8},{10,11... | collective-permute-start | bytes 589832 | tf_op jit(solution)/shard_map/ppermute | solution.py:240
  76.0 1.9 %collective-permute-start.5 = (bf16[256,384]{1,0:T(8,128)(2,1)S(1)}, bf16[256,384]{1,0:T(8,128)(2,1)S(1)}, u32[]{:S(2)}, u32[]{:S(2)}) collective-permute-start(bf16[256,384]{1,0:T(8,128)(2,1)S(1)} %get-tuple-element.28), channel_id=1, source_target_pairs={{0,8},{1,9},{2,10},{3,11},{4,12},{5,13},{6,14},{7,15},{8,0},{9,1},... | collective-permute-start | bytes 589832 | tf_op jit(solution)/shard_map/ppermute | solution.py:240
  77.9 0.7 nulls.1
  78.6 6.2 %all-to-all-start.3 = ((f32[8,2,1536]{2,1,0:T(2,128)}), f32[8,2,1536]{2,1,0:T(2,128)S(1)}, u32[]{:S(2)}, u32[]{:S(2)}) async-start(f32[8,2,1536]{2,1,0:T(2,128)} %nulls.1), calls=%async_computation.3 | async-start | bytes 196608 | tf_op jit(solution)/shard_map/all_to_all | solution.py:282
  84.8 1.0 %join.1 = (bf16[128,1536]{1,0:T(8,128)(2,1)}, bf16[128,1536]{1,0:T(8,128)(2,1)}) custom-call(bf16[256,384]{1,0:T(8,128)(2,1)S(1)} %get-tuple-element.25.refs_0_, bf16[256,384]{1,0:T(8,128)(2,1)S(1)} %collective-permute-done.3.refs_1_, bf16[256,384]{1,0:T(8,128)(2,1)S(1)} %collective-permute-done.4.refs_2_, bf16[256,384]{1,0:T(8,128)(2,1)S(1)} %collective-permute-done.5.refs_3_), custom_call_target="tpu_custom_call" | custom-call | tf_op jit(solution)/shard_map/join/pallas_call | solution.py:279
  85.7 0.6 own.1
  86.4 1.3 %all-to-all-done.3 = f32[8,2,1536]{2,1,0:T(2,128)S(1)} async-done(((f32[8,2,1536]{2,1,0:T(2,128)}), f32[8,2,1536]{2,1,0:T(2,128)S(1)}, u32[]{:S(2)}, u32[]{:S(2)}) %all-to-all-start.3) | async-done | bytes 98336 | tf_op jit(solution)/shard_map/all_to_all | solution.py:282
  87.7 0.6 slice_reduce_fusion
  (16 shorter events, 0.1 us)
Async XLA Ops:
  2.2 18.9 %copy-start = (bf16[1,128,1536]{2,1,0:T(8,128)(2,1)S(1)}, bf16[1,128,1536]{2,1,0:T(8,128)(2,1)}, u32[]{:S(2)}) copy-start(bf16[1,128,1536]{2,1,0:T(8,128)(2,1)} %param.9) | copy-start | bytes 1179652
  2.2 18.9 %copy-start.1 = (bf16[1,128,1536]{2,1,0:T(8,128)(2,1)S(1)}, bf16[1,128,1536]{2,1,0:T(8,128)(2,1)}, u32[]{:S(2)}) copy-start(bf16[1,128,1536]{2,1,0:T(8,128)(2,1)} %param.10) | copy-start | bytes 1179652
  2.2 34.2 %all-to-all-start = ((bf16[64,4,768]{2,1,0:T(4,128)(2,1)}), bf16[64,4,768]{2,1,0:T(4,128)(2,1)S(1)}, u32[]{:S(2)}, u32[]{:S(2)}) async-start(bf16[64,4,768]{2,1,0:T(4,128)(2,1)} %outgoing.1), calls=%async_computation | async-start | bytes 786432 | tf_op jit(solution)/shard_map/all_to_all | solution.py:254
  21.2 10.8 %copy-start.2 = (bf16[1536]{0:T(1024)(128)(2,1)S(1)}, bf16[1536]{0:T(1024)(128)(2,1)}, u32[]{:S(2)}) copy-start(bf16[1536]{0:T(1024)(128)(2,1)} %param.12) | copy-start | bytes 9220
  21.2 12.8 %collective-permute-start = (bf16[256,384]{1,0:T(8,128)(2,1)S(1)}, bf16[256,384]{1,0:T(8,128)(2,1)S(1)}, u32[]{:S(2)}, u32[]{:S(2)}) collective-permute-start(bf16[256,384]{1,0:T(8,128)(2,1)S(1)} %get-tuple-element.19), channel_id=1, source_target_pairs={{0,9},{1,8},{2,11},{3,10},{4,13},{5,12},{6,15},{7,14},{8,1},{9,0},... | collective-permute-start | bytes 589832 | tf_op jit(solution)/shard_map/ppermute | solution.py:240
  25.5 10.8 %collective-permute-start.1 = (bf16[256,384]{1,0:T(8,128)(2,1)S(1)}, bf16[256,384]{1,0:T(8,128)(2,1)S(1)}, u32[]{:S(2)}, u32[]{:S(2)}) collective-permute-start(bf16[256,384]{1,0:T(8,128)(2,1)S(1)} %get-tuple-element.20), channel_id=1, source_target_pairs={{0,1},{1,0},{2,3},{3,2},{4,5},{5,4},{6,7},{7,6},{8,9},{9,8},{10,11... | collective-permute-start | bytes 589832 | tf_op jit(solution)/shard_map/ppermute | solution.py:240
  27.6 4.4 %copy-start.3 = (bf16[1536]{0:T(1024)(128)(2,1)S(1)}, bf16[1536]{0:T(1024)(128)(2,1)}, u32[]{:S(2)}) copy-start(bf16[1536]{0:T(1024)(128)(2,1)} %param.13) | copy-start | bytes 9220
  27.6 8.6 %collective-permute-start.2 = (bf16[256,384]{1,0:T(8,128)(2,1)S(1)}, bf16[256,384]{1,0:T(8,128)(2,1)S(1)}, u32[]{:S(2)}, u32[]{:S(2)}) collective-permute-start(bf16[256,384]{1,0:T(8,128)(2,1)S(1)} %get-tuple-element.21), channel_id=1, source_target_pairs={{0,8},{1,9},{2,10},{3,11},{4,12},{5,13},{6,14},{7,15},{8,0},{9,1},... | collective-permute-start | bytes 589832 | tf_op jit(solution)/shard_map/ppermute | solution.py:240
  57.3 20.5 %all-to-all-start.2 = ((bf16[64,4,512]{2,1,0:T(4,128)(2,1)}), bf16[64,4,512]{2,1,0:T(4,128)(2,1)S(1)}, u32[]{:S(2)}, u32[]{:S(2)}) async-start(bf16[64,4,512]{2,1,0:T(4,128)(2,1)} %get-tuple-element.24), calls=%async_computation.2 | async-start | bytes 524288 | tf_op jit(solution)/shard_map/all_to_all | solution.py:276
  67.1 17.7 %collective-permute-start.3 = (bf16[256,384]{1,0:T(8,128)(2,1)S(1)}, bf16[256,384]{1,0:T(8,128)(2,1)S(1)}, u32[]{:S(2)}, u32[]{:S(2)}) collective-permute-start(bf16[256,384]{1,0:T(8,128)(2,1)S(1)} %get-tuple-element.26), channel_id=1, source_target_pairs={{0,9},{1,8},{2,11},{3,10},{4,13},{5,12},{6,15},{7,14},{8,1},{9,0},... | collective-permute-start | bytes 589832 | tf_op jit(solution)/shard_map/ppermute | solution.py:240
  71.6 13.1 %collective-permute-start.4 = (bf16[256,384]{1,0:T(8,128)(2,1)S(1)}, bf16[256,384]{1,0:T(8,128)(2,1)S(1)}, u32[]{:S(2)}, u32[]{:S(2)}) collective-permute-start(bf16[256,384]{1,0:T(8,128)(2,1)S(1)} %get-tuple-element.27), channel_id=1, source_target_pairs={{0,1},{1,0},{2,3},{3,2},{4,5},{5,4},{6,7},{7,6},{8,9},{9,8},{10,11... | collective-permute-start | bytes 589832 | tf_op jit(solution)/shard_map/ppermute | solution.py:240
  76.0 8.8 %collective-permute-start.5 = (bf16[256,384]{1,0:T(8,128)(2,1)S(1)}, bf16[256,384]{1,0:T(8,128)(2,1)S(1)}, u32[]{:S(2)}, u32[]{:S(2)}) collective-permute-start(bf16[256,384]{1,0:T(8,128)(2,1)S(1)} %get-tuple-element.28), channel_id=1, source_target_pairs={{0,8},{1,9},{2,10},{3,11},{4,12},{5,13},{6,14},{7,15},{8,0},{9,1},... | collective-permute-start | bytes 589832 | tf_op jit(solution)/shard_map/ppermute | solution.py:240
  78.6 9.1 %all-to-all-start.3 = ((f32[8,2,1536]{2,1,0:T(2,128)}), f32[8,2,1536]{2,1,0:T(2,128)S(1)}, u32[]{:S(2)}, u32[]{:S(2)}) async-start(f32[8,2,1536]{2,1,0:T(2,128)} %nulls.1), calls=%async_computation.3 | async-start | bytes 196608 | tf_op jit(solution)/shard_map/all_to_all | solution.py:282

commit v8 on v7

--- a/solution.py
+++ b/solution.py
@@ -23,7 +23,7 @@
 BANK = ("yq", "yb", "zq", "zb")
 NEAR = ("yb", "zb")
 ALL = ("clip",) + BANK
-GATHER_CORNER = (4, 0)
+GATHER_CORNER = (6, 0)
 STATS_CORNER = (2, 4)
 SUMS_CORNER = (0, 4)
 CLIP_FIRST = 5

time: 89.1 us -> 88.7 us (level)
  starting transfers between devices: 55 us -> 54 us
where the time goes in v8:
time: 88.7 us; the launch traced here: 87.9 us
  starting transfers between devices  54 us (61%)
  blocking collectives  17.2 us (19%)
  Pallas kernels  7.62 us (9%)
  waiting for transfers between devices  6.18 us (7%)
  between operations  2.13 us (2%)
    ppermute x6, starting transfers between devices, swap(): lax.ppermute(block, ('clip',) + BANK, partners(hop))  21.6 us
    all_to_all x1, blocking collectives, on_device(): lax.all_to_all(parts, ALL, 0, 0, axis_index_groups=far_groups(STATS_CORNE...  17.2 us
    all_to_all x1, starting transfers between devices, on_device(): lax.all_to_all(outgoing, ALL, 0, 0, axis_index_groups=bank_groups(GATHER_...  17.1 us
    all_to_all x1, starting transfers between devices, on_device(): lax.all_to_all(grad_q, ALL, 0, 0, axis_index_groups=bank_groups(SUMS_CORN...  9.07 us
    all_to_all x1, starting transfers between devices, on_device(): lax.all_to_all(nulls, ALL, 0, 0, axis_index_groups=clip_groups(CLIP_FIRST...  6.19 us
    ppermute x6, waiting for transfers between devices, swap(): lax.ppermute(block, ('clip',) + BANK, partners(hop))  4.92 us
    pallas_call x1, Pallas kernels, on_device(): kernel(grad_kernel, 'grads', [VMEM] * 4, ((64, OWN, WIDTH + HD), bf16), *...  2.76 us
  transfers between devices with their start and end apart: 9, of which 3 were waited for; matrix products, arithmetic and copies ran while one was open for 0% of the time, Pallas kernels for 3%

profile of v8, /device:TPU:1, one launch (start us, length us, event | category | flops | bytes accessed | tf_op | source)
XLA Modules:
  0.0 87.9 jit_solution(3022006077365071258)
XLA Ops:
  0.6 1.5 %outgoing.1 = bf16[64,4,768]{2,1,0:T(4,128)(2,1)} custom-call(bf16[1,4,1536]{2,1,0:T(4,128)(2,1)} %q_hbm.1, bf16[1,4,1536]{2,1,0:T(4,128)(2,1)} %do_hbm.1), custom_call_target="tpu_custom_call" | custom-call | tf_op jit(solution)/shard_map/outgoing/pallas_call | solution.py:246
  2.2 0.0 copy-start.1
  2.2 17.1 %all-to-all-start = ((bf16[64,4,768]{2,1,0:T(4,128)(2,1)}), bf16[64,4,768]{2,1,0:T(4,128)(2,1)S(1)}, u32[]{:S(2)}, u32[]{:S(2)}) async-start(bf16[64,4,768]{2,1,0:T(4,128)(2,1)} %outgoing.1), calls=%async_computation | async-start | bytes 786432 | tf_op jit(solution)/shard_map/all_to_all | solution.py:254
  20.6 0.1 share.1
  20.7 4.3 %collective-permute-start = (bf16[256,384]{1,0:T(8,128)(2,1)S(1)}, bf16[256,384]{1,0:T(8,128)(2,1)S(1)}, u32[]{:S(2)}, u32[]{:S(2)}) collective-permute-start(bf16[256,384]{1,0:T(8,128)(2,1)S(1)} %get-tuple-element.19), channel_id=1, source_target_pairs={{0,9},{1,8},{2,11},{3,10},{4,13},{5,12},{6,15},{7,14},{8,1},{9,0},... | collective-permute-start | bytes 589832 | tf_op jit(solution)/shard_map/ppermute | solution.py:240
  25.1 2.2 %collective-permute-start.1 = (bf16[256,384]{1,0:T(8,128)(2,1)S(1)}, bf16[256,384]{1,0:T(8,128)(2,1)S(1)}, u32[]{:S(2)}, u32[]{:S(2)}) collective-permute-start(bf16[256,384]{1,0:T(8,128)(2,1)S(1)} %get-tuple-element.20), channel_id=1, source_target_pairs={{0,1},{1,0},{2,3},{3,2},{4,5},{5,4},{6,7},{7,6},{8,9},{9,8},{10,11... | collective-permute-start | bytes 589832 | tf_op jit(solution)/shard_map/ppermute | solution.py:240
  27.3 4.3 %collective-permute-start.2 = (bf16[256,384]{1,0:T(8,128)(2,1)S(1)}, bf16[256,384]{1,0:T(8,128)(2,1)S(1)}, u32[]{:S(2)}, u32[]{:S(2)}) collective-permute-start(bf16[256,384]{1,0:T(8,128)(2,1)S(1)} %get-tuple-element.21), channel_id=1, source_target_pairs={{0,8},{1,9},{2,10},{3,11},{4,12},{5,13},{6,14},{7,15},{8,0},{9,1},... | collective-permute-start | bytes 589832 | tf_op jit(solution)/shard_map/ppermute | solution.py:240
  31.6 2.2 %collective-permute-done.b1 = bf16[256,384]{1,0:T(8,128)(2,1)S(1)} collective-permute-done((bf16[256,384]{1,0:T(8,128)(2,1)S(1)}, bf16[256,384]{1,0:T(8,128)(2,1)S(1)}, u32[]{:S(2)}, u32[]{:S(2)}) %collective-permute-start) | collective-permute-done | bytes 196640 | tf_op jit(solution)/shard_map/ppermute | solution.py:240
  33.8 2.7 %collective-permute-done.1.b2 = bf16[256,384]{1,0:T(8,128)(2,1)S(1)} collective-permute-done((bf16[256,384]{1,0:T(8,128)(2,1)S(1)}, bf16[256,384]{1,0:T(8,128)(2,1)S(1)}, u32[]{:S(2)}, u32[]{:S(2)}) %collective-permute-start.1) | collective-permute-done | bytes 196640 | tf_op jit(solution)/shard_map/ppermute | solution.py:240
  36.5 0.1 bank.1
  36.6 0.1 reshape.13.qd_ref
  36.7 0.9 %stats.1 = f32[16,3,3,256]{3,2,1,0:T(4,128)S(1)} custom-call(bf16[256,768]{1,0:T(8,128)(2,1)S(1)} %reshape.13.qd_ref, bf16[528,384]{1,0:T(8,128)(2,1)S(1)} %get-tuple-element.22.keys_ref, bf16[528,384]{1,0:T(8,128)(2,1)S(1)} %get-tuple-element.23.vals_ref), custom_call_target="tpu_custom_call" | custom-call | tf_op jit(solution)/shard_map/stats/pallas_call | solution.py:267
  37.6 17.2 %all_to_all.20.parts_ref = f32[16,3,3,256]{3,2,1,0:T(4,128)S(1)} all-to-all(f32[16,3,3,256]{3,2,1,0:T(4,128)S(1)} %stats.1), channel_id=1, replica_groups={{20,22,16,18,36,38,32,34,52,54,48,50,4,6,0,2},{21,23,17,19,37,39,33,35,..., dimensions={0} | all-to-all | bytes 294912 | tf_op jit(solution)/shard_map/all_to_all | solution.py:268
  54.8 2.8 %grads.1 = (bf16[64,4,512]{2,1,0:T(4,128)(2,1)}, bf16[256,384]{1,0:T(8,128)(2,1)S(1)}, bf16[256,384]{1,0:T(8,128)(2,1)S(1)}, bf16[256,384]{1,0:T(8,128)(2,1)S(1)}, bf16[256,384]{1,0:T(8,128)(2,1)S(1)}) custom-call(f32[16,3,3,256]{3,2,1,0:T(4,128)S(1)} %all_to_all.20.parts_ref, bf16[256,768]{1,0:T(8,128)(2,1)S(1)} %reshape.13.qd_ref, ...), custom_call_target="tpu_custom_call" | custom-call | tf_op jit(solution)/shard_map/grads/pallas_call | solution.py:269
  57.6 9.1 %all-to-all-start.2 = ((bf16[64,4,512]{2,1,0:T(4,128)(2,1)}), bf16[64,4,512]{2,1,0:T(4,128)(2,1)S(1)}, u32[]{:S(2)}, u32[]{:S(2)}) async-start(bf16[64,4,512]{2,1,0:T(4,128)(2,1)} %get-tuple-element.24), calls=%async_computation.2 | async-start | bytes 524288 | tf_op jit(solution)/shard_map/all_to_all | solution.py:276
  66.7 4.6 %collective-permute-start.3 = (bf16[256,384]{1,0:T(8,128)(2,1)S(1)}, bf16[256,384]{1,0:T(8,128)(2,1)S(1)}, u32[]{:S(2)}, u32[]{:S(2)}) collective-permute-start(bf16[256,384]{1,0:T(8,128)(2,1)S(1)} %get-tuple-element.26), channel_id=1, source_target_pairs={{0,9},{1,8},{2,11},{3,10},{4,13},{5,12},{6,15},{7,14},{8,1},{9,0},... | collective-permute-start | bytes 589832 | tf_op jit(solution)/shard_map/ppermute | solution.py:240
  71.3 4.3 %collective-permute-start.4 = (bf16[256,384]{1,0:T(8,128)(2,1)S(1)}, bf16[256,384]{1,0:T(8,128)(2,1)S(1)}, u32[]{:S(2)}, u32[]{:S(2)}) collective-permute-start(bf16[256,384]{1,0:T(8,128)(2,1)S(1)} %get-tuple-element.27), channel_id=1, source_target_pairs={{0,1},{1,0},{2,3},{3,2},{4,5},{5,4},{6,7},{7,6},{8,9},{9,8},{10,11... | collective-permute-start | bytes 589832 | tf_op jit(solution)/shard_map/ppermute | solution.py:240
  75.6 1.9 %collective-permute-start.5 = (bf16[256,384]{1,0:T(8,128)(2,1)S(1)}, bf16[256,384]{1,0:T(8,128)(2,1)S(1)}, u32[]{:S(2)}, u32[]{:S(2)}) collective-permute-start(bf16[256,384]{1,0:T(8,128)(2,1)S(1)} %get-tuple-element.28), channel_id=1, source_target_pairs={{0,8},{1,9},{2,10},{3,11},{4,12},{5,13},{6,14},{7,15},{8,0},{9,1},... | collective-permute-start | bytes 589832 | tf_op jit(solution)/shard_map/ppermute | solution.py:240
  77.5 0.7 nulls.1
  78.2 6.2 %all-to-all-start.3 = ((f32[8,2,1536]{2,1,0:T(2,128)}), f32[8,2,1536]{2,1,0:T(2,128)S(1)}, u32[]{:S(2)}, u32[]{:S(2)}) async-start(f32[8,2,1536]{2,1,0:T(2,128)} %nulls.1), calls=%async_computation.3 | async-start | bytes 196608 | tf_op jit(solution)/shard_map/all_to_all | solution.py:282
  84.4 1.0 %join.1 = (bf16[128,1536]{1,0:T(8,128)(2,1)}, bf16[128,1536]{1,0:T(8,128)(2,1)}) custom-call(bf16[256,384]{1,0:T(8,128)(2,1)S(1)} %get-tuple-element.25.refs_0_, bf16[256,384]{1,0:T(8,128)(2,1)S(1)} %collective-permute-done.3.refs_1_, bf16[256,384]{1,0:T(8,128)(2,1)S(1)} %collective-permute-done.4.refs_2_, bf16[256,384]{1,0:T(8,128)(2,1)S(1)} %collective-permute-done.5.refs_3_), custom_call_target="tpu_custom_call" | custom-call | tf_op jit(solution)/shard_map/join/pallas_call | solution.py:279
  85.3 0.6 own.1
  86.0 1.3 %all-to-all-done.3 = f32[8,2,1536]{2,1,0:T(2,128)S(1)} async-done(((f32[8,2,1536]{2,1,0:T(2,128)}), f32[8,2,1536]{2,1,0:T(2,128)S(1)}, u32[]{:S(2)}, u32[]{:S(2)}) %all-to-all-start.3) | async-done | bytes 98336 | tf_op jit(solution)/shard_map/all_to_all | solution.py:282
  87.3 0.6 slice_reduce_fusion
  (16 shorter events, 0.1 us)
Async XLA Ops:
  2.2 18.4 %copy-start = (bf16[1,128,1536]{2,1,0:T(8,128)(2,1)S(1)}, bf16[1,128,1536]{2,1,0:T(8,128)(2,1)}, u32[]{:S(2)}) copy-start(bf16[1,128,1536]{2,1,0:T(8,128)(2,1)} %param.9) | copy-start | bytes 1179652
  2.2 18.4 %copy-start.1 = (bf16[1,128,1536]{2,1,0:T(8,128)(2,1)S(1)}, bf16[1,128,1536]{2,1,0:T(8,128)(2,1)}, u32[]{:S(2)}) copy-start(bf16[1,128,1536]{2,1,0:T(8,128)(2,1)} %param.10) | copy-start | bytes 1179652
  2.2 34.4 %all-to-all-start = ((bf16[64,4,768]{2,1,0:T(4,128)(2,1)}), bf16[64,4,768]{2,1,0:T(4,128)(2,1)S(1)}, u32[]{:S(2)}, u32[]{:S(2)}) async-start(bf16[64,4,768]{2,1,0:T(4,128)(2,1)} %outgoing.1), calls=%async_computation | async-start | bytes 786432 | tf_op jit(solution)/shard_map/all_to_all | solution.py:254
  20.7 10.8 %copy-start.2 = (bf16[1536]{0:T(1024)(128)(2,1)S(1)}, bf16[1536]{0:T(1024)(128)(2,1)}, u32[]{:S(2)}) copy-start(bf16[1536]{0:T(1024)(128)(2,1)} %param.12) | copy-start | bytes 9220
  20.7 13.0 %collective-permute-start = (bf16[256,384]{1,0:T(8,128)(2,1)S(1)}, bf16[256,384]{1,0:T(8,128)(2,1)S(1)}, u32[]{:S(2)}, u32[]{:S(2)}) collective-permute-start(bf16[256,384]{1,0:T(8,128)(2,1)S(1)} %get-tuple-element.19), channel_id=1, source_target_pairs={{0,9},{1,8},{2,11},{3,10},{4,13},{5,12},{6,15},{7,14},{8,1},{9,0},... | collective-permute-start | bytes 589832 | tf_op jit(solution)/shard_map/ppermute | solution.py:240
  25.1 11.5 %collective-permute-start.1 = (bf16[256,384]{1,0:T(8,128)(2,1)S(1)}, bf16[256,384]{1,0:T(8,128)(2,1)S(1)}, u32[]{:S(2)}, u32[]{:S(2)}) collective-permute-start(bf16[256,384]{1,0:T(8,128)(2,1)S(1)} %get-tuple-element.20), channel_id=1, source_target_pairs={{0,1},{1,0},{2,3},{3,2},{4,5},{5,4},{6,7},{7,6},{8,9},{9,8},{10,11... | collective-permute-start | bytes 589832 | tf_op jit(solution)/shard_map/ppermute | solution.py:240
  27.2 4.4 %copy-start.3 = (bf16[1536]{0:T(1024)(128)(2,1)S(1)}, bf16[1536]{0:T(1024)(128)(2,1)}, u32[]{:S(2)}) copy-start(bf16[1536]{0:T(1024)(128)(2,1)} %param.13) | copy-start | bytes 9220
  27.3 9.3 %collective-permute-start.2 = (bf16[256,384]{1,0:T(8,128)(2,1)S(1)}, bf16[256,384]{1,0:T(8,128)(2,1)S(1)}, u32[]{:S(2)}, u32[]{:S(2)}) collective-permute-start(bf16[256,384]{1,0:T(8,128)(2,1)S(1)} %get-tuple-element.21), channel_id=1, source_target_pairs={{0,8},{1,9},{2,10},{3,11},{4,12},{5,13},{6,14},{7,15},{8,0},{9,1},... | collective-permute-start | bytes 589832 | tf_op jit(solution)/shard_map/ppermute | solution.py:240
  57.6 19.9 %all-to-all-start.2 = ((bf16[64,4,512]{2,1,0:T(4,128)(2,1)}), bf16[64,4,512]{2,1,0:T(4,128)(2,1)S(1)}, u32[]{:S(2)}, u32[]{:S(2)}) async-start(bf16[64,4,512]{2,1,0:T(4,128)(2,1)} %get-tuple-element.24), calls=%async_computation.2 | async-start | bytes 524288 | tf_op jit(solution)/shard_map/all_to_all | solution.py:276
  66.7 17.7 %collective-permute-start.3 = (bf16[256,384]{1,0:T(8,128)(2,1)S(1)}, bf16[256,384]{1,0:T(8,128)(2,1)S(1)}, u32[]{:S(2)}, u32[]{:S(2)}) collective-permute-start(bf16[256,384]{1,0:T(8,128)(2,1)S(1)} %get-tuple-element.26), channel_id=1, source_target_pairs={{0,9},{1,8},{2,11},{3,10},{4,13},{5,12},{6,15},{7,14},{8,1},{9,0},... | collective-permute-start | bytes 589832 | tf_op jit(solution)/shard_map/ppermute | solution.py:240
  71.3 13.1 %collective-permute-start.4 = (bf16[256,384]{1,0:T(8,128)(2,1)S(1)}, bf16[256,384]{1,0:T(8,128)(2,1)S(1)}, u32[]{:S(2)}, u32[]{:S(2)}) collective-permute-start(bf16[256,384]{1,0:T(8,128)(2,1)S(1)} %get-tuple-element.27), channel_id=1, source_target_pairs={{0,1},{1,0},{2,3},{3,2},{4,5},{5,4},{6,7},{7,6},{8,9},{9,8},{10,11... | collective-permute-start | bytes 589832 | tf_op jit(solution)/shard_map/ppermute | solution.py:240
  75.6 8.8 %collective-permute-start.5 = (bf16[256,384]{1,0:T(8,128)(2,1)S(1)}, bf16[256,384]{1,0:T(8,128)(2,1)S(1)}, u32[]{:S(2)}, u32[]{:S(2)}) collective-permute-start(bf16[256,384]{1,0:T(8,128)(2,1)S(1)} %get-tuple-element.28), channel_id=1, source_target_pairs={{0,8},{1,9},{2,10},{3,11},{4,12},{5,13},{6,14},{7,15},{8,0},{9,1},... | collective-permute-start | bytes 589832 | tf_op jit(solution)/shard_map/ppermute | solution.py:240
  78.2 9.1 %all-to-all-start.3 = ((f32[8,2,1536]{2,1,0:T(2,128)}), f32[8,2,1536]{2,1,0:T(2,128)S(1)}, u32[]{:S(2)}, u32[]{:S(2)}) async-start(f32[8,2,1536]{2,1,0:T(2,128)} %nulls.1), calls=%async_computation.3 | async-start | bytes 196608 | tf_op jit(solution)/shard_map/all_to_all | solution.py:282
